TPU v7x, 32 devices: a whole 2x2x4 slice. The times are simulated.
32 devices in a mesh: enc: 4 (over z), llm: 2 (over x), tp: 4 (over y, core).
Axes of the slice: x: 2, y: 2, z: 4, core: 2. Of those that a mesh axis runs over, the one named last changes fastest.
Arguments:
- visual: bfloat16 [4, 2, 4, 4, 8192], P('enc', 'llm'), may hold values from -6 to 6
- counts: int32 [4, 2, 4], P('enc', 'llm'), may hold values from 0 to 4, as said below
- merger_bias: float32 [8192], replicated, may hold values from -3 to 3
- norm_gain: float32 [8192], replicated, may hold values from 0.1 to 1.9
- kv_weight: bfloat16 [8192, 2048], P(None, 'tp'), may hold values from -0.0625 to 0.0625
- kv_cotangent: bfloat16 [4, 2, 4, 4, 2048], P('enc', 'llm', None, None, 'tp'), may hold values from -6 to 6
Outputs:
- key_values: bfloat16 [4, 2, 4, 4, 2048], P('enc', 'llm', None, None, 'tp')
- visual_grad: bfloat16 [4, 2, 4, 4, 8192], P('enc', 'llm', None, None, 'tp')
- bias_grad: float32 [8192], P('tp')
Inputs may be any that keep to these rules, and one draw needn't show every extreme that they name: Slots c < counts[s, g, b] of block (s, g, b) hold live merged patch blocks, the others hold unused data. For every group g some bucket b receives 4 live slots from every source s.
All inputs are finite; a program needn't handle non-finite values.
Results may differ from a plain program's by a relative error of at most 0.0049.
Values may be sent and summed in bfloat16 or wider, within the bound.
No kernel may reach another device: no remote copies, remote signals or barrier semaphores. Data moves between devices by JAX's collectives and lax.ppermute only.
A program may use at most 64 MiB of HBM per device.

v0:
```python
import jax
import jax.numpy as jnp
from jax import lax
from jax.sharding import PartitionSpec as P


def per_device(visual, counts, merger_bias, norm_gain, kv_weight, kv_cotangent):
    enc_count = lax.axis_size("enc")
    tp_count = lax.axis_size("tp")
    capacity = visual.shape[3]
    features = visual.shape[4]
    own_width = features // tp_count
    own_start = lax.axis_index("tp") * own_width
    columns = kv_weight.shape[1]
    total_rows = enc_count * capacity
    own_slice = lax.dynamic_slice_in_dim(visual[0, 0], own_start, own_width, 2)
    sliced, got_counts = (
        lax.all_to_all(own_slice, "enc", split_axis=0, concat_axis=0, tiled=True),
        lax.all_to_all(counts[0, 0], "enc", split_axis=0, concat_axis=0, tiled=True),
    )
    arrived = lax.all_gather(sliced, "tp", axis=2, tiled=True)
    flat_rows = arrived.reshape(total_rows, features)
    validity = (
        lax.broadcasted_iota(jnp.int32, (enc_count, capacity), 1) < got_counts[:, None]
    ).reshape(total_rows, 1)
    inputs = flat_rows.astype(jnp.float32) + merger_bias
    inv_rms = lax.rsqrt(jnp.mean(inputs * inputs, axis=1, keepdims=True) + 1e-06)
    normed = (inputs * inv_rms * norm_gain).astype(jnp.bfloat16)
    projected = jnp.dot(normed, kv_weight, preferred_element_type=jnp.float32)
    key_out = jnp.where(validity, projected, jnp.zeros_like(projected)).astype(jnp.bfloat16)
    cot_rows = kv_cotangent[0, 0].reshape(total_rows, columns)
    masked = jnp.where(validity, cot_rows, jnp.zeros_like(cot_rows))
    part_dots = jnp.sum(masked.astype(jnp.float32) * projected, axis=1, keepdims=True)
    grad_part = lax.dot_general(
        masked, kv_weight, (((1,), (1,)), ((), ())), preferred_element_type=jnp.float32
    )
    dots_wide = jnp.broadcast_to(part_dots, (total_rows, tp_count))
    grad_normed, row_dot = (
        lax.psum_scatter(grad_part, "tp", scatter_dimension=1, tiled=True),
        lax.psum_scatter(dots_wide, "tp", scatter_dimension=1, tiled=True),
    )
    own_inputs = lax.dynamic_slice_in_dim(inputs, own_start, own_width, 1)
    own_gain = lax.dynamic_slice_in_dim(norm_gain, own_start, own_width, 0)
    grad_rows = (
        inv_rms * own_gain * grad_normed - own_inputs * (inv_rms * inv_rms) * row_dot / features
    )
    bias_part = jnp.sum(grad_rows, axis=0)
    bias_grad = lax.psum(bias_part, ("enc", "llm"))
    returned = lax.all_to_all(
        grad_rows.astype(jnp.bfloat16).reshape(enc_count, capacity, own_width),
        "enc",
        split_axis=0,
        concat_axis=0,
        tiled=True,
    )
    visual_grad = returned.reshape(1, 1, enc_count, capacity, own_width)
    key_values = key_out.reshape(1, 1, enc_count, capacity, columns)
    return (key_values, visual_grad, bias_grad)


def solution(mesh):
    return jax.shard_map(
        per_device,
        mesh=mesh,
        in_specs=(
            P("enc", "llm", None, None, None),
            P("enc", "llm", None),
            P(),
            P(),
            P(None, "tp"),
            P("enc", "llm", None, None, "tp"),
        ),
        out_specs=(P("enc", "llm", None, None, "tp"), P("enc", "llm", None, None, "tp"), P("tp")),
        check_vma=False,
    )
```

profile of v0, /device:TPU:0, one launch (start us, length us, event | category | flops | bytes accessed | tf_op | source)
XLA Modules:
  0.0 90.7 jit_solution(17607185548406516096)
XLA Ops:
  7.2 0.0 copy-start
  7.2 0.0 copy-start.2
  7.2 0.0 copy-start.1
  7.2 1.4 %copy.10 = s32[4,1,1]{2,1,0:T(1,128)} copy(s32[4,1,1]{0,2,1:T(1,128)} %bitcast.10) | data formatting | bytes 32 | tf_op jit(solution)/shard_map/all_to_all | solution.py:19
  8.6 6.3 %all-to-all-start = ((s32[4,1,1]{2,1,0:T(1,128)}), s32[4,1,1]{2,1,0:T(1,128)S(1)}, u32[]{:S(2)}, u32[]{:S(2)}) async-start(s32[4,1,1]{2,1,0:T(1,128)} %copy.10), calls=%async_computation | async-start | bytes 4096 | tf_op jit(solution)/shard_map/all_to_all | solution.py:19
  14.9 0.7 reshape_squeeze.3
  15.6 0.0 copy-done
  15.6 0.7 dynamic-slice_bitcast_fusion
  16.3 1.2 %dynamic-slice.1 = u32[1]{0:T(128)} dynamic-slice(u32[32]{0:T(128)} %constant.28, u32[]{:T(128)S(6)} %add.43), dynamic_slice_sizes={1} | dynamic-slice | bytes 12
  17.5 2.8 %all-to-all-done = s32[4,1,1]{2,1,0:T(1,128)S(1)} async-done(((s32[4,1,1]{2,1,0:T(1,128)}), s32[4,1,1]{2,1,0:T(1,128)S(1)}, u32[]{:S(2)}, u32[]{:S(2)}) %all-to-all-start) | async-done | bytes 48 | tf_op jit(solution)/shard_map/all_to_all | solution.py:19
  20.3 3.3 %all-to-all-start.1 = ((bf16[4,4,2048]{2,1,0:T(4,128)(2,1)}), bf16[4,4,2048]{2,1,0:T(4,128)(2,1)S(1)}, u32[]{:S(2)}, u32[]{:S(2)}) async-start(bf16[4,4,2048]{2,1,0:T(4,128)(2,1)} %dynamic-slice_bitcast_fusion), calls=%async_computation.1 | async-start | bytes 131072 | tf_op jit(solution)/shard_map/all_to_all | solution.py:18
  23.6 0.0 reduce-scatter.2.cloned.1.call-start
  23.7 0.2 reduce.1
  23.9 0.1 iota_compare_fusion
  23.9 0.1 lt.25
  24.0 6.5 %fusion.3 = f32[16,8192]{1,0:T(8,128)} fusion(bf16[8192,512]{1,0:T(8,128)(2,1)} %param.10, bf16[16,512]{1,0:T(8,128)(2,1)S(1)} %reshape_squeeze.3, pred[16]{0:T(512)(128)(4,1)S(1)} %lt.25), kind=kOutput, calls=%fused_computation.11 | convolution fusion | flops 134225920 | bytes 8929296 | tf_op jit(solution)/shard_map/dot_general | solution.py:34
  30.5 0.0 dynamic-slice-start
  30.5 0.0 reduce-scatter.2.cloned.1.call-update
  30.5 0.0 all-to-all-done.1
  30.5 5.8 %all_gather.3 = bf16[4,4,8192]{2,1,0:T(4,128)(2,1)S(1)} all-gather(bf16[4,4,2048]{2,1,0:T(4,128)(2,1)S(1)} %all-to-all-done.1), channel_id=1, replica_groups=mesh['enc'=4,'llm'=2,'tp'=4] {'tp'}, dimensions={2}, use_global_device_ids=true | all-gather | bytes 327680 | tf_op jit(solution)/shard_map/all_gather | solution.py:21
  36.4 0.0 copy-done.1
  36.4 0.3 multiply_reduce_fusion
  36.7 0.1 rsqrt.15
  36.8 0.0 copy-done.2
  36.8 4.8 %select_convert_fusion = (bf16[16,512]{1,0:T(8,128)(2,1)S(1)}, f32[16,512]{1,0:T(8,128)S(1)}) fusion(pred[16]{0:T(512)(128)(4,1)S(1)} %lt.25, bf16[8192,512]{1,0:T(8,128)(2,1)} %param.10, f32[16,8192]{1,0:T(8,128)S(1)} %broadcast_add_fusion, f32[8192]{0:T(1024)S(1)} %copy-done.2, f32[16]{0:T(128)S(1)} %rsqrt.15), kind=kOutput, calls=%fused_computation.9 | convolution fusion | flops 134619136 | bytes 8994896 | tf_op jit(solution)/shard_map/dot_general | solution.py:29
  41.6 0.2 multiply_reduce_fusion.1
  41.8 7.1 %all-reduce = f32[16,4]{0,1:T(4,128)S(1)} all-reduce(f32[16,4]{0,1:T(4,128)S(1)} %broadcast_in_dim.34), channel_id=3, replica_groups=mesh['enc'=4,'llm'=2,'tp'=4] {'tp'}, use_global_device_ids=true, to_apply=%region_3.4.clone | all-reduce | flops 64 | bytes 512
  48.9 0.6 dynamic-slice_bitcast_fusion.1
  49.6 4.1 %reduce-scatter.2.cloned.1.call-done = f32[16,2048]{1,0:T(8,128)} async-done(((f32[16,8192]{1,0:T(8,128)}), f32[16,2048]{1,0:T(8,128)}) %reduce-scatter.2.cloned.1.call-update) | async-done | bytes 131088 | tf_op jit(solution)/shard_map/reduce_scatter | solution.py:39
  53.7 0.0 dynamic-slice-done
  53.7 1.0 %fusion.5 = (f32[2048]{0:T(1024)S(1)}, bf16[16,2048]{1,0:T(8,128)(2,1)S(1)}) fusion(f32[16]{0:T(128)S(1)} %dynamic-slice_bitcast_fusion.1, f32[16]{0:T(128)S(1)} %mul.78, f32[16,8192]{1,0:T(8,128)S(1)} %broadcast_add_fusion, s32[]{:T(128)} %select_n.13, f32[16,2048]{1,0:T(8,128)} %reduce-scatter.2.cloned.1.call-done, f32[2048]{0:T(1024)S(1)} %dynamic-slice-done, ...), kind=kLoop, calls=%fused_computation.16 | loop fusion | flops 260096 | bytes 344260 | tf_op jit(solution)/shard_map/reduce_sum | solution.py:47
  54.8 0.7 reshape.71
  55.4 4.6 %all-to-all-start.2 = ((bf16[4,4,2048]{2,1,0:T(4,128)(2,1)}), bf16[4,4,2048]{2,1,0:T(4,128)(2,1)S(1)}, u32[]{:S(2)}, u32[]{:S(2)}) async-start(bf16[4,4,2048]{2,1,0:T(4,128)(2,1)} %reshape.71), calls=%async_computation.3 | async-start | bytes 131072 | tf_op jit(solution)/shard_map/all_to_all | solution.py:49
  60.0 0.6 reshape.70
  60.6 22.6 %psum.7 = f32[2048]{0:T(1024)} all-reduce(f32[2048]{0:T(1024)S(1)} %get-tuple-element.3), channel_id=1, replica_groups=mesh['enc'=4,'llm'=2,'tp'=4] {'enc','llm'}, use_global_device_ids=true, to_apply=%region_5.6 | all-reduce | flops 2048 | bytes 16384 | tf_op jit(solution)/shard_map/psum | solution.py:48
  83.3 0.0 all-to-all-done.2
  83.3 0.6 copy.12
  (5 shorter events, 0.1 us)
Async XLA Ops:
  7.2 8.4 %copy-start = (bf16[1,1,4,4,8192]{4,3,2,1,0:T(4,128)(2,1)S(1)}, bf16[1,1,4,4,8192]{4,3,2,1,0:T(4,128)(2,1)}, u32[]{:S(2)}) copy-start(bf16[1,1,4,4,8192]{4,3,2,1,0:T(4,128)(2,1)} %param.6) | copy-start | bytes 786436
  7.2 29.6 %copy-start.2 = (f32[8192]{0:T(1024)S(1)}, f32[8192]{0:T(1024)}, u32[]{:S(2)}) copy-start(f32[8192]{0:T(1024)} %param.9) | copy-start | bytes 98308
  7.2 29.2 %copy-start.1 = (f32[8192]{0:T(1024)S(1)}, f32[8192]{0:T(1024)}, u32[]{:S(2)}) copy-start(f32[8192]{0:T(1024)} %param.8) | copy-start | bytes 98308
  8.6 11.8 %all-to-all-start = ((s32[4,1,1]{2,1,0:T(1,128)}), s32[4,1,1]{2,1,0:T(1,128)S(1)}, u32[]{:S(2)}, u32[]{:S(2)}) async-start(s32[4,1,1]{2,1,0:T(1,128)} %copy.10), calls=%async_computation | async-start | bytes 4096 | tf_op jit(solution)/shard_map/all_to_all | solution.py:19
  20.3 10.2 %all-to-all-start.1 = ((bf16[4,4,2048]{2,1,0:T(4,128)(2,1)}), bf16[4,4,2048]{2,1,0:T(4,128)(2,1)S(1)}, u32[]{:S(2)}, u32[]{:S(2)}) async-start(bf16[4,4,2048]{2,1,0:T(4,128)(2,1)} %dynamic-slice_bitcast_fusion), calls=%async_computation.1 | async-start | bytes 131072 | tf_op jit(solution)/shard_map/all_to_all | solution.py:18
  23.6 30.1 %reduce-scatter.2.cloned.1.call-start = ((), (), s32[]{:S(2)}) async-start(), calls=%async_computation.4 | async-start | bytes 655360 | tf_op jit(solution)/shard_map/reduce_scatter | solution.py:39
  30.5 23.2 %dynamic-slice-start = ((f32[8192]{0:T(1024)}, s32[]{:T(128)}), f32[2048]{0:T(1024)S(1)}, s32[]{:S(2)}) async-start(f32[8192]{0:T(1024)} %param.9, s32[]{:T(128)} %select_n.13), calls=%async_computation.5 | async-start | bytes 16896 | tf_op jit(solution)/shard_map/dynamic_slice | solution.py:43
  55.4 27.8 %all-to-all-start.2 = ((bf16[4,4,2048]{2,1,0:T(4,128)(2,1)}), bf16[4,4,2048]{2,1,0:T(4,128)(2,1)S(1)}, u32[]{:S(2)}, u32[]{:S(2)}) async-start(bf16[4,4,2048]{2,1,0:T(4,128)(2,1)} %reshape.71), calls=%async_computation.3 | async-start | bytes 131072 | tf_op jit(solution)/shard_map/all_to_all | solution.py:49
Sparse Core Ops, SparseCore 0:
  30.6 23.0 reduce-scatter.1
where the time goes:
time: 91.3 us; the launch traced here: 90.7 us
  blocking collectives  35.6 us (39%)
  starting transfers between devices  14.2 us (16%)
  between operations  14.1 us (15%)
  matrix products  11.3 us (12%)
  waiting for transfers between devices  7 us (8%)
  local copies, waits for them, and re-layouts  6.76 us (7%)
  other arithmetic  1.78 us (2%)
    psum x1, blocking collectives, per_device(): bias_grad = lax.psum(bias_part, ('enc', 'llm'))  22.6 us
    unnamed x1, blocking collectives  7.14 us
    dot_general x1, matrix products, per_device(): lax.dot_general(masked, kv_weight, (((1,), (1,)), ((), ())), preferred_el...  6.48 us
    all_to_all x1, starting transfers between devices, per_device(): lax.all_to_all(counts[0, 0], 'enc', split_axis=0, concat_axis=0, tiled=True)  6.32 us
    all_gather x1, blocking collectives, per_device(): arrived = lax.all_gather(sliced, 'tp', axis=2, tiled=True)  5.79 us
    dot_general x1, matrix products, per_device(): projected = jnp.dot(normed, kv_weight, preferred_element_type=jnp.float32)  4.79 us
    all_to_all x1, starting transfers between devices, per_device(): lax.all_to_all(grad_rows.astype(jnp.bfloat16).reshape(enc_count, capacity...  4.59 us
    reduce_scatter x1, waiting for transfers between devices, per_device(): lax.psum_scatter(grad_part, 'tp', scatter_dimension=1, tiled=True)  4.15 us
  transfers between devices with their start and end apart: 4, of which 2 were waited for; matrix products, arithmetic and copies ran while one was open for 18% of the time, Pallas kernels for 0%

commit v1 on v0

v1 whole, which is shorter than its diff:
```python
import jax
import jax.numpy as jnp
from jax import lax
from jax.sharding import PartitionSpec as P


def is_power(n):
    return n & (n - 1) == 0


def xor_order(blocks, index):
    n = blocks.shape[0]
    bit = 1
    while bit < n:
        pairs = blocks.reshape((n // (2 * bit), 2, bit) + blocks.shape[1:])
        flipped = jnp.flip(pairs, axis=1).reshape(blocks.shape)
        blocks = jnp.where((index & bit) != 0, flipped, blocks)
        bit *= 2
    return blocks


def swap(x, axis, k):
    n = lax.axis_size(axis)
    return lax.ppermute(x, axis, [(i, i ^ k) for i in range(n)])


def exchange(blocks, axis):
    n = lax.axis_size(axis)
    if not is_power(n) or n > 8:
        return lax.all_to_all(blocks, axis, split_axis=0, concat_axis=0, tiled=True)
    index = lax.axis_index(axis)
    ordered = xor_order(blocks, index)
    got = [ordered[0]] + [swap(ordered[k], axis, k) for k in range(1, n)]
    return xor_order(jnp.stack(got), index)


def all_sum(x, axis):
    n = lax.axis_size(axis)
    if not is_power(n) or n > 8:
        return lax.psum(x, axis)
    return x + sum(swap(x, axis, k) for k in range(1, n))


def per_device(visual, counts, merger_bias, norm_gain, kv_weight, kv_cotangent):
    buckets, capacity, features = visual.shape[2:]
    tp_count = lax.axis_size("tp")
    own_width = features // tp_count
    tp_index = lax.axis_index("tp")
    own_start = tp_index * own_width
    columns = kv_weight.shape[1]
    rows = buckets * capacity
    cot_rows = exchange(kv_cotangent[0, 0], "enc").reshape(rows, columns)
    validity = (
        lax.broadcasted_iota(jnp.int32, (buckets, capacity), 1) < counts[0, 0][:, None]
    ).reshape(rows, 1)
    inputs = visual.reshape(rows, features).astype(jnp.float32) + merger_bias
    inv_rms = lax.rsqrt(jnp.mean(inputs * inputs, axis=1, keepdims=True) + 1e-06)
    normed = (inputs * inv_rms * norm_gain).astype(jnp.bfloat16)
    projected = jnp.dot(normed, kv_weight, preferred_element_type=jnp.float32)
    masked_out = jnp.where(validity, projected, jnp.zeros_like(projected)).astype(jnp.bfloat16)
    key_out = exchange(masked_out.reshape(buckets, capacity, columns), "enc")
    masked = jnp.where(validity, cot_rows, jnp.zeros_like(cot_rows))
    part_dots = jnp.sum(masked.astype(jnp.float32) * projected, axis=1)
    grad_part = lax.dot_general(
        masked, kv_weight, (((1,), (1,)), ((), ())), preferred_element_type=jnp.float32
    )
    row_dot = all_sum(part_dots, "tp")[:, None]
    parts = grad_part.reshape(rows, tp_count, own_width).transpose(1, 0, 2)
    ordered = xor_order(parts, tp_index)
    grad_normed = ordered[0]
    for k in range(1, tp_count):
        got = swap(ordered[k].astype(jnp.bfloat16), "tp", k)
        grad_normed = grad_normed + got.astype(jnp.float32)
    own_inputs = lax.dynamic_slice_in_dim(inputs, own_start, own_width, 1)
    own_gain = lax.dynamic_slice_in_dim(norm_gain, own_start, own_width, 0)
    grad_rows = (
        inv_rms * own_gain * grad_normed - own_inputs * (inv_rms * inv_rms) * row_dot / features
    )
    bias_grad = all_sum(all_sum(jnp.sum(grad_rows, axis=0), "enc"), "llm")
    visual_grad = grad_rows.astype(jnp.bfloat16).reshape(1, 1, buckets, capacity, own_width)
    key_values = key_out.reshape(1, 1, buckets, capacity, columns)
    return (key_values, visual_grad, bias_grad)


def solution(mesh):
    return jax.shard_map(
        per_device,
        mesh=mesh,
        in_specs=(
            P("enc", "llm", None, None, None),
            P("enc", "llm", None),
            P(),
            P(),
            P(None, "tp"),
            P("enc", "llm", None, None, "tp"),
        ),
        out_specs=(P("enc", "llm", None, None, "tp"), P("enc", "llm", None, None, "tp"), P("tp")),
        check_vma=False,
    )
```

time: 91.3 us -> 52.4 us (0.57)
  blocking collectives: 35.6 us -> 0 us
  between operations: 14.1 us -> 0.93 us
  starting transfers between devices: 14.2 us -> 20.3 us
  other arithmetic: 1.78 us -> 6.94 us
  local copies, waits for them, and re-layouts: 6.76 us -> 3.42 us
  waiting for transfers between devices: 7 us -> 9.99 us
  matrix products: 11.3 us -> 10.3 us
    psum x1 -> x0, blocking collectives: 22.6 us -> none  [per_device(): bias_grad = lax.psum(bias_part, ('enc', 'llm'))]
    ppermute x0 -> x16, starting transfers between devices: none -> 20.3 us  [swap(): return lax.ppermute(x, axis, [(i, i ^ k) for i in range(n)])]
    all_to_all x3 -> x0, starting transfers between devices: 14.2 us -> none  [the longest x1 6.32 us: per_device(): lax.all_to_all(counts[0, 0], 'enc', split_axis=0, concat_axis=0, tiled=True)]
    ppermute x0 -> x16, waiting for transfers between devices: none -> 9.99 us  [swap(): return lax.ppermute(x, axis, [(i, i ^ k) for i in range(n)])]
    unnamed x1 -> x0, blocking collectives: 7.14 us -> none
    all_gather x1 -> x0, blocking collectives: 5.79 us -> none  [per_device(): arrived = lax.all_gather(sliced, 'tp', axis=2, tiled=True)]
    reduce_scatter x1 -> x0, waiting for transfers between devices: 4.15 us -> none  [per_device(): lax.psum_scatter(grad_part, 'tp', scatter_dimension=1, tiled=True)]
    all_to_all x3 -> x0, waiting for transfers between devices: 2.83 us -> none  [the longest x1 2.83 us: per_device(): lax.all_to_all(counts[0, 0], 'enc', split_axis=0, concat_axis=0, tiled=True)]
  transfers between devices with their start and end apart: 4 -> 16, of which waited for: 2 -> 5; matrix products, arithmetic and copies ran while one was open for 18% -> 34% of each run, Pallas kernels for 0% -> 0%
where the time goes in v1:
time: 52.4 us; the launch traced here: 51.9 us
  starting transfers between devices  20.3 us (39%)
  matrix products  10.3 us (20%)
  waiting for transfers between devices  9.99 us (19%)
  other arithmetic  6.94 us (13%)
  local copies, waits for them, and re-layouts  3.42 us (7%)
  between operations  0.93 us (2%)
    ppermute x16, starting transfers between devices, swap(): return lax.ppermute(x, axis, [(i, i ^ k) for i in range(n)])  20.3 us
    ppermute x16, waiting for transfers between devices, swap(): return lax.ppermute(x, axis, [(i, i ^ k) for i in range(n)])  9.99 us
    dot_general x1, matrix products, per_device(): lax.dot_general(masked, kv_weight, (((1,), (1,)), ((), ())), preferred_el...  5.66 us
    dot_general x1, matrix products, per_device(): projected = jnp.dot(normed, kv_weight, preferred_element_type=jnp.float32)  4.63 us
    select_n x8, other arithmetic, xor_order(): blocks = jnp.where(index & bit != 0, flipped, blocks)  2.3 us
    reduce_sum x1, other arithmetic, per_device(): jnp.mean(inputs * inputs, axis=1, keepdims=True) + 1e-06  1.25 us
  transfers between devices with their start and end apart: 16, of which 5 were waited for; matrix products, arithmetic and copies ran while one was open for 34% of the time, Pallas kernels for 0%

profile of v1, /device:TPU:0, one launch (start us, length us, event | category | flops | bytes accessed | tf_op | source)
XLA Modules:
  0.0 51.9 jit_solution(12838875151597103191)
XLA Ops:
  0.6 0.0 copy-start
  0.6 0.7 %rev.38 = bf16[2,2,1,4,512]{4,3,1,0,2:T(4,128)(2,1)S(1)} reverse(bf16[2,2,1,4,512]{4,3,1,0,2:T(4,128)(2,1)} %bitcast.101), dimensions={1} | reverse | bytes 32768 | tf_op jit(solution)/shard_map/jit(_flip)/rev | solution.py:16
  1.4 0.8 %bitcast_select_fusion.4 = bf16[1,2,2,4,512]{4,3,2,1,0:T(4,128)(2,1)S(1)} fusion(bf16[1,2,2,4,512]{4,3,2,1,0:T(4,128)(2,1)} %bitcast.103, pred[]{:T(512)S(6)} %ne.9, bf16[2,2,1,4,512]{4,3,1,0,2:T(4,128)(2,1)} %bitcast.102), kind=kLoop, calls=%fused_computation.26 | loop fusion | flops 8192 | bytes 49153 | tf_op jit(solution)/shard_map/jit(_where)/select_n | solution.py:17
  2.2 0.7 %fusion.9 = bf16[4,4,512]{2,1,0:T(4,128)(2,1)S(1)} fusion(bf16[1,1,4,4,512]{4,3,2,1,0:T(4,128)(2,1)} %param.11, bf16[2,2,1,4,512]{4,3,1,0,2:T(4,128)(2,1)S(1)} %rev.38, bf16[1,2,2,4,512]{4,3,2,1,0:T(4,128)(2,1)S(1)} %rev.39, pred[]{:T(512)S(6)} %ne.9, pred[]{:T(512)S(6)} %ne.8), kind=kLoop, calls=%fused_computation.25 | loop fusion | flops 16384 | bytes 65538 | tf_op jit(solution)/shard_map/jit(_where)/select_n | solution.py:17
  3.0 3.0 %collective-permute-start.3 = (bf16[4,512]{1,0:T(4,128)(2,1)S(1)}, bf16[4,512]{1,0:T(4,128)(2,1)S(1)}, u32[]{:S(2)}, u32[]{:S(2)}) collective-permute-start(bf16[4,512]{1,0:T(4,128)(2,1)S(1)} %get-tuple-element.13), channel_id=1, source_target_pairs={{0,8},{8,0},{16,24},{24,16},{1,9},{9,1},{17,25},{25,17},{2,10},{10... | collective-permute-start | bytes 12296 | tf_op jit(solution)/shard_map/ppermute | solution.py:24
  6.0 2.6 %collective-permute-start.4 = (bf16[4,512]{1,0:T(4,128)(2,1)S(1)}, bf16[4,512]{1,0:T(4,128)(2,1)S(1)}, u32[]{:S(2)}, u32[]{:S(2)}) collective-permute-start(bf16[4,512]{1,0:T(4,128)(2,1)S(1)} %get-tuple-element.12), channel_id=1, source_target_pairs={{0,16},{8,24},{16,0},{24,8},{1,17},{9,25},{17,1},{25,9},{2,18},{10... | collective-permute-start | bytes 12296 | tf_op jit(solution)/shard_map/ppermute | solution.py:24
  8.6 0.0 collective-permute-start.5
  8.6 1.0 %reshape.309 = f32[16,8192]{1,0:T(8,128)S(1)} reshape(bf16[1,1,4,4,8192]{4,3,2,1,0:T(4,128)(2,1)} %param.6) | data formatting | bytes 786432 | tf_op jit(solution)/shard_map/convert_element_type | solution.py:56
  9.6 1.2 %multiply_reduce_fusion = f32[4,4]{1,0:T(4,128)S(1)} fusion(f32[8192]{0:T(1024)} %param.8, bf16[1,1,4,4,8192]{4,3,2,1,0:T(4,128)(2,1)} %param.6), kind=kLoop, calls=%fused_computation.3 | loop fusion | flops 524272 | bytes 294976 | tf_op jit(solution)/shard_map/reduce_sum | solution.py:57
  10.8 0.1 rsqrt.15
  10.9 0.8 %broadcast_add_fusion = f32[16,8192]{1,0:T(8,128)S(1)} fusion(f32[16,8192]{1,0:T(8,128)S(1)} %reshape.309, f32[8192]{0:T(1024)} %param.8), kind=kLoop, calls=%fused_computation.7 | loop fusion | flops 131072 | bytes 1081344 | tf_op jit(solution)/shard_map/add | solution.py:56
  11.7 0.7 %iota_compare_fusion.1 = pred[4,4]{1,0:T(4,128)(4,1)S(1)} fusion(s32[4]{0:T(128)} %bitcast.114), kind=kLoop, calls=%fused_computation.41 | loop fusion | flops 16 | bytes 32 | tf_op jit(solution)/shard_map/lt | solution.py:54
  12.4 0.1 lt.31
  12.5 4.6 %select_convert_fusion = (bf16[16,512]{1,0:T(8,128)(2,1)S(1)}, f32[16,512]{1,0:T(8,128)S(1)}) fusion(pred[16]{0:T(512)(128)(4,1)S(1)} %lt.31, bf16[8192,512]{1,0:T(8,128)(2,1)} %param.10, f32[16,8192]{1,0:T(8,128)S(1)} %broadcast_add_fusion, f32[8192]{0:T(1024)} %param.9, f32[16]{0:T(128)S(1)} %rsqrt.15), kind=kOutput, calls=%fused_computation.18 | convolution fusion | flops 134619136 | bytes 8994896 | tf_op jit(solution)/shard_map/dot_general | solution.py:59
  17.3 1.0 %collective-permute-start = (bf16[4,512]{1,0:T(4,128)(2,1)S(1)}, bf16[4,512]{1,0:T(4,128)(2,1)S(1)}, u32[]{:S(2)}, u32[]{:S(2)}) collective-permute-start(bf16[4,512]{1,0:T(4,128)(2,1)S(1)} %get-tuple-element.18), channel_id=1, source_target_pairs={{0,8},{8,0},{16,24},{24,16},{1,9},{9,1},{17,25},{25,17},{2,10},{10... | collective-permute-start | bytes 12296 | tf_op jit(solution)/shard_map/ppermute | solution.py:24
  18.3 3.5 %collective-permute-start.1 = (bf16[4,512]{1,0:T(4,128)(2,1)S(1)}, bf16[4,512]{1,0:T(4,128)(2,1)S(1)}, u32[]{:S(2)}, u32[]{:S(2)}) collective-permute-start(bf16[4,512]{1,0:T(4,128)(2,1)S(1)} %get-tuple-element.17), channel_id=1, source_target_pairs={{0,16},{8,24},{16,0},{24,8},{1,17},{9,25},{17,1},{25,9},{2,18},{10... | collective-permute-start | bytes 12296 | tf_op jit(solution)/shard_map/ppermute | solution.py:24
  21.8 0.5 broadcast.102
  22.3 0.0 copy-done
  22.3 0.7 %reduce.4 = s32[4]{0:T(128)S(1)} reduce(s32[1,1,4]{2,1,0:T(1,128)S(1)} %copy-done, s32[]{:T(128)} %broadcast.102), dimensions={0,1}, to_apply=%param.7.reduce_sub_computation.3 | reduce | bytes 36 | tf_op args[1]
  22.9 0.1 lt.33
  23.0 0.1 iota_compare_fusion
  23.1 0.0 dynamic-slice-start
  23.1 0.0 collective-permute-done.3
  23.1 0.1 collective-permute-start.2
  23.2 0.0 collective-permute-done.4
  23.2 0.0 collective-permute-done.5
  23.4 0.2 multiply_reduce_fusion.1
  23.5 1.8 %collective-permute-start.10 = (f32[16]{0:T(128)S(1)}, f32[16]{0:T(128)S(1)}, u32[]{:S(2)}, u32[]{:S(2)}) collective-permute-start(f32[16]{0:T(128)S(1)} %multiply_reduce_fusion.1), channel_id=1, source_target_pairs={{0,2},{1,3},{2,0},{3,1},{4,6},{5,7},{6,4},{7,5},{8,10},{9,11},{10,... | collective-permute-start | bytes 200 | tf_op jit(solution)/shard_map/ppermute | solution.py:24
  25.4 0.0 collective-permute-start.11
  25.4 0.1 select_select_fusion
  25.5 5.7 %fusion.16 = f32[16,4,2048]{2,0,1:T(8,128)S(1)} fusion(bf16[16,512,1]{1,0,2:T(8,128)(2,1)S(1)} %reshape.310, bf16[4,2048,512]{2,1,0:T(8,128)(2,1)} %bitcast.92), kind=kOutput, calls=%fused_computation.48 | convolution fusion | flops 134217728 | bytes 8929280 | tf_op jit(solution)/shard_map/dot_general | solution.py:64
  31.2 0.1 bitcast_select_fusion.1
  31.3 0.1 fusion.13
  31.4 0.0 collective-permute-done
  31.4 0.4 collective-permute-start.9
  31.8 0.0 collective-permute-done.1
  31.9 0.2 collective-permute-start.6
  32.0 0.0 collective-permute-done.2
  32.0 1.7 %collective-permute-start.7 = (bf16[16,2048]{1,0:T(8,128)(2,1)S(1)}, bf16[16,2048]{1,0:T(8,128)(2,1)S(1)}, u32[]{:S(2)}, u32[]{:S(2)}) collective-permute-start(bf16[16,2048]{1,0:T(8,128)(2,1)S(1)} %get-tuple-element.9), channel_id=1, source_target_pairs={{0,2},{1,3},{2,0},{3,1},{4,6},{5,7},{6,4},{7,5},{8,10},{9,11},{10,... | collective-permute-start | bytes 196616 | tf_op jit(solution)/shard_map/ppermute | solution.py:24
  33.7 0.0 collective-permute-done.10
  33.8 0.1 collective-permute-start.8
  33.9 0.0 collective-permute-done.11
  33.9 0.0 collective-permute-done.9
  33.9 0.0 collective-permute-done.6
  33.9 2.5 %collective-permute-done.7 = bf16[16,2048]{1,0:T(8,128)(2,1)S(1)} collective-permute-done((bf16[16,2048]{1,0:T(8,128)(2,1)S(1)}, bf16[16,2048]{1,0:T(8,128)(2,1)S(1)}, u32[]{:S(2)}, u32[]{:S(2)}) %collective-permute-start.7) | collective-permute-done | bytes 65568 | tf_op jit(solution)/shard_map/ppermute | solution.py:24
  36.4 1.5 %collective-permute-done.8 = bf16[16,2048]{1,0:T(8,128)(2,1)S(1)} collective-permute-done((bf16[16,2048]{1,0:T(8,128)(2,1)S(1)}, bf16[16,2048]{1,0:T(8,128)(2,1)S(1)}, u32[]{:S(2)}, u32[]{:S(2)}) %collective-permute-start.8) | collective-permute-done | bytes 65568 | tf_op jit(solution)/shard_map/ppermute | solution.py:24
  37.9 0.0 dynamic-slice-done
  37.9 0.1 fusion.11
  38.0 0.3 collective-permute-start.12
  38.3 3.8 %collective-permute-start.13 = (f32[2048]{0:T(1024)S(1)}, f32[2048]{0:T(1024)S(1)}, u32[]{:S(2)}, u32[]{:S(2)}) collective-permute-start(f32[2048]{0:T(1024)S(1)} %get-tuple-element.3), channel_id=1, source_target_pairs={{0,16},{8,24},{16,0},{24,8},{1,17},{9,25},{17,1},{25,9},{2,18},{10... | collective-permute-start | bytes 24584 | tf_op jit(solution)/shard_map/ppermute | solution.py:24
  42.2 0.3 collective-permute-start.14
  42.5 0.0 collective-permute-done.12
  42.5 1.3 %collective-permute-done.13 = f32[2048]{0:T(1024)S(1)} collective-permute-done((f32[2048]{0:T(1024)S(1)}, f32[2048]{0:T(1024)S(1)}, u32[]{:S(2)}, u32[]{:S(2)}) %collective-permute-start.13) | collective-permute-done | bytes 8224 | tf_op jit(solution)/shard_map/ppermute | solution.py:24
  43.8 3.8 %collective-permute-done.14 = f32[2048]{0:T(1024)S(1)} collective-permute-done((f32[2048]{0:T(1024)S(1)}, f32[2048]{0:T(1024)S(1)}, u32[]{:S(2)}, u32[]{:S(2)}) %collective-permute-start.14) | collective-permute-done | bytes 8224 | tf_op jit(solution)/shard_map/ppermute | solution.py:24
  47.6 1.5 %collective-permute-start.15 = (f32[2048]{0:T(1024)S(1)}, f32[2048]{0:T(1024)S(1)}, u32[]{:S(2)}, u32[]{:S(2)}) collective-permute-start(f32[2048]{0:T(1024)S(1)} %add_add_fusion), channel_id=1, source_target_pairs={{0,4},{4,0},{1,5},{5,1},{2,6},{6,2},{3,7},{7,3},{8,12},{12,8},{9,1... | collective-permute-start | bytes 24584 | tf_op jit(solution)/shard_map/ppermute | solution.py:24
  49.1 0.6 %fusion.8 = bf16[1,1,4,4,512]{4,3,2,1,0:T(4,128)(2,1)} fusion(bf16[1,1,1,4,512]{4,3,2,1,0:T(4,128)(2,1)S(1)} %bitcast.110, bf16[1,1,1,4,512]{4,3,2,1,0:T(4,128)(2,1)S(1)} %bitcast.108, bf16[1,1,1,4,512]{4,3,2,1,0:T(4,128)(2,1)S(1)} %bitcast.106, bf16[1,1,1,4,512]{4,3,2,1,0:T(4,128)(2,1)S(1)} %get-tuple-element.15, bf16[2,2,1,4,512]{4,3,1,0,2:T(4,128)(2,1)S(1)} %rev.36, ...), kind=kLoop, calls=%fused_computation.21 | loop fusion | flops 40960 | bytes 65538 | tf_op jit(solution)/shard_map/jit(_where)/select_n | solution.py:17
  49.7 0.7 %reshape.308 = bf16[1,1,4,4,2048]{4,3,2,1,0:T(4,128)(2,1)} reshape(bf16[16,2048]{1,0:T(8,128)(2,1)S(1)} %get-tuple-element.4) | data formatting | bytes 131072 | tf_op jit(solution)/shard_map/reshape | solution.py:80
  50.4 0.9 %collective-permute-done.15 = f32[2048]{0:T(1024)S(1)} collective-permute-done((f32[2048]{0:T(1024)S(1)}, f32[2048]{0:T(1024)S(1)}, u32[]{:S(2)}, u32[]{:S(2)}) %collective-permute-start.15) | collective-permute-done | bytes 8224 | tf_op jit(solution)/shard_map/ppermute | solution.py:24
  51.3 0.6 %add.74 = f32[2048]{0:T(1024)} add(f32[2048]{0:T(1024)S(1)} %add_add_fusion, f32[2048]{0:T(1024)S(1)} %collective-permute-done.15) | non-fusion elementwise | flops 2048 | bytes 24576 | tf_op jit(solution)/shard_map/add | solution.py:41
  (29 shorter events, 0.4 us)
Async XLA Ops:
  0.6 21.7 %copy-start = (s32[1,1,4]{2,1,0:T(1,128)S(1)}, s32[1,1,4]{2,1,0:T(1,128)}, u32[]{:S(2)}) copy-start(s32[1,1,4]{2,1,0:T(1,128)} %param.7) | copy-start | bytes 52
  3.0 20.2 %collective-permute-start.3 = (bf16[4,512]{1,0:T(4,128)(2,1)S(1)}, bf16[4,512]{1,0:T(4,128)(2,1)S(1)}, u32[]{:S(2)}, u32[]{:S(2)}) collective-permute-start(bf16[4,512]{1,0:T(4,128)(2,1)S(1)} %get-tuple-element.13), channel_id=1, source_target_pairs={{0,8},{8,0},{16,24},{24,16},{1,9},{9,1},{17,25},{25,17},{2,10},{10... | collective-permute-start | bytes 12296 | tf_op jit(solution)/shard_map/ppermute | solution.py:24
  6.0 17.2 %collective-permute-start.4 = (bf16[4,512]{1,0:T(4,128)(2,1)S(1)}, bf16[4,512]{1,0:T(4,128)(2,1)S(1)}, u32[]{:S(2)}, u32[]{:S(2)}) collective-permute-start(bf16[4,512]{1,0:T(4,128)(2,1)S(1)} %get-tuple-element.12), channel_id=1, source_target_pairs={{0,16},{8,24},{16,0},{24,8},{1,17},{9,25},{17,1},{25,9},{2,18},{10... | collective-permute-start | bytes 12296 | tf_op jit(solution)/shard_map/ppermute | solution.py:24
  8.6 14.6 %collective-permute-start.5 = (bf16[4,512]{1,0:T(4,128)(2,1)S(1)}, bf16[4,512]{1,0:T(4,128)(2,1)S(1)}, u32[]{:S(2)}, u32[]{:S(2)}) collective-permute-start(bf16[4,512]{1,0:T(4,128)(2,1)S(1)} %get-tuple-element.11), channel_id=1, source_target_pairs={{0,24},{8,16},{16,8},{24,0},{1,25},{9,17},{17,9},{25,1},{2,26},{10... | collective-permute-start | bytes 12296 | tf_op jit(solution)/shard_map/ppermute | solution.py:24
  17.3 14.1 %collective-permute-start = (bf16[4,512]{1,0:T(4,128)(2,1)S(1)}, bf16[4,512]{1,0:T(4,128)(2,1)S(1)}, u32[]{:S(2)}, u32[]{:S(2)}) collective-permute-start(bf16[4,512]{1,0:T(4,128)(2,1)S(1)} %get-tuple-element.18), channel_id=1, source_target_pairs={{0,8},{8,0},{16,24},{24,16},{1,9},{9,1},{17,25},{25,17},{2,10},{10... | collective-permute-start | bytes 12296 | tf_op jit(solution)/shard_map/ppermute | solution.py:24
  18.3 13.6 %collective-permute-start.1 = (bf16[4,512]{1,0:T(4,128)(2,1)S(1)}, bf16[4,512]{1,0:T(4,128)(2,1)S(1)}, u32[]{:S(2)}, u32[]{:S(2)}) collective-permute-start(bf16[4,512]{1,0:T(4,128)(2,1)S(1)} %get-tuple-element.17), channel_id=1, source_target_pairs={{0,16},{8,24},{16,0},{24,8},{1,17},{9,25},{17,1},{25,9},{2,18},{10... | collective-permute-start | bytes 12296 | tf_op jit(solution)/shard_map/ppermute | solution.py:24
  23.1 14.8 %dynamic-slice-start = ((f32[8192]{0:T(1024)}, s32[]{:T(128)}), f32[2048]{0:T(1024)S(1)}, s32[]{:S(2)}) async-start(f32[8192]{0:T(1024)} %param.9, s32[]{:T(128)} %select_n.149), calls=%async_computation | async-start | bytes 16896 | tf_op jit(solution)/shard_map/dynamic_slice | solution.py:75
  23.1 8.9 %collective-permute-start.2 = (bf16[4,512]{1,0:T(4,128)(2,1)S(1)}, bf16[4,512]{1,0:T(4,128)(2,1)S(1)}, u32[]{:S(2)}, u32[]{:S(2)}) collective-permute-start(bf16[4,512]{1,0:T(4,128)(2,1)S(1)} %get-tuple-element.16), channel_id=1, source_target_pairs={{0,24},{8,16},{16,8},{24,0},{1,25},{9,17},{17,9},{25,1},{2,26},{10... | collective-permute-start | bytes 12296 | tf_op jit(solution)/shard_map/ppermute | solution.py:24
  23.5 10.2 %collective-permute-start.10 = (f32[16]{0:T(128)S(1)}, f32[16]{0:T(128)S(1)}, u32[]{:S(2)}, u32[]{:S(2)}) collective-permute-start(f32[16]{0:T(128)S(1)} %multiply_reduce_fusion.1), channel_id=1, source_target_pairs={{0,2},{1,3},{2,0},{3,1},{4,6},{5,7},{6,4},{7,5},{8,10},{9,11},{10,... | collective-permute-start | bytes 200 | tf_op jit(solution)/shard_map/ppermute | solution.py:24
  25.4 8.5 %collective-permute-start.11 = (f32[16]{0:T(128)S(1)}, f32[16]{0:T(128)S(1)}, u32[]{:S(2)}, u32[]{:S(2)}) collective-permute-start(f32[16]{0:T(128)S(1)} %multiply_reduce_fusion.1), channel_id=1, source_target_pairs={{0,3},{1,2},{2,1},{3,0},{4,7},{5,6},{6,5},{7,4},{8,11},{9,10},{10,... | collective-permute-start | bytes 200 | tf_op jit(solution)/shard_map/ppermute | solution.py:24
  31.4 2.4 %collective-permute-start.9 = (f32[16]{0:T(128)S(1)}, f32[16]{0:T(128)S(1)}, u32[]{:S(2)}, u32[]{:S(2)}) collective-permute-start(f32[16]{0:T(128)S(1)} %multiply_reduce_fusion.1), channel_id=1, source_target_pairs={{0,1},{1,0},{2,3},{3,2},{4,5},{5,4},{6,7},{7,6},{8,9},{9,8},{10,11... | collective-permute-start | bytes 200 | tf_op jit(solution)/shard_map/ppermute | solution.py:24
  31.9 2.0 %collective-permute-start.6 = (bf16[16,2048]{1,0:T(8,128)(2,1)S(1)}, bf16[16,2048]{1,0:T(8,128)(2,1)S(1)}, u32[]{:S(2)}, u32[]{:S(2)}) collective-permute-start(bf16[16,2048]{1,0:T(8,128)(2,1)S(1)} %get-tuple-element.7), channel_id=1, source_target_pairs={{0,1},{1,0},{2,3},{3,2},{4,5},{5,4},{6,7},{7,6},{8,9},{9,8},{10,11... | collective-permute-start | bytes 196616 | tf_op jit(solution)/shard_map/ppermute | solution.py:24
  32.0 4.4 %collective-permute-start.7 = (bf16[16,2048]{1,0:T(8,128)(2,1)S(1)}, bf16[16,2048]{1,0:T(8,128)(2,1)S(1)}, u32[]{:S(2)}, u32[]{:S(2)}) collective-permute-start(bf16[16,2048]{1,0:T(8,128)(2,1)S(1)} %get-tuple-element.9), channel_id=1, source_target_pairs={{0,2},{1,3},{2,0},{3,1},{4,6},{5,7},{6,4},{7,5},{8,10},{9,11},{10,... | collective-permute-start | bytes 196616 | tf_op jit(solution)/shard_map/ppermute | solution.py:24
  33.8 4.1 %collective-permute-start.8 = (bf16[16,2048]{1,0:T(8,128)(2,1)S(1)}, bf16[16,2048]{1,0:T(8,128)(2,1)S(1)}, u32[]{:S(2)}, u32[]{:S(2)}) collective-permute-start(bf16[16,2048]{1,0:T(8,128)(2,1)S(1)} %get-tuple-element.8), channel_id=1, source_target_pairs={{0,3},{1,2},{2,1},{3,0},{4,7},{5,6},{6,5},{7,4},{8,11},{9,10},{10,... | collective-permute-start | bytes 196616 | tf_op jit(solution)/shard_map/ppermute | solution.py:24
  38.0 4.5 %collective-permute-start.12 = (f32[2048]{0:T(1024)S(1)}, f32[2048]{0:T(1024)S(1)}, u32[]{:S(2)}, u32[]{:S(2)}) collective-permute-start(f32[2048]{0:T(1024)S(1)} %get-tuple-element.3), channel_id=1, source_target_pairs={{0,8},{8,0},{16,24},{24,16},{1,9},{9,1},{17,25},{25,17},{2,10},{10... | collective-permute-start | bytes 24584 | tf_op jit(solution)/shard_map/ppermute | solution.py:24
  38.3 5.4 %collective-permute-start.13 = (f32[2048]{0:T(1024)S(1)}, f32[2048]{0:T(1024)S(1)}, u32[]{:S(2)}, u32[]{:S(2)}) collective-permute-start(f32[2048]{0:T(1024)S(1)} %get-tuple-element.3), channel_id=1, source_target_pairs={{0,16},{8,24},{16,0},{24,8},{1,17},{9,25},{17,1},{25,9},{2,18},{10... | collective-permute-start | bytes 24584 | tf_op jit(solution)/shard_map/ppermute | solution.py:24
  42.2 5.4 %collective-permute-start.14 = (f32[2048]{0:T(1024)S(1)}, f32[2048]{0:T(1024)S(1)}, u32[]{:S(2)}, u32[]{:S(2)}) collective-permute-start(f32[2048]{0:T(1024)S(1)} %get-tuple-element.3), channel_id=1, source_target_pairs={{0,24},{8,16},{16,8},{24,0},{1,25},{9,17},{17,9},{25,1},{2,26},{10... | collective-permute-start | bytes 24584 | tf_op jit(solution)/shard_map/ppermute | solution.py:24
  47.6 3.7 %collective-permute-start.15 = (f32[2048]{0:T(1024)S(1)}, f32[2048]{0:T(1024)S(1)}, u32[]{:S(2)}, u32[]{:S(2)}) collective-permute-start(f32[2048]{0:T(1024)S(1)} %add_add_fusion), channel_id=1, source_target_pairs={{0,4},{4,0},{1,5},{5,1},{2,6},{6,2},{3,7},{7,3},{8,12},{12,8},{9,1... | collective-permute-start | bytes 24584 | tf_op jit(solution)/shard_map/ppermute | solution.py:24

commit v2 on v0

v2 whole, which is shorter than its diff:
```python
import functools

import jax
import jax.numpy as jnp
from jax import lax
from jax.experimental import pallas as pl
from jax.experimental.pallas import tpu as pltpu
from jax.sharding import PartitionSpec as P

LANES = 128
PIECES = 3
VMEM = pl.BlockSpec(memory_space=pltpu.VMEM)
SMEM = pl.BlockSpec(memory_space=pltpu.SMEM)
F32 = jnp.float32
BF16 = jnp.bfloat16


def partner(index, k, n):
    if n & (n - 1) == 0:
        return index ^ k, index ^ k
    return lax.rem(index + k, n), lax.rem(index + n - k, n)


def swap(x, axis, k):
    n = lax.axis_size(axis)
    return lax.ppermute(x, axis, [(i, int(partner(i, k, n)[0])) for i in range(n)])


def call(kernel, outs, args, scratch=(), smem=()):
    size = sum(a.size * a.dtype.itemsize for a in (*args, *outs))
    size += sum(4 * functools.reduce(lambda x, y: x * y, s) for s in scratch)
    return pl.pallas_call(
        kernel,
        out_shape=tuple(outs),
        in_specs=[SMEM if i in smem else VMEM for i in range(len(args))],
        out_specs=tuple(VMEM for _ in outs),
        scratch_shapes=[pltpu.VMEM(s, F32) for s in scratch],
        compiler_params=pltpu.CompilerParams(vmem_limit_bytes=int(1.25 * size) + 4 * 2**20),
    )(*args)


def norm_kernel(vis_ref, bias_ref, gain_ref, normed_ref, inv_ref, rows_ref):
    buckets, capacity, features = vis_ref.shape
    for q in range(buckets):
        rows_ref[q * capacity : (q + 1) * capacity, :] = vis_ref[q].astype(F32) + bias_ref[...]
    inputs = rows_ref[...]
    mean = jnp.sum(inputs * inputs, axis=1, keepdims=True) / features
    inv_rms = lax.rsqrt(mean + 1e-06)
    normed_ref[...] = (inputs * inv_rms * gain_ref[...]).astype(BF16)
    inv_ref[...] = jnp.broadcast_to(inv_rms, inv_ref.shape)


def project_kernel(normed_ref, weight_ref, projected_ref):
    projected_ref[...] = jnp.dot(normed_ref[...], weight_ref[...], preferred_element_type=F32)


def backward_kernel(enc, tp, *refs):
    counts_ref, projected_ref, weight_ref = refs[:3]
    cots, refs = refs[3 : 3 + enc], refs[3 + enc :]
    kv_ref, dots_ref, own_ref = refs[:3]
    sends, (picked_ref, masked_ref) = refs[3 : 2 + tp], refs[2 + tp :]
    buckets, capacity, columns = kv_ref.shape
    me, place = lax.axis_index("enc"), lax.axis_index("tp")
    for k in range(enc):
        picked_ref[partner(me, k, enc)[1]] = cots[k][me].astype(F32)
    slot = lax.broadcasted_iota(jnp.int32, (capacity, columns), 0)
    for q in range(buckets):
        rows = slice(q * capacity, (q + 1) * capacity)
        live = slot < counts_ref[0, q]
        masked_ref[rows, :] = jnp.where(live, picked_ref[q], 0.0)
        kv_ref[q] = jnp.where(live, projected_ref[rows, :], 0.0)
    masked = masked_ref[...]
    dots = jnp.sum(masked * projected_ref[...], axis=1, keepdims=True)
    dots = jnp.broadcast_to(dots, dots_ref.shape)
    dots_ref[...] = dots
    lane = lax.broadcasted_iota(jnp.int32, dots.shape, 1)
    pieces, rest = jnp.zeros(dots.shape, F32), dots
    for i in range(PIECES):
        piece = rest.astype(BF16).astype(F32)
        pieces = jnp.where(lane == i, piece, pieces)
        rest = rest - piece
    lhs = masked.astype(BF16)
    width = own_ref.shape[1]
    for k in [*range(1, tp), 0]:
        start = pl.multiple_of(partner(place, k, tp)[0] * width, width)
        part = lax.dot_general(
            lhs,
            weight_ref[pl.ds(start, width), :],
            (((1,), (1,)), ((), ())),
            preferred_element_type=F32,
        )
        if k:
            sends[k - 1][:, :width] = part.astype(BF16)
            sends[k - 1][:, width:] = pieces.astype(BF16)
        else:
            own_ref[...] = part


def combine_kernel(enc, tp, *refs):
    vis_ref, bias_ref, gain_ref, inv_ref, kv_ref, dots_ref, own_ref = refs[:7]
    gots, refs = refs[7 : 6 + tp], refs[6 + tp :]
    grad_ref, total_ref = refs[:2]
    sends, (rows_ref,) = refs[2 : 1 + enc], refs[1 + enc :]
    buckets, capacity, features = vis_ref.shape
    width = own_ref.shape[1]
    me, place = lax.axis_index("enc"), lax.axis_index("tp")
    own = pl.ds(pl.multiple_of(place * width, width), width)
    for q in range(buckets):
        rows_ref[q * capacity : (q + 1) * capacity, :] = (
            vis_ref[q, :, own].astype(F32) + bias_ref[:, own]
        )
    grad_normed, row_dot = own_ref[...], dots_ref[:, :1]
    for got in gots:
        grad_normed = grad_normed + got[:, :width].astype(F32)
        row_dot = row_dot + jnp.sum(got[:, width:].astype(F32), axis=1, keepdims=True)
    inv_rms = inv_ref[:, :1]
    grad_rows = (
        inv_rms * gain_ref[:, own] * grad_normed
        - rows_ref[...] * (inv_rms * inv_rms) * row_dot / features
    )
    grad_ref[...] = grad_rows
    total = jnp.sum(grad_rows, axis=0, keepdims=True)
    chunks = width // LANES
    for j in range(chunks):
        total_ref[j : j + 1, :] = total[:, j * LANES : (j + 1) * LANES]
    for k in range(1, enc):
        sends[k - 1][:chunks, :] = total_ref[...]
        block = kv_ref[partner(me, k, enc)[0]]
        for j in range(block.shape[1] // LANES):
            at = chunks + j * capacity
            sends[k - 1][at : at + capacity, :] = block[:, j * LANES : (j + 1) * LANES]


def round_kernel(grad_ref, out_ref):
    buckets, capacity, _ = out_ref.shape
    for q in range(buckets):
        out_ref[q] = grad_ref[q * capacity : (q + 1) * capacity, :].astype(BF16)


def sum_kernel(chunks, *refs):
    total = refs[0][...]
    for got in refs[1:-1]:
        total = total + got[:chunks, :]
    refs[-1][...] = total


def keys_kernel(enc, kv_ref, *refs):
    gots, out_ref = refs[: enc - 1], refs[enc - 1]
    buckets, capacity, columns = kv_ref.shape
    me = lax.axis_index("enc")
    out_ref[me] = kv_ref[me].astype(BF16)
    chunks = gots[0].shape[0] - capacity * columns // LANES
    for k in range(1, enc):
        source = partner(me, k, enc)[1]
        for j in range(columns // LANES):
            at = chunks + j * capacity
            out_ref[source, :, j * LANES : (j + 1) * LANES] = gots[k - 1][
                at : at + capacity, :
            ].astype(BF16)


def per_device(visual, counts, merger_bias, norm_gain, kv_weight, kv_cotangent):
    buckets, capacity, features = visual.shape[2:]
    enc, llm, tp = (lax.axis_size(a) for a in ("enc", "llm", "tp"))
    width, columns, rows = features // tp, kv_weight.shape[1], buckets * capacity
    chunks = width // LANES
    vis, bias, gain = visual[0, 0], merger_bias[None], norm_gain[None]
    own_cot = kv_cotangent[0, 0]
    struct = jax.ShapeDtypeStruct

    cots = [own_cot] + [swap(own_cot, "enc", k) for k in range(1, enc)]
    normed, inv_rms = call(
        norm_kernel,
        (struct((rows, features), BF16), struct((rows, LANES), F32)),
        (vis, bias, gain),
        scratch=[(rows, features)],
    )
    (projected,) = call(project_kernel, (struct((rows, columns), F32),), (normed, kv_weight))
    kv, dots, own, *sends = call(
        functools.partial(backward_kernel, enc, tp),
        (
            struct((buckets, capacity, columns), F32),
            struct((rows, LANES), F32),
            struct((rows, width), F32),
            *[struct((rows, width + LANES), BF16)] * (tp - 1),
        ),
        (counts[0], projected, kv_weight, *cots),
        scratch=[(buckets, capacity, columns), (rows, columns)],
        smem=(0,),
    )
    gots = [swap(s, "tp", k + 1) for k, s in enumerate(sends)]
    grad, total, *sends = call(
        functools.partial(combine_kernel, enc, tp),
        (
            struct((rows, width), F32),
            struct((chunks, LANES), F32),
            *[struct((chunks + capacity * columns // LANES, LANES), F32)] * (enc - 1),
        ),
        (vis, bias, gain, inv_rms, kv, dots, own, *gots),
        scratch=[(rows, width)],
    )
    gots = [swap(s, "enc", k + 1) for k, s in enumerate(sends)]
    (visual_grad,) = call(round_kernel, (struct((buckets, capacity, width), BF16),), (grad,))
    add = functools.partial(sum_kernel, chunks)
    (total,) = call(add, (struct((chunks, LANES), F32),), (total, *gots))
    others = [swap(total, "llm", k) for k in range(1, llm)]
    (key_values,) = call(
        functools.partial(keys_kernel, enc),
        (struct((buckets, capacity, columns), BF16),),
        (kv, *gots),
    )
    (bias_grad,) = call(add, (struct((chunks, LANES), F32),), (total, *others))
    return (key_values[None, None], visual_grad[None, None], bias_grad.reshape(width))


def solution(mesh):
    return jax.shard_map(
        per_device,
        mesh=mesh,
        in_specs=(
            P("enc", "llm", None, None, None),
            P("enc", "llm", None),
            P(),
            P(),
            P(None, "tp"),
            P("enc", "llm", None, None, "tp"),
        ),
        out_specs=(P("enc", "llm", None, None, "tp"), P("enc", "llm", None, None, "tp"), P("tp")),
        check_vma=False,
    )
```

time: 91.3 us -> 39.3 us (0.43)
  blocking collectives: 35.6 us -> 0 us
  between operations: 14.1 us -> 0.71 us
  matrix products: 11.3 us -> 0 us
  Pallas kernels: 0 us -> 6.39 us
  waiting for transfers between devices: 7 us -> 10.3 us
  other arithmetic: 1.78 us -> 0 us
  local copies, waits for them, and re-layouts: 6.76 us -> 8 us
    psum x1 -> x0, blocking collectives: 22.6 us -> none  [per_device(): bias_grad = lax.psum(bias_part, ('enc', 'llm'))]
    all_to_all x3 -> x0, starting transfers between devices: 14.2 us -> none  [the longest x1 6.32 us: per_device(): lax.all_to_all(counts[0, 0], 'enc', split_axis=0, concat_axis=0, tiled=True)]
    ppermute x0 -> x10, starting transfers between devices: none -> 13.6 us  [swap(): lax.ppermute(x, axis, [(i, int(partner(i, k, n)[0])) for i in range(n)])]
    dot_general x2 -> x0, matrix products: 11.3 us -> none  [the longest x1 6.48 us: per_device(): lax.dot_general(masked, kv_weight, (((1,), (1,)), ((), ())), preferred_el...]
    ppermute x0 -> x10, waiting for transfers between devices: none -> 10.3 us  [swap(): lax.ppermute(x, axis, [(i, int(partner(i, k, n)[0])) for i in range(n)])]
    unnamed x1 -> x0, blocking collectives: 7.14 us -> none
    pallas_call x0 -> x8, Pallas kernels: none -> 6.39 us  [call(): pl.pallas_call(kernel, out_shape=tuple(outs), in_specs=[SMEM if i in smem...]
    unnamed x8 -> x20, local copies, waits for them, and re-layouts: 1.9 us -> 8 us
  transfers between devices with their start and end apart: 4 -> 10, of which waited for: 2 -> 5; matrix products, arithmetic and copies ran while one was open for 18% -> 0% of each run, Pallas kernels for 0% -> 7%
where the time goes in v2:
time: 39.3 us; the launch traced here: 38.9 us
  starting transfers between devices  13.6 us (35%)
  waiting for transfers between devices  10.3 us (26%)
  local copies, waits for them, and re-layouts  8 us (20%)
  Pallas kernels  6.39 us (16%)
  between operations  0.71 us (2%)
    ppermute x10, starting transfers between devices, swap(): lax.ppermute(x, axis, [(i, int(partner(i, k, n)[0])) for i in range(n)])  13.6 us
    ppermute x10, waiting for transfers between devices, swap(): lax.ppermute(x, axis, [(i, int(partner(i, k, n)[0])) for i in range(n)])  10.3 us
    unnamed x20, local copies, waits for them, and re-layouts  8 us
    pallas_call x8, Pallas kernels, call(): pl.pallas_call(kernel, out_shape=tuple(outs), in_specs=[SMEM if i in smem...  6.39 us
  transfers between devices with their start and end apart: 10, of which 5 were waited for; matrix products, arithmetic and copies ran while one was open for 0% of the time, Pallas kernels for 7%

profile of v2, /device:TPU:0, one launch (start us, length us, event | category | flops | bytes accessed | tf_op | source)
XLA Modules:
  0.0 38.9 jit_solution(10514246927753299200)
XLA Ops:
  0.6 0.0 copy-start.9
  0.6 5.1 %collective-permute-start.2 = (bf16[4,4,512]{2,1,0:T(4,128)(2,1)}, bf16[4,4,512]{2,1,0:T(4,128)(2,1)S(1)}, u32[]{:S(2)}, u32[]{:S(2)}) collective-permute-start(bf16[4,4,512]{2,1,0:T(4,128)(2,1)} %bitcast.14), channel_id=1, source_target_pairs={{0,24},{8,16},{16,8},{24,0},{1,25},{9,17},{17,9},{25,1},{2,26},{10... | collective-permute-start | bytes 49160 | tf_op jit(solution)/shard_map/ppermute | solution.py:26
  5.8 0.0 collective-permute-start.1
  5.8 0.6 %collective-permute-start = (bf16[4,4,512]{2,1,0:T(4,128)(2,1)}, bf16[4,4,512]{2,1,0:T(4,128)(2,1)S(1)}, u32[]{:S(2)}, u32[]{:S(2)}) collective-permute-start(bf16[4,4,512]{2,1,0:T(4,128)(2,1)} %bitcast.16), channel_id=1, source_target_pairs={{0,8},{8,0},{16,24},{24,16},{1,9},{9,1},{17,25},{25,17},{2,10},{10... | collective-permute-start | bytes 49160 | tf_op jit(solution)/shard_map/ppermute | solution.py:26
  6.4 0.0 copy-start.2
  6.4 0.9 %copy-done.2 = bf16[1,1,4,4,8192]{4,3,2,1,0:T(4,128)(2,1)S(1)} copy-done((bf16[1,1,4,4,8192]{4,3,2,1,0:T(4,128)(2,1)S(1)}, bf16[1,1,4,4,8192]{4,3,2,1,0:T(4,128)(2,1)}, u32[]{:S(2)}) %copy-start.2) | copy-done | bytes 262168
  7.3 0.0 copy-start.4
  7.3 0.8 %copy-done.4 = f32[8192]{0:T(1024)S(1)} copy-done((f32[8192]{0:T(1024)S(1)}, f32[8192]{0:T(1024)}, u32[]{:S(2)}) %copy-start.4) | copy-done | bytes 32792
  8.1 0.0 copy-start.6
  8.1 0.8 %copy-done.6 = f32[8192]{0:T(1024)S(1)} copy-done((f32[8192]{0:T(1024)S(1)}, f32[8192]{0:T(1024)}, u32[]{:S(2)}) %copy-start.6) | copy-done | bytes 32792
  8.9 0.0 copy-start.8
  8.9 0.3 shard_map.85
  9.2 0.0 copy-start
  9.2 3.4 %copy-done = bf16[8192,512]{1,0:T(8,128)(2,1)S(1)} copy-done((bf16[8192,512]{1,0:T(8,128)(2,1)S(1)}, bf16[8192,512]{1,0:T(8,128)(2,1)}, u32[]{:S(2)}) %copy-start) | copy-done | bytes 8388632
  12.6 0.0 copy-start.1
  12.6 0.0 copy-start.3
  12.6 0.0 copy-start.5
  12.6 0.0 copy-start.7
  12.6 1.2 %shard_map.86.refs_1_ = f32[16,512]{1,0:T(8,128)S(1)} custom-call(bf16[16,8192]{1,0:T(8,128)(2,1)S(1)} %get-tuple-element.16.normed_ref, bf16[8192,512]{1,0:T(8,128)(2,1)S(1)} %copy-done), custom_call_target="tpu_custom_call" | custom-call | tf_op jit(solution)/shard_map/pallas_call | solution.py:32
  13.7 0.0 collective-permute-done.2.refs_6_
  13.8 0.0 collective-permute-done.1.refs_5_
  13.8 0.0 collective-permute-done.refs_4_
  13.8 0.0 copy-done.9
  13.8 0.0 copy-done.8
  13.8 2.1 %copy-done.1 = bf16[8192,512]{1,0:T(8,128)(2,1)S(1)} copy-done((bf16[8192,512]{1,0:T(8,128)(2,1)S(1)}, bf16[8192,512]{1,0:T(8,128)(2,1)}, u32[]{:S(2)}) %copy-start.1) | copy-done | bytes 8388632
  15.9 2.8 %shard_map.87 = (f32[4,4,512]{2,1,0:T(4,128)S(1)}, f32[16,128]{1,0:T(8,128)S(1)}, f32[16,2048]{1,0:T(8,128)S(1)}, bf16[16,2176]{1,0:T(8,128)(2,1)S(1)}, bf16[16,...) custom-call(s32[1,4]{1,0:T(1,128)S(1)} %bitcast.18, f32[16,512]{1,0:T(8,128)S(1)} %shard_map.86.refs_1_, ...), custom_call_target="tpu_custom_call" | custom-call | tf_op jit(solution)/shard_map/pallas_call | solution.py:32
  18.8 0.0 collective-permute-start.3
  18.8 1.7 %collective-permute-start.4 = (bf16[16,2176]{1,0:T(8,128)(2,1)S(1)}, bf16[16,2176]{1,0:T(8,128)(2,1)S(1)}, u32[]{:S(2)}, u32[]{:S(2)}) collective-permute-start(bf16[16,2176]{1,0:T(8,128)(2,1)S(1)} %get-tuple-element.22), channel_id=1, source_target_pairs={{0,2},{1,3},{2,0},{3,1},{4,6},{5,7},{6,4},{7,5},{8,10},{9,11},{10,... | collective-permute-start | bytes 208904 | tf_op jit(solution)/shard_map/ppermute | solution.py:26
  20.5 0.1 collective-permute-start.5
  20.6 0.0 collective-permute-done.3.refs_7_
  20.7 2.7 %collective-permute-done.4.refs_8_ = bf16[16,2176]{1,0:T(8,128)(2,1)S(1)} collective-permute-done((bf16[16,2176]{1,0:T(8,128)(2,1)S(1)}, bf16[16,2176]{1,0:T(8,128)(2,1)S(1)}, u32[]{:S(2)}, u32[]{:S(2)}) %collective-permute-start.4) | collective-permute-done | bytes 69664 | tf_op jit(solution)/shard_map/ppermute | solution.py:26
  23.4 1.3 %collective-permute-done.5.refs_9_ = bf16[16,2176]{1,0:T(8,128)(2,1)S(1)} collective-permute-done((bf16[16,2176]{1,0:T(8,128)(2,1)S(1)}, bf16[16,2176]{1,0:T(8,128)(2,1)S(1)}, u32[]{:S(2)}, u32[]{:S(2)}) %collective-permute-start.5) | collective-permute-done | bytes 69664 | tf_op jit(solution)/shard_map/ppermute | solution.py:26
  24.7 0.0 copy-done.3
  24.7 0.0 copy-done.5
  24.7 0.0 copy-done.7
  24.7 0.2 shard_map.88
  24.9 1.3 %collective-permute-start.6 = (f32[32,128]{1,0:T(8,128)S(1)}, f32[32,128]{1,0:T(8,128)S(1)}, u32[]{:S(2)}, u32[]{:S(2)}) collective-permute-start(f32[32,128]{1,0:T(8,128)S(1)} %get-tuple-element.24), channel_id=1, source_target_pairs={{0,8},{8,0},{16,24},{24,16},{1,9},{9,1},{17,25},{25,17},{2,10},{10... | collective-permute-start | bytes 49160 | tf_op jit(solution)/shard_map/ppermute | solution.py:26
  26.2 2.9 %collective-permute-start.7 = (f32[32,128]{1,0:T(8,128)S(1)}, f32[32,128]{1,0:T(8,128)S(1)}, u32[]{:S(2)}, u32[]{:S(2)}) collective-permute-start(f32[32,128]{1,0:T(8,128)S(1)} %get-tuple-element.25), channel_id=1, source_target_pairs={{0,16},{8,24},{16,0},{24,8},{1,17},{9,25},{17,1},{25,9},{2,18},{10... | collective-permute-start | bytes 49160 | tf_op jit(solution)/shard_map/ppermute | solution.py:26
  29.1 0.2 collective-permute-start.8
  29.4 0.0 collective-permute-done.6.refs_0_.refs_1_
  29.4 1.5 %collective-permute-done.7.refs_1_.refs_2_ = f32[32,128]{1,0:T(8,128)S(1)} collective-permute-done((f32[32,128]{1,0:T(8,128)S(1)}, f32[32,128]{1,0:T(8,128)S(1)}, u32[]{:S(2)}, u32[]{:S(2)}) %collective-permute-start.7) | collective-permute-done | bytes 16416 | tf_op jit(solution)/shard_map/ppermute | solution.py:26
  30.9 3.8 %collective-permute-done.8.refs_2_.refs_3_ = f32[32,128]{1,0:T(8,128)S(1)} collective-permute-done((f32[32,128]{1,0:T(8,128)S(1)}, f32[32,128]{1,0:T(8,128)S(1)}, u32[]{:S(2)}, u32[]{:S(2)}) %collective-permute-start.8) | collective-permute-done | bytes 16416 | tf_op jit(solution)/shard_map/ppermute | solution.py:26
  34.7 1.5 %collective-permute-start.9 = (f32[16,128]{1,0:T(8,128)S(1)}, f32[16,128]{1,0:T(8,128)S(1)}, u32[]{:S(2)}, u32[]{:S(2)}) collective-permute-start(f32[16,128]{1,0:T(8,128)S(1)} %shard_map.91.refs_0_), channel_id=1, source_target_pairs={{0,4},{4,0},{1,5},{5,1},{2,6},{6,2},{3,7},{7,3},{8,12},{12,8},{9,1... | collective-permute-start | bytes 24584 | tf_op jit(solution)/shard_map/ppermute | solution.py:26
  36.2 0.6 %shard_map.90 = bf16[4,4,2048]{2,1,0:T(4,128)(2,1)} custom-call(f32[16,2048]{1,0:T(8,128)S(1)} %get-tuple-element.27.grad_ref), custom_call_target="tpu_custom_call" | custom-call | tf_op jit(solution)/shard_map/pallas_call | solution.py:32
  36.8 0.6 %shard_map.89 = bf16[4,4,512]{2,1,0:T(4,128)(2,1)} custom-call(f32[4,4,512]{2,1,0:T(4,128)S(1)} %get-tuple-element.17.refs_4_.kv_ref, f32[32,128]{1,0:T(8,128)S(1)} %collective-permute-done.6.refs_0_.refs_1_, f32[32,128]{1,0:T(8,128)S(1)} %collective-permute-done.7.refs_1_.refs_2_, f32[32,128]{1,0:T(8,128)S(1)} %collective-permute-done.8.refs_2_.refs_3_), custom_call_target="tpu_custom_call" | custom-call | tf_op jit(solution)/shard_map/pallas_call | solution.py:32
  37.4 0.9 %collective-permute-done.9.refs_1_ = f32[16,128]{1,0:T(8,128)S(1)} collective-permute-done((f32[16,128]{1,0:T(8,128)S(1)}, f32[16,128]{1,0:T(8,128)S(1)}, u32[]{:S(2)}, u32[]{:S(2)}) %collective-permute-start.9) | collective-permute-done | bytes 8224 | tf_op jit(solution)/shard_map/ppermute | solution.py:26
  38.3 0.6 %shard_map.92 = f32[16,128]{1,0:T(8,128)} custom-call(f32[16,128]{1,0:T(8,128)S(1)} %shard_map.91.refs_0_, f32[16,128]{1,0:T(8,128)S(1)} %collective-permute-done.9.refs_1_), custom_call_target="tpu_custom_call" | custom-call | tf_op jit(solution)/shard_map/pallas_call | solution.py:32
  (1 shorter events, 0.0 us)
Async XLA Ops:
  0.6 13.1 %copy-start.9 = (s32[1,1,4]{2,1,0:T(1,128)S(1)}, s32[1,1,4]{2,1,0:T(1,128)}, u32[]{:S(2)}) copy-start(s32[1,1,4]{2,1,0:T(1,128)} %param.7) | copy-start | bytes 52
  0.6 13.1 %collective-permute-start.2 = (bf16[4,4,512]{2,1,0:T(4,128)(2,1)}, bf16[4,4,512]{2,1,0:T(4,128)(2,1)S(1)}, u32[]{:S(2)}, u32[]{:S(2)}) collective-permute-start(bf16[4,4,512]{2,1,0:T(4,128)(2,1)} %bitcast.14), channel_id=1, source_target_pairs={{0,24},{8,16},{16,8},{24,0},{1,25},{9,17},{17,9},{25,1},{2,26},{10... | collective-permute-start | bytes 49160 | tf_op jit(solution)/shard_map/ppermute | solution.py:26
  5.8 8.0 %collective-permute-start.1 = (bf16[4,4,512]{2,1,0:T(4,128)(2,1)}, bf16[4,4,512]{2,1,0:T(4,128)(2,1)S(1)}, u32[]{:S(2)}, u32[]{:S(2)}) collective-permute-start(bf16[4,4,512]{2,1,0:T(4,128)(2,1)} %bitcast.15), channel_id=1, source_target_pairs={{0,16},{8,24},{16,0},{24,8},{1,17},{9,25},{17,1},{25,9},{2,18},{10... | collective-permute-start | bytes 49160 | tf_op jit(solution)/shard_map/ppermute | solution.py:26
  5.8 8.0 %collective-permute-start = (bf16[4,4,512]{2,1,0:T(4,128)(2,1)}, bf16[4,4,512]{2,1,0:T(4,128)(2,1)S(1)}, u32[]{:S(2)}, u32[]{:S(2)}) collective-permute-start(bf16[4,4,512]{2,1,0:T(4,128)(2,1)} %bitcast.16), channel_id=1, source_target_pairs={{0,8},{8,0},{16,24},{24,16},{1,9},{9,1},{17,25},{25,17},{2,10},{10... | collective-permute-start | bytes 49160 | tf_op jit(solution)/shard_map/ppermute | solution.py:26
  6.4 0.9 %copy-start.2 = (bf16[1,1,4,4,8192]{4,3,2,1,0:T(4,128)(2,1)S(1)}, bf16[1,1,4,4,8192]{4,3,2,1,0:T(4,128)(2,1)}, u32[]{:S(2)}) copy-start(bf16[1,1,4,4,8192]{4,3,2,1,0:T(4,128)(2,1)} %param.6) | copy-start | bytes 786436
  7.3 0.8 %copy-start.4 = (f32[8192]{0:T(1024)S(1)}, f32[8192]{0:T(1024)}, u32[]{:S(2)}) copy-start(f32[8192]{0:T(1024)} %param.8) | copy-start | bytes 98308
  8.1 0.8 %copy-start.6 = (f32[8192]{0:T(1024)S(1)}, f32[8192]{0:T(1024)}, u32[]{:S(2)}) copy-start(f32[8192]{0:T(1024)} %param.9) | copy-start | bytes 98308
  8.9 4.9 %copy-start.8 = (bf16[1,1,4,4,512]{4,3,2,1,0:T(4,128)(2,1)S(1)}, bf16[1,1,4,4,512]{4,3,2,1,0:T(4,128)(2,1)}, u32[]{:S(2)}) copy-start(bf16[1,1,4,4,512]{4,3,2,1,0:T(4,128)(2,1)} %param.11) | copy-start | bytes 49156
  9.2 3.4 %copy-start = (bf16[8192,512]{1,0:T(8,128)(2,1)S(1)}, bf16[8192,512]{1,0:T(8,128)(2,1)}, u32[]{:S(2)}) copy-start(bf16[8192,512]{1,0:T(8,128)(2,1)} %refs_2_.1) | copy-start | bytes 25165828
  12.6 3.4 %copy-start.1 = (bf16[8192,512]{1,0:T(8,128)(2,1)S(1)}, bf16[8192,512]{1,0:T(8,128)(2,1)}, u32[]{:S(2)}) copy-start(bf16[8192,512]{1,0:T(8,128)(2,1)} %refs_2_.1) | copy-start | bytes 25165828
  12.6 12.2 %copy-start.3 = (bf16[1,1,4,4,8192]{4,3,2,1,0:T(4,128)(2,1)S(1)}, bf16[1,1,4,4,8192]{4,3,2,1,0:T(4,128)(2,1)}, u32[]{:S(2)}) copy-start(bf16[1,1,4,4,8192]{4,3,2,1,0:T(4,128)(2,1)} %param.6) | copy-start | bytes 786436
  12.6 12.2 %copy-start.5 = (f32[8192]{0:T(1024)S(1)}, f32[8192]{0:T(1024)}, u32[]{:S(2)}) copy-start(f32[8192]{0:T(1024)} %param.8) | copy-start | bytes 98308
  12.6 12.2 %copy-start.7 = (f32[8192]{0:T(1024)S(1)}, f32[8192]{0:T(1024)}, u32[]{:S(2)}) copy-start(f32[8192]{0:T(1024)} %param.9) | copy-start | bytes 98308
  18.8 1.9 %collective-permute-start.3 = (bf16[16,2176]{1,0:T(8,128)(2,1)S(1)}, bf16[16,2176]{1,0:T(8,128)(2,1)S(1)}, u32[]{:S(2)}, u32[]{:S(2)}) collective-permute-start(bf16[16,2176]{1,0:T(8,128)(2,1)S(1)} %get-tuple-element.21), channel_id=1, source_target_pairs={{0,1},{1,0},{2,3},{3,2},{4,5},{5,4},{6,7},{7,6},{8,9},{9,8},{10,11... | collective-permute-start | bytes 208904 | tf_op jit(solution)/shard_map/ppermute | solution.py:26
  18.8 4.6 %collective-permute-start.4 = (bf16[16,2176]{1,0:T(8,128)(2,1)S(1)}, bf16[16,2176]{1,0:T(8,128)(2,1)S(1)}, u32[]{:S(2)}, u32[]{:S(2)}) collective-permute-start(bf16[16,2176]{1,0:T(8,128)(2,1)S(1)} %get-tuple-element.22), channel_id=1, source_target_pairs={{0,2},{1,3},{2,0},{3,1},{4,6},{5,7},{6,4},{7,5},{8,10},{9,11},{10,... | collective-permute-start | bytes 208904 | tf_op jit(solution)/shard_map/ppermute | solution.py:26
  20.5 4.2 %collective-permute-start.5 = (bf16[16,2176]{1,0:T(8,128)(2,1)S(1)}, bf16[16,2176]{1,0:T(8,128)(2,1)S(1)}, u32[]{:S(2)}, u32[]{:S(2)}) collective-permute-start(bf16[16,2176]{1,0:T(8,128)(2,1)S(1)} %get-tuple-element.23), channel_id=1, source_target_pairs={{0,3},{1,2},{2,1},{3,0},{4,7},{5,6},{6,5},{7,4},{8,11},{9,10},{10,... | collective-permute-start | bytes 208904 | tf_op jit(solution)/shard_map/ppermute | solution.py:26
  24.9 4.5 %collective-permute-start.6 = (f32[32,128]{1,0:T(8,128)S(1)}, f32[32,128]{1,0:T(8,128)S(1)}, u32[]{:S(2)}, u32[]{:S(2)}) collective-permute-start(f32[32,128]{1,0:T(8,128)S(1)} %get-tuple-element.24), channel_id=1, source_target_pairs={{0,8},{8,0},{16,24},{24,16},{1,9},{9,1},{17,25},{25,17},{2,10},{10... | collective-permute-start | bytes 49160 | tf_op jit(solution)/shard_map/ppermute | solution.py:26
  26.2 4.6 %collective-permute-start.7 = (f32[32,128]{1,0:T(8,128)S(1)}, f32[32,128]{1,0:T(8,128)S(1)}, u32[]{:S(2)}, u32[]{:S(2)}) collective-permute-start(f32[32,128]{1,0:T(8,128)S(1)} %get-tuple-element.25), channel_id=1, source_target_pairs={{0,16},{8,24},{16,0},{24,8},{1,17},{9,25},{17,1},{25,9},{2,18},{10... | collective-permute-start | bytes 49160 | tf_op jit(solution)/shard_map/ppermute | solution.py:26
  29.1 5.5 %collective-permute-start.8 = (f32[32,128]{1,0:T(8,128)S(1)}, f32[32,128]{1,0:T(8,128)S(1)}, u32[]{:S(2)}, u32[]{:S(2)}) collective-permute-start(f32[32,128]{1,0:T(8,128)S(1)} %get-tuple-element.26), channel_id=1, source_target_pairs={{0,24},{8,16},{16,8},{24,0},{1,25},{9,17},{17,9},{25,1},{2,26},{10... | collective-permute-start | bytes 49160 | tf_op jit(solution)/shard_map/ppermute | solution.py:26
  34.7 3.7 %collective-permute-start.9 = (f32[16,128]{1,0:T(8,128)S(1)}, f32[16,128]{1,0:T(8,128)S(1)}, u32[]{:S(2)}, u32[]{:S(2)}) collective-permute-start(f32[16,128]{1,0:T(8,128)S(1)} %shard_map.91.refs_0_), channel_id=1, source_target_pairs={{0,4},{4,0},{1,5},{5,1},{2,6},{6,2},{3,7},{7,3},{8,12},{12,8},{9,1... | collective-permute-start | bytes 24584 | tf_op jit(solution)/shard_map/ppermute | solution.py:26

commit v3 on v2

v3 whole, which is shorter than its diff:
```python
import functools

import jax
import jax.numpy as jnp
from jax import lax
from jax.experimental import pallas as pl
from jax.experimental.pallas import tpu as pltpu
from jax.sharding import PartitionSpec as P

LANES = 128
PIECES = 3
VMEM = pl.BlockSpec(memory_space=pltpu.VMEM)
SMEM = pl.BlockSpec(memory_space=pltpu.SMEM)
HBM = pl.BlockSpec(memory_space=pltpu.HBM)
F32 = jnp.float32
BF16 = jnp.bfloat16


def swap(x, axis, k):
    n = lax.axis_size(axis)
    return lax.ppermute(x, axis, [(i, i ^ k) for i in range(n)])


def call(limit, kernel, outs, args, scratch=(), specs=None):
    return pl.pallas_call(
        kernel,
        out_shape=tuple(outs),
        in_specs=specs or [VMEM] * len(args),
        out_specs=tuple(VMEM for _ in outs),
        scratch_shapes=list(scratch),
        compiler_params=pltpu.CompilerParams(vmem_limit_bytes=limit),
    )(*args)


def norm_kernel(
    vis_hbm, bias_hbm, gain_hbm, cot_hbm, _, cot_ref, vis_ref, bias_ref, gain_ref,
    normed_ref, inv_ref, rows_ref, sems,
):
    pairs = [(cot_hbm, cot_ref), (vis_hbm, vis_ref), (bias_hbm, bias_ref), (gain_hbm, gain_ref)]
    copies = [pltpu.make_async_copy(a, b, sems.at[i]) for i, (a, b) in enumerate(pairs)]
    for copy in copies:
        copy.start()
    for copy in copies:
        copy.wait()
    buckets, capacity, features = vis_ref.shape
    for q in range(buckets):
        rows_ref[q * capacity : (q + 1) * capacity, :] = vis_ref[q].astype(F32) + bias_ref[...]
    inputs = rows_ref[...]
    mean = jnp.sum(inputs * inputs, axis=1, keepdims=True) / features
    inv_rms = lax.rsqrt(mean + 1e-06)
    normed_ref[...] = (inputs * inv_rms * gain_ref[...]).astype(BF16)
    inv_ref[...] = jnp.broadcast_to(inv_rms, inv_ref.shape)


def project_kernel(normed_ref, weight_ref, projected_ref):
    projected_ref[...] = jnp.dot(normed_ref[...], weight_ref[...], preferred_element_type=F32)


def split(value, dtype):
    if dtype == F32:
        return [value]
    pieces = []
    for _ in range(PIECES):
        pieces.append(value.astype(dtype))
        value = value - pieces[-1].astype(F32)
    return pieces


def side(count, rows, dtype):
    return LANES + len(split_shape(dtype)) * -(-count // rows) * LANES


def split_shape(dtype):
    return range(1 if dtype == F32 else PIECES)


def put_side(send_ref, start, dots, row, at, count):
    rows, dtype = send_ref.shape[0], send_ref.dtype
    if dots is not None:
        lane = lax.broadcasted_iota(jnp.int32, dots.shape, 1)
        block = jnp.zeros(dots.shape, F32)
        for i, piece in enumerate(split(dots, dtype)):
            block = jnp.where(lane == i, piece.astype(F32), block)
        send_ref[:, start : start + LANES] = block.astype(dtype)
    blocks = (send_ref.shape[1] - start) // LANES - 1
    blocks //= len(split_shape(dtype))
    for i, piece in enumerate(split(row, dtype)):
        for j in range(count):
            line, col = (at + j) % rows, start + LANES * (1 + i * blocks + (at + j) // rows)
            send_ref[line : line + 1, col : col + LANES] = piece[:, j * LANES : (j + 1) * LANES]


def get_dots(got_ref, start):
    return jnp.sum(got_ref[:, start : start + LANES].astype(F32), axis=1, keepdims=True)


def get_side(got_ref, start, at, count):
    rows, dtype = got_ref.shape[0], got_ref.dtype
    blocks = (got_ref.shape[1] - start) // LANES - 1
    blocks //= len(split_shape(dtype))
    out = []
    for j in range(0, count):
        line = (at + j) % rows
        total = None
        for i in split_shape(dtype):
            col = start + LANES * (1 + i * blocks + (at + j) // rows)
            piece = got_ref[line : line + 1, col : col + LANES].astype(F32)
            total = piece if total is None else total + piece
        out.append(total)
    return out


def products(k, tp, lhs_ref, weight_ref, vis_ref, bias_ref, gain_ref, inv_ref, dots_ref, rows_ref):
    buckets, capacity, features = vis_ref.shape
    width = features // tp
    place = lax.axis_index("tp")
    cols = pl.ds(pl.multiple_of((place ^ k) * width, width), width)
    term = lax.dot_general(
        lhs_ref[...], weight_ref[cols, :], (((1,), (1,)), ((), ())), preferred_element_type=F32
    )
    for q in range(buckets):
        rows_ref[q * capacity : (q + 1) * capacity, :] = (
            vis_ref[q, :, cols].astype(F32) + bias_ref[:, cols]
        )
    inv_rms = inv_ref[:, :1]
    scale = inv_rms * inv_rms * dots_ref[:, :1] / features
    row = gain_ref[:, cols] * jnp.sum(inv_rms * term, axis=0, keepdims=True)
    return term, row - jnp.sum(rows_ref[...] * scale, axis=0, keepdims=True)


def sent_kernel(enc, tp, counts_ref, projected_ref, weight_ref, vis_ref, bias_ref, gain_ref, inv_ref, *refs):
    cots = refs[:enc]
    kv_ref, dots_ref, lhs_ref, send_ref, picked_ref, masked_ref, rows_ref = refs[enc:]
    buckets, capacity, columns = kv_ref.shape
    me = lax.axis_index("enc")
    cots = cots[::-1]
    for k in range(enc):
        picked_ref[me ^ k] = cots[k][me].astype(F32)
    slot = lax.broadcasted_iota(jnp.int32, (capacity, columns), 0)
    for q in range(buckets):
        rows = slice(q * capacity, (q + 1) * capacity)
        live = slot < counts_ref[0, q]
        masked_ref[rows, :] = jnp.where(live, picked_ref[q], 0.0)
        kv_ref[q] = jnp.where(live, projected_ref[rows, :], 0.0)
    masked = masked_ref[...]
    dots = jnp.sum(masked * projected_ref[...], axis=1, keepdims=True)
    dots = jnp.broadcast_to(dots, dots_ref.shape)
    dots_ref[...] = dots
    lhs_ref[...] = masked.astype(BF16)
    width = vis_ref.shape[2] // tp
    chunks, half = width // LANES, tp // 2 * width
    for j in range(tp // 2):
        term, row = products(
            2 * j + 1, tp, lhs_ref, weight_ref, vis_ref, bias_ref, gain_ref, inv_ref, dots_ref, rows_ref
        )
        send_ref[:, j * width : (j + 1) * width] = term
        put_side(send_ref, half, None if j else dots, row, j * chunks, chunks)


def kept_kernel(tp, lhs_ref, weight_ref, vis_ref, bias_ref, gain_ref, inv_ref, dots_ref, kept_ref, sums_ref, rows_ref):
    width = vis_ref.shape[2] // tp
    chunks = width // LANES
    for j in range(tp // 2):
        term, row = products(
            2 * j, tp, lhs_ref, weight_ref, vis_ref, bias_ref, gain_ref, inv_ref, dots_ref, rows_ref
        )
        kept_ref[:, j * width : (j + 1) * width] = term
        for i in range(chunks):
            sums_ref[j * chunks + i : j * chunks + i + 1, :] = row[:, i * LANES : (i + 1) * LANES]


def fold_kernel(width, got_ref, kept_ref, dots_ref, sums_ref, all_ref, own_ref, *refs):
    pairs = kept_ref.shape[1] // width
    half, chunks = kept_ref.shape[1], width // LANES
    sends, totals = refs[: pairs - 1], refs[pairs - 1 :]
    dots = dots_ref[...] + get_dots(got_ref, half)
    all_ref[...] = dots
    for j in range(pairs):
        cols = slice(j * width, (j + 1) * width)
        term = kept_ref[:, cols] + got_ref[:, cols]
        for i, line in enumerate(get_side(got_ref, half, j * chunks, chunks)):
            row = sums_ref[j * chunks + i : j * chunks + i + 1, :] + line
            totals[j][i : i + 1, :] = row
            if j:
                put_side(sends[j - 1], width, None if i else dots, row, i, 1)
        if j:
            sends[j - 1][:, :width] = term.astype(BF16)
        else:
            own_ref[...] = term


def combine_kernel(enc, pairs, vis_ref, bias_ref, gain_ref, inv_ref, kv_ref, dots_ref, own_ref, sum_ref, *refs):
    gots, refs = refs[: pairs - 1], refs[pairs - 1 :]
    sums, refs = refs[: -enc - 2], refs[-enc - 2 :]
    grad_ref, total_ref = refs[:2]
    sends, rows_ref = refs[2:-1], refs[-1]
    buckets, capacity, features = vis_ref.shape
    width = own_ref.shape[1]
    chunks = width // LANES
    me, place = lax.axis_index("enc"), lax.axis_index("tp")
    own = pl.ds(pl.multiple_of(place * width, width), width)
    total = sum_ref[...]
    for got in sums:
        total = total + got[...]
    total_ref[...] = total
    for got in gots:
        for i, line in enumerate(get_side(got, width, 0, chunks)):
            total_ref[i : i + 1, :] = total_ref[i : i + 1, :] + line
    for k in range(1, enc):
        sends[k - 1][:chunks, :] = total_ref[...]
        block = kv_ref[me ^ k]
        for j in range(block.shape[1] // LANES):
            at = chunks + j * capacity
            sends[k - 1][at : at + capacity, :] = block[:, j * LANES : (j + 1) * LANES]
    for q in range(buckets):
        rows_ref[q * capacity : (q + 1) * capacity, :] = (
            vis_ref[q, :, own].astype(F32) + bias_ref[:, own]
        )
    grad_normed, row_dot = own_ref[...], dots_ref[:, :1]
    for got in gots:
        grad_normed = grad_normed + got[:, :width].astype(F32)
        row_dot = row_dot + get_dots(got, width)
    inv_rms = inv_ref[:, :1]
    grad_ref[...] = (
        inv_rms * gain_ref[:, own] * grad_normed
        - rows_ref[...] * (inv_rms * inv_rms) * row_dot / features
    )


def round_kernel(grad_ref, out_ref):
    buckets, capacity, _ = out_ref.shape
    for q in range(buckets):
        out_ref[q] = grad_ref[q * capacity : (q + 1) * capacity, :].astype(BF16)


def final_kernel(enc, total_ref, kv_ref, *refs):
    gots, (sum_ref, out_ref) = refs[: enc - 1][::-1], refs[enc - 1 :]
    buckets, capacity, columns = kv_ref.shape
    chunks = total_ref.shape[0]
    me = lax.axis_index("enc")
    total = total_ref[...]
    for got in gots:
        total = total + got[:chunks, :]
    sum_ref[...] = total
    out_ref[me] = kv_ref[me].astype(BF16)
    for k in range(1, enc):
        for j in range(columns // LANES):
            at = chunks + j * capacity
            out_ref[me ^ k, :, j * LANES : (j + 1) * LANES] = gots[k - 1][
                at : at + capacity, :
            ].astype(BF16)


def per_device(visual, counts, merger_bias, norm_gain, kv_weight, kv_cotangent):
    buckets, capacity, features = visual.shape[2:]
    enc, llm, tp = (lax.axis_size(a) for a in ("enc", "llm", "tp"))
    width, columns, rows = features // tp, kv_weight.shape[1], buckets * capacity
    chunks, pairs = width // LANES, tp // 2
    half = pairs * width
    part = functools.partial
    struct = jax.ShapeDtypeStruct
    run = part(call, 2 * kv_weight.size * 2 + 16 * rows * features)

    vis, bias, gain, cot = visual[0, 0], merger_bias[None], norm_gain[None], kv_cotangent[0, 0]
    own_cot, vis, bias, gain, normed, inv_rms = run(
        norm_kernel,
        (
            *[struct(a.shape, a.dtype) for a in (cot, vis, bias, gain)],
            struct((rows, features), BF16),
            struct((rows, LANES), F32),
        ),
        [
            pltpu.with_memory_space_constraint(a, pltpu.HBM)
            for a in (vis, bias, gain, cot, kv_weight)
        ],
        scratch=[pltpu.VMEM((rows, features), F32), pltpu.SemaphoreType.DMA((4,))],
        specs=[HBM] * 5,
    )
    cots = [own_cot] + [swap(own_cot, "enc", k) for k in range(1, enc)]
    (projected,) = run(project_kernel, (struct((rows, columns), F32),), (normed, kv_weight))
    kv, dots, lhs, send = run(
        part(sent_kernel, enc, tp),
        (
            struct((buckets, capacity, columns), F32),
            struct((rows, LANES), F32),
            struct((rows, columns), BF16),
            struct((rows, half + side(pairs * chunks, rows, F32)), F32),
        ),
        (counts[0], projected, kv_weight, vis, bias, gain, inv_rms, *cots[::-1]),
        scratch=[
            pltpu.VMEM((buckets, capacity, columns), F32),
            pltpu.VMEM((rows, columns), F32),
            pltpu.VMEM((rows, width), F32),
        ],
        specs=[SMEM, *[VMEM] * (6 + enc)],
    )
    got = swap(send, "tp", 1)
    kept, sums = run(
        part(kept_kernel, tp),
        (struct((rows, half), F32), struct((pairs * chunks, LANES), F32)),
        (lhs, kv_weight, vis, bias, gain, inv_rms, dots),
        scratch=[pltpu.VMEM((rows, width), F32)],
    )
    dots, own, *refs = run(
        part(fold_kernel, width),
        (
            struct((rows, LANES), F32),
            struct((rows, width), F32),
            *[struct((rows, width + side(chunks, rows, BF16)), BF16)] * (pairs - 1),
            *[struct((chunks, LANES), F32)] * pairs,
        ),
        (got, kept, dots, sums),
    )
    sends, totals = refs[: pairs - 1], refs[pairs - 1 :]
    gots = [swap(s, "tp", 2 * (j + 1)) for j, s in enumerate(sends)]
    others = [
        swap(t, ("llm", "tp"), tp * g + 2 * j) for g in range(1, llm) for j, t in enumerate(totals)
    ]
    grad, total, *sends = run(
        part(combine_kernel, enc, pairs),
        (
            struct((rows, width), F32),
            struct((chunks, LANES), F32),
            *[struct((chunks + capacity * columns // LANES, LANES), F32)] * (enc - 1),
        ),
        (vis, bias, gain, inv_rms, kv, dots, own, totals[0], *gots, *others),
        scratch=[pltpu.VMEM((rows, width), F32)],
    )
    gots = [swap(s, "enc", k + 1) for k, s in enumerate(sends)]
    (visual_grad,) = run(round_kernel, (struct((buckets, capacity, width), BF16),), (grad,))
    bias_grad, key_values = run(
        part(final_kernel, enc),
        (struct((chunks, LANES), F32), struct((buckets, capacity, columns), BF16)),
        (total, kv, *gots[::-1]),
    )
    return (key_values[None, None], visual_grad[None, None], bias_grad.reshape(width))


def solution(mesh):
    return jax.shard_map(
        per_device,
        mesh=mesh,
        in_specs=(
            P("enc", "llm", None, None, None),
            P("enc", "llm", None),
            P(),
            P(),
            P(None, "tp"),
            P("enc", "llm", None, None, "tp"),
        ),
        out_specs=(P("enc", "llm", None, None, "tp"), P("enc", "llm", None, None, "tp"), P("tp")),
        check_vma=False,
    )
```

time: 39.3 us -> 30.3 us (0.77)
  local copies, waits for them, and re-layouts: 8 us -> 0.01 us
  waiting for transfers between devices: 10.3 us -> 8.44 us
  Pallas kernels: 6.39 us -> 7.18 us
    unnamed x20 -> x4, local copies, waits for them, and re-layouts: 8 us -> 0.01 us
    ppermute x10, waiting for transfers between devices: 10.3 us -> 8.44 us  [swap(): return lax.ppermute(x, axis, [(i, i ^ k) for i in range(n)])]
    pallas_call x8, Pallas kernels: 6.39 us -> 7.18 us  [call(): pl.pallas_call(kernel, out_shape=tuple(outs), in_specs=specs or [VMEM] *...]
  transfers between devices with their start and end apart: 10 -> 10, of which waited for: 5 -> 7; matrix products, arithmetic and copies ran while one was open for 0% -> 0% of each run, Pallas kernels for 7% -> 10%
where the time goes in v3:
time: 30.3 us; the launch traced here: 30.2 us
  starting transfers between devices  13.8 us (46%)
  waiting for transfers between devices  8.44 us (28%)
  Pallas kernels  7.18 us (24%)
  between operations  0.69 us (2%)
    ppermute x10, starting transfers between devices, swap(): return lax.ppermute(x, axis, [(i, i ^ k) for i in range(n)])  13.8 us
    ppermute x10, waiting for transfers between devices, swap(): return lax.ppermute(x, axis, [(i, i ^ k) for i in range(n)])  8.44 us
    pallas_call x8, Pallas kernels, call(): pl.pallas_call(kernel, out_shape=tuple(outs), in_specs=specs or [VMEM] *...  7.18 us
  transfers between devices with their start and end apart: 10, of which 7 were waited for; matrix products, arithmetic and copies ran while one was open for 0% of the time, Pallas kernels for 10%

profile of v3, /device:TPU:0, one launch (start us, length us, event | category | flops | bytes accessed | tf_op | source)
XLA Modules:
  0.0 30.2 jit_solution(3521690217067551969)
XLA Ops:
  0.6 0.0 copy-start
  0.6 0.0 copy-start.1
  0.7 1.5 %shard_map.85 = (bf16[4,4,512]{2,1,0:T(4,128)(2,1)S(1)}, bf16[4,4,8192]{2,1,0:T(4,128)(2,1)S(1)}, f32[1,8192]{1,0:T(1,128)S(1)}, f32[1,8192]{1,0:T(1,128)S(1)}, ...) custom-call(bf16[4,4,8192]{2,1,0:T(4,128)(2,1)} %bitcast.9, f32[1,8192]{1,0:T(1,128)} %bitcast.11, ...), custom_call_target="tpu_custom_call" | custom-call | tf_op jit(solution)/shard_map/pallas_call | solution.py:25
  2.1 5.1 %collective-permute-start = (bf16[4,4,512]{2,1,0:T(4,128)(2,1)S(1)}, bf16[4,4,512]{2,1,0:T(4,128)(2,1)S(1)}, u32[]{:S(2)}, u32[]{:S(2)}) collective-permute-start(bf16[4,4,512]{2,1,0:T(4,128)(2,1)S(1)} %get-tuple-element.32.refs_3_), channel_id=1, source_target_pairs={{0,24},{8,16},{16,8},{24,0},{1,25},{9,17},{17,9},{25,1},{2,26},{10... | collective-permute-start | bytes 49160 | tf_op jit(solution)/shard_map/ppermute | solution.py:21
  7.2 0.0 collective-permute-start.1
  7.2 0.6 %collective-permute-start.2 = (bf16[4,4,512]{2,1,0:T(4,128)(2,1)S(1)}, bf16[4,4,512]{2,1,0:T(4,128)(2,1)S(1)}, u32[]{:S(2)}, u32[]{:S(2)}) collective-permute-start(bf16[4,4,512]{2,1,0:T(4,128)(2,1)S(1)} %get-tuple-element.32.refs_3_), channel_id=1, source_target_pairs={{0,8},{8,0},{16,24},{24,16},{1,9},{9,1},{17,25},{25,17},{2,10},{10... | collective-permute-start | bytes 49160 | tf_op jit(solution)/shard_map/ppermute | solution.py:21
  7.9 0.0 copy-done
  7.9 1.2 %shard_map.86.projected_ref = f32[16,512]{1,0:T(8,128)S(1)} custom-call(bf16[16,8192]{1,0:T(8,128)(2,1)S(1)} %get-tuple-element.31.normed_ref, bf16[8192,512]{1,0:T(8,128)(2,1)S(1)} %copy-done), custom_call_target="tpu_custom_call" | custom-call | tf_op jit(solution)/shard_map/pallas_call | solution.py:25
  9.1 0.0 collective-permute-done.refs_0_
  9.1 2.8 %collective-permute-done.1.refs_1_ = bf16[4,4,512]{2,1,0:T(4,128)(2,1)S(1)} collective-permute-done((bf16[4,4,512]{2,1,0:T(4,128)(2,1)S(1)}, bf16[4,4,512]{2,1,0:T(4,128)(2,1)S(1)}, u32[]{:S(2)}, u32[]{:S(2)}) %collective-permute-start.1) | collective-permute-done | bytes 16416 | tf_op jit(solution)/shard_map/ppermute | solution.py:21
  11.9 0.0 collective-permute-done.2.refs_2_
  11.9 0.0 copy-done.1
  11.9 1.8 %shard_map.87 = (f32[4,4,512]{2,1,0:T(4,128)S(1)}, f32[16,128]{1,0:T(8,128)S(1)}, bf16[16,512]{1,0:T(8,128)(2,1)S(1)}, f32[16,4480]{1,0:T(8,128)S(1)}) custom-call(s32[1,4]{1,0:T(1,128)S(1)} %bitcast.8, f32[16,512]{1,0:T(8,128)S(1)} %shard_map.86.projected_ref, bf16[8192,512]{1,0:T(8,128)(2,1)S(1)} %copy-done, ...), custom_call_target="tpu_custom_call" | custom-call | tf_op jit(solution)/shard_map/pallas_call | solution.py:25
  13.7 0.1 collective-permute-start.3
  13.7 1.2 %shard_map.88 = (f32[16,4096]{1,0:T(8,128)S(1)}, f32[32,128]{1,0:T(8,128)S(1)}) custom-call(bf16[16,512]{1,0:T(8,128)(2,1)S(1)} %get-tuple-element.35.lhs_ref, bf16[8192,512]{1,0:T(8,128)(2,1)S(1)} %copy-done, bf16[4,4,8192]{2,1,0:T(4,128)(2,1)S(1)} %get-tuple-element.27.vis_ref, f32[1,8192]{1,0:T(1,128)S(1)} %get-tuple-element.28.bias_ref, ...), custom_call_target="tpu_custom_call" | custom-call | tf_op jit(solution)/shard_map/pallas_call | solution.py:25
  15.0 0.3 %collective-permute-done.3.got_ref = f32[16,4480]{1,0:T(8,128)S(1)} collective-permute-done((f32[16,4480]{1,0:T(8,128)S(1)}, f32[16,4480]{1,0:T(8,128)S(1)}, u32[]{:S(2)}, u32[]{:S(2)}) %collective-permute-start.3) | collective-permute-done | bytes 286752 | tf_op jit(solution)/shard_map/ppermute | solution.py:21
  15.3 0.1 shard_map.89
  15.4 1.6 %collective-permute-start.4 = (bf16[16,2560]{1,0:T(8,128)(2,1)S(1)}, bf16[16,2560]{1,0:T(8,128)(2,1)S(1)}, u32[]{:S(2)}, u32[]{:S(2)}) collective-permute-start(bf16[16,2560]{1,0:T(8,128)(2,1)S(1)} %get-tuple-element.42), channel_id=1, source_target_pairs={{0,2},{1,3},{2,0},{3,1},{4,6},{5,7},{6,4},{7,5},{8,10},{9,11},{10,... | collective-permute-start | bytes 245768 | tf_op jit(solution)/shard_map/ppermute | solution.py:21
  17.0 1.5 %collective-permute-start.5 = (f32[16,128]{1,0:T(8,128)S(1)}, f32[16,128]{1,0:T(8,128)S(1)}, u32[]{:S(2)}, u32[]{:S(2)}) collective-permute-start(f32[16,128]{1,0:T(8,128)S(1)} %get-tuple-element.41.sum_ref), channel_id=1, source_target_pairs={{0,4},{1,5},{2,6},{3,7},{4,0},{5,1},{6,2},{7,3},{8,12},{9,13},{10,... | collective-permute-start | bytes 24584 | tf_op jit(solution)/shard_map/ppermute | solution.py:21
  18.5 0.5 %collective-permute-start.6 = (f32[16,128]{1,0:T(8,128)S(1)}, f32[16,128]{1,0:T(8,128)S(1)}, u32[]{:S(2)}, u32[]{:S(2)}) collective-permute-start(f32[16,128]{1,0:T(8,128)S(1)} %get-tuple-element.43), channel_id=1, source_target_pairs={{0,6},{1,7},{2,4},{3,5},{4,2},{5,3},{6,0},{7,1},{8,14},{9,15},{10,... | collective-permute-start | bytes 24584 | tf_op jit(solution)/shard_map/ppermute | solution.py:21
  18.9 1.7 %collective-permute-done.5.refs_1_ = f32[16,128]{1,0:T(8,128)S(1)} collective-permute-done((f32[16,128]{1,0:T(8,128)S(1)}, f32[16,128]{1,0:T(8,128)S(1)}, u32[]{:S(2)}, u32[]{:S(2)}) %collective-permute-start.5) | collective-permute-done | bytes 8224 | tf_op jit(solution)/shard_map/ppermute | solution.py:21
  20.6 2.4 %collective-permute-done.6.refs_2_ = f32[16,128]{1,0:T(8,128)S(1)} collective-permute-done((f32[16,128]{1,0:T(8,128)S(1)}, f32[16,128]{1,0:T(8,128)S(1)}, u32[]{:S(2)}, u32[]{:S(2)}) %collective-permute-start.6) | collective-permute-done | bytes 8224 | tf_op jit(solution)/shard_map/ppermute | solution.py:21
  23.0 0.0 collective-permute-done.4.refs_0_
  23.0 0.2 shard_map.90
  23.2 1.5 %collective-permute-start.7 = (f32[32,128]{1,0:T(8,128)S(1)}, f32[32,128]{1,0:T(8,128)S(1)}, u32[]{:S(2)}, u32[]{:S(2)}) collective-permute-start(f32[32,128]{1,0:T(8,128)S(1)} %get-tuple-element.45), channel_id=1, source_target_pairs={{0,24},{8,16},{16,8},{24,0},{1,25},{9,17},{17,9},{25,1},{2,26},{10... | collective-permute-start | bytes 49160 | tf_op jit(solution)/shard_map/ppermute | solution.py:21
  24.7 0.6 %collective-permute-start.8 = (f32[32,128]{1,0:T(8,128)S(1)}, f32[32,128]{1,0:T(8,128)S(1)}, u32[]{:S(2)}, u32[]{:S(2)}) collective-permute-start(f32[32,128]{1,0:T(8,128)S(1)} %get-tuple-element.46), channel_id=1, source_target_pairs={{0,16},{8,24},{16,0},{24,8},{1,17},{9,25},{17,1},{25,9},{2,18},{10... | collective-permute-start | bytes 49160 | tf_op jit(solution)/shard_map/ppermute | solution.py:21
  25.4 2.3 %collective-permute-start.9 = (f32[32,128]{1,0:T(8,128)S(1)}, f32[32,128]{1,0:T(8,128)S(1)}, u32[]{:S(2)}, u32[]{:S(2)}) collective-permute-start(f32[32,128]{1,0:T(8,128)S(1)} %get-tuple-element.47), channel_id=1, source_target_pairs={{0,8},{8,0},{16,24},{24,16},{1,9},{9,1},{17,25},{25,17},{2,10},{10... | collective-permute-start | bytes 49160 | tf_op jit(solution)/shard_map/ppermute | solution.py:21
  27.6 0.6 %shard_map.92 = bf16[4,4,2048]{2,1,0:T(4,128)(2,1)} custom-call(f32[16,2048]{1,0:T(8,128)S(1)} %get-tuple-element.49.grad_ref), custom_call_target="tpu_custom_call" | custom-call | tf_op jit(solution)/shard_map/pallas_call | solution.py:25
  28.3 0.5 %collective-permute-done.7.refs_0_ = f32[32,128]{1,0:T(8,128)S(1)} collective-permute-done((f32[32,128]{1,0:T(8,128)S(1)}, f32[32,128]{1,0:T(8,128)S(1)}, u32[]{:S(2)}, u32[]{:S(2)}) %collective-permute-start.7) | collective-permute-done | bytes 16416 | tf_op jit(solution)/shard_map/ppermute | solution.py:21
  28.8 0.6 %collective-permute-done.8.refs_1_ = f32[32,128]{1,0:T(8,128)S(1)} collective-permute-done((f32[32,128]{1,0:T(8,128)S(1)}, f32[32,128]{1,0:T(8,128)S(1)}, u32[]{:S(2)}, u32[]{:S(2)}) %collective-permute-start.8) | collective-permute-done | bytes 16416 | tf_op jit(solution)/shard_map/ppermute | solution.py:21
  29.4 0.2 collective-permute-done.9.refs_2_
  29.5 0.6 %shard_map.91 = (f32[16,128]{1,0:T(8,128)}, bf16[4,4,512]{2,1,0:T(4,128)(2,1)}) custom-call(f32[16,128]{1,0:T(8,128)S(1)} %get-tuple-element.44.total_ref, f32[4,4,512]{2,1,0:T(4,128)S(1)} %get-tuple-element.33.kv_ref, f32[32,128]{1,0:T(8,128)S(1)} %collective-permute-done.7.refs_0_, f32[32,128]{1,0:T(8,128)S(1)} %collective-permute-done.8.refs_1_, ...), custom_call_target="tpu_custom_call" | custom-call | tf_op jit(solution)/shard_map/pallas_call | solution.py:25
Async XLA Ops:
  0.6 7.2 %copy-start = (bf16[8192,512]{1,0:T(8,128)(2,1)S(1)}, bf16[8192,512]{1,0:T(8,128)(2,1)}, u32[]{:S(2)}) copy-start(bf16[8192,512]{1,0:T(8,128)(2,1)} %weight_ref.5) | copy-start | bytes 25165828
  0.6 11.2 %copy-start.1 = (s32[1,1,4]{2,1,0:T(1,128)S(1)}, s32[1,1,4]{2,1,0:T(1,128)}, u32[]{:S(2)}) copy-start(s32[1,1,4]{2,1,0:T(1,128)} %param.7) | copy-start | bytes 52
  2.1 6.9 %collective-permute-start = (bf16[4,4,512]{2,1,0:T(4,128)(2,1)S(1)}, bf16[4,4,512]{2,1,0:T(4,128)(2,1)S(1)}, u32[]{:S(2)}, u32[]{:S(2)}) collective-permute-start(bf16[4,4,512]{2,1,0:T(4,128)(2,1)S(1)} %get-tuple-element.32.refs_3_), channel_id=1, source_target_pairs={{0,24},{8,16},{16,8},{24,0},{1,25},{9,17},{17,9},{25,1},{2,26},{10... | collective-permute-start | bytes 49160 | tf_op jit(solution)/shard_map/ppermute | solution.py:21
  7.2 4.6 %collective-permute-start.1 = (bf16[4,4,512]{2,1,0:T(4,128)(2,1)S(1)}, bf16[4,4,512]{2,1,0:T(4,128)(2,1)S(1)}, u32[]{:S(2)}, u32[]{:S(2)}) collective-permute-start(bf16[4,4,512]{2,1,0:T(4,128)(2,1)S(1)} %get-tuple-element.32.refs_3_), channel_id=1, source_target_pairs={{0,16},{8,24},{16,0},{24,8},{1,17},{9,25},{17,1},{25,9},{2,18},{10... | collective-permute-start | bytes 49160 | tf_op jit(solution)/shard_map/ppermute | solution.py:21
  7.2 4.6 %collective-permute-start.2 = (bf16[4,4,512]{2,1,0:T(4,128)(2,1)S(1)}, bf16[4,4,512]{2,1,0:T(4,128)(2,1)S(1)}, u32[]{:S(2)}, u32[]{:S(2)}) collective-permute-start(bf16[4,4,512]{2,1,0:T(4,128)(2,1)S(1)} %get-tuple-element.32.refs_3_), channel_id=1, source_target_pairs={{0,8},{8,0},{16,24},{24,16},{1,9},{9,1},{17,25},{25,17},{2,10},{10... | collective-permute-start | bytes 49160 | tf_op jit(solution)/shard_map/ppermute | solution.py:21
  13.7 1.6 %collective-permute-start.3 = (f32[16,4480]{1,0:T(8,128)S(1)}, f32[16,4480]{1,0:T(8,128)S(1)}, u32[]{:S(2)}, u32[]{:S(2)}) collective-permute-start(f32[16,4480]{1,0:T(8,128)S(1)} %get-tuple-element.34), channel_id=1, source_target_pairs={{0,1},{1,0},{2,3},{3,2},{4,5},{5,4},{6,7},{7,6},{8,9},{9,8},{10,11... | collective-permute-start | bytes 860168 | tf_op jit(solution)/shard_map/ppermute | solution.py:21
  15.4 7.6 %collective-permute-start.4 = (bf16[16,2560]{1,0:T(8,128)(2,1)S(1)}, bf16[16,2560]{1,0:T(8,128)(2,1)S(1)}, u32[]{:S(2)}, u32[]{:S(2)}) collective-permute-start(bf16[16,2560]{1,0:T(8,128)(2,1)S(1)} %get-tuple-element.42), channel_id=1, source_target_pairs={{0,2},{1,3},{2,0},{3,1},{4,6},{5,7},{6,4},{7,5},{8,10},{9,11},{10,... | collective-permute-start | bytes 245768 | tf_op jit(solution)/shard_map/ppermute | solution.py:21
  17.0 3.7 %collective-permute-start.5 = (f32[16,128]{1,0:T(8,128)S(1)}, f32[16,128]{1,0:T(8,128)S(1)}, u32[]{:S(2)}, u32[]{:S(2)}) collective-permute-start(f32[16,128]{1,0:T(8,128)S(1)} %get-tuple-element.41.sum_ref), channel_id=1, source_target_pairs={{0,4},{1,5},{2,6},{3,7},{4,0},{5,1},{6,2},{7,3},{8,12},{9,13},{10,... | collective-permute-start | bytes 24584 | tf_op jit(solution)/shard_map/ppermute | solution.py:21
  18.5 4.5 %collective-permute-start.6 = (f32[16,128]{1,0:T(8,128)S(1)}, f32[16,128]{1,0:T(8,128)S(1)}, u32[]{:S(2)}, u32[]{:S(2)}) collective-permute-start(f32[16,128]{1,0:T(8,128)S(1)} %get-tuple-element.43), channel_id=1, source_target_pairs={{0,6},{1,7},{2,4},{3,5},{4,2},{5,3},{6,0},{7,1},{8,14},{9,15},{10,... | collective-permute-start | bytes 24584 | tf_op jit(solution)/shard_map/ppermute | solution.py:21
  23.2 5.6 %collective-permute-start.7 = (f32[32,128]{1,0:T(8,128)S(1)}, f32[32,128]{1,0:T(8,128)S(1)}, u32[]{:S(2)}, u32[]{:S(2)}) collective-permute-start(f32[32,128]{1,0:T(8,128)S(1)} %get-tuple-element.45), channel_id=1, source_target_pairs={{0,24},{8,16},{16,8},{24,0},{1,25},{9,17},{17,9},{25,1},{2,26},{10... | collective-permute-start | bytes 49160 | tf_op jit(solution)/shard_map/ppermute | solution.py:21
  24.7 4.7 %collective-permute-start.8 = (f32[32,128]{1,0:T(8,128)S(1)}, f32[32,128]{1,0:T(8,128)S(1)}, u32[]{:S(2)}, u32[]{:S(2)}) collective-permute-start(f32[32,128]{1,0:T(8,128)S(1)} %get-tuple-element.46), channel_id=1, source_target_pairs={{0,16},{8,24},{16,0},{24,8},{1,17},{9,25},{17,1},{25,9},{2,18},{10... | collective-permute-start | bytes 49160 | tf_op jit(solution)/shard_map/ppermute | solution.py:21
  25.4 4.2 %collective-permute-start.9 = (f32[32,128]{1,0:T(8,128)S(1)}, f32[32,128]{1,0:T(8,128)S(1)}, u32[]{:S(2)}, u32[]{:S(2)}) collective-permute-start(f32[32,128]{1,0:T(8,128)S(1)} %get-tuple-element.47), channel_id=1, source_target_pairs={{0,8},{8,0},{16,24},{24,16},{1,9},{9,1},{17,25},{25,17},{2,10},{10... | collective-permute-start | bytes 49160 | tf_op jit(solution)/shard_map/ppermute | solution.py:21

commit v4 on v3

--- a/solution.py
+++ b/solution.py
@@ -276,7 +276,7 @@
         scratch=[pltpu.VMEM((rows, features), F32), pltpu.SemaphoreType.DMA((4,))],
         specs=[HBM] * 5,
     )
-    cots = [own_cot] + [swap(own_cot, "enc", k) for k in range(1, enc)]
+    cots = [own_cot] + [swap(cot, "enc", k) for k in range(1, enc)]
     (projected,) = run(project_kernel, (struct((rows, columns), F32),), (normed, kv_weight))
     kv, dots, lhs, send = run(
         part(sent_kernel, enc, tp),
@@ -323,7 +323,7 @@
             struct((chunks, LANES), F32),
             *[struct((chunks + capacity * columns // LANES, LANES), F32)] * (enc - 1),
         ),
-        (vis, bias, gain, inv_rms, kv, dots, own, totals[0], *gots, *others),
+        (vis, bias, gain, inv_rms, kv, dots, own, totals[0], *gots, *others[::-1]),
         scratch=[pltpu.VMEM((rows, width), F32)],
     )
     gots = [swap(s, "enc", k + 1) for k, s in enumerate(sends)]

time: 30.3 us -> 28.7 us (0.947)
  waiting for transfers between devices: 8.44 us -> 6.93 us
    ppermute x10, waiting for transfers between devices: 8.44 us -> 6.93 us  [swap(): return lax.ppermute(x, axis, [(i, i ^ k) for i in range(n)])]
  transfers between devices with their start and end apart: 10 -> 10, of which waited for: 7 -> 6; matrix products, arithmetic and copies ran while one was open for 0% -> 0% of each run, Pallas kernels for 10% -> 15%
where the time goes in v4:
time: 28.7 us; the launch traced here: 28.5 us
  starting transfers between devices  13.8 us (48%)
  Pallas kernels  7.05 us (25%)
  waiting for transfers between devices  6.93 us (24%)
  between operations  0.69 us (2%)
    ppermute x10, starting transfers between devices, swap(): return lax.ppermute(x, axis, [(i, i ^ k) for i in range(n)])  13.8 us
    pallas_call x8, Pallas kernels, call(): pl.pallas_call(kernel, out_shape=tuple(outs), in_specs=specs or [VMEM] *...  7.05 us
    ppermute x10, waiting for transfers between devices, swap(): return lax.ppermute(x, axis, [(i, i ^ k) for i in range(n)])  6.93 us
  transfers between devices with their start and end apart: 10, of which 6 were waited for; matrix products, arithmetic and copies ran while one was open for 0% of the time, Pallas kernels for 15%

profile of v4, /device:TPU:0, one launch (start us, length us, event | category | flops | bytes accessed | tf_op | source)
XLA Modules:
  0.0 28.5 jit_solution(11227224757198917476)
XLA Ops:
  0.6 0.0 copy-start
  0.6 5.1 %collective-permute-start = (bf16[4,4,512]{2,1,0:T(4,128)(2,1)}, bf16[4,4,512]{2,1,0:T(4,128)(2,1)S(1)}, u32[]{:S(2)}, u32[]{:S(2)}) collective-permute-start(bf16[4,4,512]{2,1,0:T(4,128)(2,1)} %bitcast.13), channel_id=1, source_target_pairs={{0,24},{8,16},{16,8},{24,0},{1,25},{9,17},{17,9},{25,1},{2,26},{10... | collective-permute-start | bytes 49160 | tf_op jit(solution)/shard_map/ppermute | solution.py:21
  5.8 0.0 collective-permute-start.1
  5.8 0.6 %collective-permute-start.2 = (bf16[4,4,512]{2,1,0:T(4,128)(2,1)}, bf16[4,4,512]{2,1,0:T(4,128)(2,1)S(1)}, u32[]{:S(2)}, u32[]{:S(2)}) collective-permute-start(bf16[4,4,512]{2,1,0:T(4,128)(2,1)} %bitcast.15), channel_id=1, source_target_pairs={{0,8},{8,0},{16,24},{24,16},{1,9},{9,1},{17,25},{25,17},{2,10},{10... | collective-permute-start | bytes 49160 | tf_op jit(solution)/shard_map/ppermute | solution.py:21
  6.4 0.0 copy-start.1
  6.4 1.3 %shard_map.85 = (bf16[4,4,512]{2,1,0:T(4,128)(2,1)S(1)}, bf16[4,4,8192]{2,1,0:T(4,128)(2,1)S(1)}, f32[1,8192]{1,0:T(1,128)S(1)}, f32[1,8192]{1,0:T(1,128)S(1)}, ...) custom-call(bf16[4,4,8192]{2,1,0:T(4,128)(2,1)} %bitcast.9, f32[1,8192]{1,0:T(1,128)} %bitcast.11, ...), custom_call_target="tpu_custom_call" | custom-call | tf_op jit(solution)/shard_map/pallas_call | solution.py:25
  7.7 0.0 copy-done
  7.7 1.2 %shard_map.86.projected_ref = f32[16,512]{1,0:T(8,128)S(1)} custom-call(bf16[16,8192]{1,0:T(8,128)(2,1)S(1)} %get-tuple-element.31.normed_ref, bf16[8192,512]{1,0:T(8,128)(2,1)S(1)} %copy-done), custom_call_target="tpu_custom_call" | custom-call | tf_op jit(solution)/shard_map/pallas_call | solution.py:25
  8.9 0.0 collective-permute-done.refs_0_
  8.9 1.7 %collective-permute-done.1.refs_1_ = bf16[4,4,512]{2,1,0:T(4,128)(2,1)S(1)} collective-permute-done((bf16[4,4,512]{2,1,0:T(4,128)(2,1)}, bf16[4,4,512]{2,1,0:T(4,128)(2,1)S(1)}, u32[]{:S(2)}, u32[]{:S(2)}) %collective-permute-start.1) | collective-permute-done | bytes 16416 | tf_op jit(solution)/shard_map/ppermute | solution.py:21
  10.6 0.0 collective-permute-done.2.refs_2_
  10.6 0.0 copy-done.1
  10.6 1.8 %shard_map.87 = (f32[4,4,512]{2,1,0:T(4,128)S(1)}, f32[16,128]{1,0:T(8,128)S(1)}, bf16[16,512]{1,0:T(8,128)(2,1)S(1)}, f32[16,4480]{1,0:T(8,128)S(1)}) custom-call(s32[1,4]{1,0:T(1,128)S(1)} %bitcast.8, f32[16,512]{1,0:T(8,128)S(1)} %shard_map.86.projected_ref, bf16[8192,512]{1,0:T(8,128)(2,1)S(1)} %copy-done, ...), custom_call_target="tpu_custom_call" | custom-call | tf_op jit(solution)/shard_map/pallas_call | solution.py:25
  12.4 0.1 collective-permute-start.3
  12.5 1.2 %shard_map.88 = (f32[16,4096]{1,0:T(8,128)S(1)}, f32[32,128]{1,0:T(8,128)S(1)}) custom-call(bf16[16,512]{1,0:T(8,128)(2,1)S(1)} %get-tuple-element.35.lhs_ref, bf16[8192,512]{1,0:T(8,128)(2,1)S(1)} %copy-done, bf16[4,4,8192]{2,1,0:T(4,128)(2,1)S(1)} %get-tuple-element.27.vis_ref, f32[1,8192]{1,0:T(1,128)S(1)} %get-tuple-element.28.bias_ref, ...), custom_call_target="tpu_custom_call" | custom-call | tf_op jit(solution)/shard_map/pallas_call | solution.py:25
  13.7 0.3 %collective-permute-done.3.got_ref = f32[16,4480]{1,0:T(8,128)S(1)} collective-permute-done((f32[16,4480]{1,0:T(8,128)S(1)}, f32[16,4480]{1,0:T(8,128)S(1)}, u32[]{:S(2)}, u32[]{:S(2)}) %collective-permute-start.3) | collective-permute-done | bytes 286752 | tf_op jit(solution)/shard_map/ppermute | solution.py:21
  14.0 0.1 shard_map.89
  14.1 1.6 %collective-permute-start.4 = (bf16[16,2560]{1,0:T(8,128)(2,1)S(1)}, bf16[16,2560]{1,0:T(8,128)(2,1)S(1)}, u32[]{:S(2)}, u32[]{:S(2)}) collective-permute-start(bf16[16,2560]{1,0:T(8,128)(2,1)S(1)} %get-tuple-element.42), channel_id=1, source_target_pairs={{0,2},{1,3},{2,0},{3,1},{4,6},{5,7},{6,4},{7,5},{8,10},{9,11},{10,... | collective-permute-start | bytes 245768 | tf_op jit(solution)/shard_map/ppermute | solution.py:21
  15.7 1.4 %collective-permute-start.5 = (f32[16,128]{1,0:T(8,128)S(1)}, f32[16,128]{1,0:T(8,128)S(1)}, u32[]{:S(2)}, u32[]{:S(2)}) collective-permute-start(f32[16,128]{1,0:T(8,128)S(1)} %get-tuple-element.43), channel_id=1, source_target_pairs={{0,6},{1,7},{2,4},{3,5},{4,2},{5,3},{6,0},{7,1},{8,14},{9,15},{10,... | collective-permute-start | bytes 24584 | tf_op jit(solution)/shard_map/ppermute | solution.py:21
  17.1 0.5 %collective-permute-start.6 = (f32[16,128]{1,0:T(8,128)S(1)}, f32[16,128]{1,0:T(8,128)S(1)}, u32[]{:S(2)}, u32[]{:S(2)}) collective-permute-start(f32[16,128]{1,0:T(8,128)S(1)} %get-tuple-element.41.sum_ref), channel_id=1, source_target_pairs={{0,4},{1,5},{2,6},{3,7},{4,0},{5,1},{6,2},{7,3},{8,12},{9,13},{10,... | collective-permute-start | bytes 24584 | tf_op jit(solution)/shard_map/ppermute | solution.py:21
  17.7 2.6 %collective-permute-done.5.refs_1_ = f32[16,128]{1,0:T(8,128)S(1)} collective-permute-done((f32[16,128]{1,0:T(8,128)S(1)}, f32[16,128]{1,0:T(8,128)S(1)}, u32[]{:S(2)}, u32[]{:S(2)}) %collective-permute-start.5) | collective-permute-done | bytes 8224 | tf_op jit(solution)/shard_map/ppermute | solution.py:21
  20.2 0.5 %collective-permute-done.6.refs_2_ = f32[16,128]{1,0:T(8,128)S(1)} collective-permute-done((f32[16,128]{1,0:T(8,128)S(1)}, f32[16,128]{1,0:T(8,128)S(1)}, u32[]{:S(2)}, u32[]{:S(2)}) %collective-permute-start.6) | collective-permute-done | bytes 8224 | tf_op jit(solution)/shard_map/ppermute | solution.py:21
  20.8 0.0 collective-permute-done.4.refs_0_
  20.8 0.2 shard_map.90
  21.0 2.2 %collective-permute-start.7 = (f32[32,128]{1,0:T(8,128)S(1)}, f32[32,128]{1,0:T(8,128)S(1)}, u32[]{:S(2)}, u32[]{:S(2)}) collective-permute-start(f32[32,128]{1,0:T(8,128)S(1)} %get-tuple-element.45), channel_id=1, source_target_pairs={{0,24},{8,16},{16,8},{24,0},{1,25},{9,17},{17,9},{25,1},{2,26},{10... | collective-permute-start | bytes 49160 | tf_op jit(solution)/shard_map/ppermute | solution.py:21
  23.1 0.0 collective-permute-start.8
  23.1 2.3 %collective-permute-start.9 = (f32[32,128]{1,0:T(8,128)S(1)}, f32[32,128]{1,0:T(8,128)S(1)}, u32[]{:S(2)}, u32[]{:S(2)}) collective-permute-start(f32[32,128]{1,0:T(8,128)S(1)} %get-tuple-element.47), channel_id=1, source_target_pairs={{0,8},{8,0},{16,24},{24,16},{1,9},{9,1},{17,25},{25,17},{2,10},{10... | collective-permute-start | bytes 49160 | tf_op jit(solution)/shard_map/ppermute | solution.py:21
  25.4 0.6 %shard_map.92 = bf16[4,4,2048]{2,1,0:T(4,128)(2,1)} custom-call(f32[16,2048]{1,0:T(8,128)S(1)} %get-tuple-element.49.grad_ref), custom_call_target="tpu_custom_call" | custom-call | tf_op jit(solution)/shard_map/pallas_call | solution.py:25
  26.1 0.5 %collective-permute-done.7.refs_0_ = f32[32,128]{1,0:T(8,128)S(1)} collective-permute-done((f32[32,128]{1,0:T(8,128)S(1)}, f32[32,128]{1,0:T(8,128)S(1)}, u32[]{:S(2)}, u32[]{:S(2)}) %collective-permute-start.7) | collective-permute-done | bytes 16416 | tf_op jit(solution)/shard_map/ppermute | solution.py:21
  26.6 1.3 %collective-permute-done.8.refs_1_ = f32[32,128]{1,0:T(8,128)S(1)} collective-permute-done((f32[32,128]{1,0:T(8,128)S(1)}, f32[32,128]{1,0:T(8,128)S(1)}, u32[]{:S(2)}, u32[]{:S(2)}) %collective-permute-start.8) | collective-permute-done | bytes 16416 | tf_op jit(solution)/shard_map/ppermute | solution.py:21
  27.9 0.0 collective-permute-done.9.refs_2_
  27.9 0.6 %shard_map.91 = (f32[16,128]{1,0:T(8,128)}, bf16[4,4,512]{2,1,0:T(4,128)(2,1)}) custom-call(f32[16,128]{1,0:T(8,128)S(1)} %get-tuple-element.44.total_ref, f32[4,4,512]{2,1,0:T(4,128)S(1)} %get-tuple-element.33.kv_ref, f32[32,128]{1,0:T(8,128)S(1)} %collective-permute-done.7.refs_0_, f32[32,128]{1,0:T(8,128)S(1)} %collective-permute-done.8.refs_1_, ...), custom_call_target="tpu_custom_call" | custom-call | tf_op jit(solution)/shard_map/pallas_call | solution.py:25
Async XLA Ops:
  0.6 7.1 %copy-start = (bf16[8192,512]{1,0:T(8,128)(2,1)S(1)}, bf16[8192,512]{1,0:T(8,128)(2,1)}, u32[]{:S(2)}) copy-start(bf16[8192,512]{1,0:T(8,128)(2,1)} %weight_ref.5) | copy-start | bytes 25165828
  0.6 8.3 %collective-permute-start = (bf16[4,4,512]{2,1,0:T(4,128)(2,1)}, bf16[4,4,512]{2,1,0:T(4,128)(2,1)S(1)}, u32[]{:S(2)}, u32[]{:S(2)}) collective-permute-start(bf16[4,4,512]{2,1,0:T(4,128)(2,1)} %bitcast.13), channel_id=1, source_target_pairs={{0,24},{8,16},{16,8},{24,0},{1,25},{9,17},{17,9},{25,1},{2,26},{10... | collective-permute-start | bytes 49160 | tf_op jit(solution)/shard_map/ppermute | solution.py:21
  5.8 4.8 %collective-permute-start.1 = (bf16[4,4,512]{2,1,0:T(4,128)(2,1)}, bf16[4,4,512]{2,1,0:T(4,128)(2,1)S(1)}, u32[]{:S(2)}, u32[]{:S(2)}) collective-permute-start(bf16[4,4,512]{2,1,0:T(4,128)(2,1)} %bitcast.14), channel_id=1, source_target_pairs={{0,16},{8,24},{16,0},{24,8},{1,17},{9,25},{17,1},{25,9},{2,18},{10... | collective-permute-start | bytes 49160 | tf_op jit(solution)/shard_map/ppermute | solution.py:21
  5.8 4.8 %collective-permute-start.2 = (bf16[4,4,512]{2,1,0:T(4,128)(2,1)}, bf16[4,4,512]{2,1,0:T(4,128)(2,1)S(1)}, u32[]{:S(2)}, u32[]{:S(2)}) collective-permute-start(bf16[4,4,512]{2,1,0:T(4,128)(2,1)} %bitcast.15), channel_id=1, source_target_pairs={{0,8},{8,0},{16,24},{24,16},{1,9},{9,1},{17,25},{25,17},{2,10},{10... | collective-permute-start | bytes 49160 | tf_op jit(solution)/shard_map/ppermute | solution.py:21
  6.4 4.2 %copy-start.1 = (s32[1,1,4]{2,1,0:T(1,128)S(1)}, s32[1,1,4]{2,1,0:T(1,128)}, u32[]{:S(2)}) copy-start(s32[1,1,4]{2,1,0:T(1,128)} %param.7) | copy-start | bytes 52
  12.4 1.6 %collective-permute-start.3 = (f32[16,4480]{1,0:T(8,128)S(1)}, f32[16,4480]{1,0:T(8,128)S(1)}, u32[]{:S(2)}, u32[]{:S(2)}) collective-permute-start(f32[16,4480]{1,0:T(8,128)S(1)} %get-tuple-element.34), channel_id=1, source_target_pairs={{0,1},{1,0},{2,3},{3,2},{4,5},{5,4},{6,7},{7,6},{8,9},{9,8},{10,11... | collective-permute-start | bytes 860168 | tf_op jit(solution)/shard_map/ppermute | solution.py:21
  14.1 6.7 %collective-permute-start.4 = (bf16[16,2560]{1,0:T(8,128)(2,1)S(1)}, bf16[16,2560]{1,0:T(8,128)(2,1)S(1)}, u32[]{:S(2)}, u32[]{:S(2)}) collective-permute-start(bf16[16,2560]{1,0:T(8,128)(2,1)S(1)} %get-tuple-element.42), channel_id=1, source_target_pairs={{0,2},{1,3},{2,0},{3,1},{4,6},{5,7},{6,4},{7,5},{8,10},{9,11},{10,... | collective-permute-start | bytes 245768 | tf_op jit(solution)/shard_map/ppermute | solution.py:21
  15.7 4.5 %collective-permute-start.5 = (f32[16,128]{1,0:T(8,128)S(1)}, f32[16,128]{1,0:T(8,128)S(1)}, u32[]{:S(2)}, u32[]{:S(2)}) collective-permute-start(f32[16,128]{1,0:T(8,128)S(1)} %get-tuple-element.43), channel_id=1, source_target_pairs={{0,6},{1,7},{2,4},{3,5},{4,2},{5,3},{6,0},{7,1},{8,14},{9,15},{10,... | collective-permute-start | bytes 24584 | tf_op jit(solution)/shard_map/ppermute | solution.py:21
  17.1 3.7 %collective-permute-start.6 = (f32[16,128]{1,0:T(8,128)S(1)}, f32[16,128]{1,0:T(8,128)S(1)}, u32[]{:S(2)}, u32[]{:S(2)}) collective-permute-start(f32[16,128]{1,0:T(8,128)S(1)} %get-tuple-element.41.sum_ref), channel_id=1, source_target_pairs={{0,4},{1,5},{2,6},{3,7},{4,0},{5,1},{6,2},{7,3},{8,12},{9,13},{10,... | collective-permute-start | bytes 24584 | tf_op jit(solution)/shard_map/ppermute | solution.py:21
  21.0 5.6 %collective-permute-start.7 = (f32[32,128]{1,0:T(8,128)S(1)}, f32[32,128]{1,0:T(8,128)S(1)}, u32[]{:S(2)}, u32[]{:S(2)}) collective-permute-start(f32[32,128]{1,0:T(8,128)S(1)} %get-tuple-element.45), channel_id=1, source_target_pairs={{0,24},{8,16},{16,8},{24,0},{1,25},{9,17},{17,9},{25,1},{2,26},{10... | collective-permute-start | bytes 49160 | tf_op jit(solution)/shard_map/ppermute | solution.py:21
  23.1 4.7 %collective-permute-start.8 = (f32[32,128]{1,0:T(8,128)S(1)}, f32[32,128]{1,0:T(8,128)S(1)}, u32[]{:S(2)}, u32[]{:S(2)}) collective-permute-start(f32[32,128]{1,0:T(8,128)S(1)} %get-tuple-element.46), channel_id=1, source_target_pairs={{0,16},{8,24},{16,0},{24,8},{1,17},{9,25},{17,1},{25,9},{2,18},{10... | collective-permute-start | bytes 49160 | tf_op jit(solution)/shard_map/ppermute | solution.py:21
  23.1 4.7 %collective-permute-start.9 = (f32[32,128]{1,0:T(8,128)S(1)}, f32[32,128]{1,0:T(8,128)S(1)}, u32[]{:S(2)}, u32[]{:S(2)}) collective-permute-start(f32[32,128]{1,0:T(8,128)S(1)} %get-tuple-element.47), channel_id=1, source_target_pairs={{0,8},{8,0},{16,24},{24,16},{1,9},{9,1},{17,25},{25,17},{2,10},{10... | collective-permute-start | bytes 49160 | tf_op jit(solution)/shard_map/ppermute | solution.py:21

commit v5 on v4

--- a/solution.py
+++ b/solution.py
@@ -32,16 +32,12 @@
     )(*args)
 
 
-def norm_kernel(
-    vis_hbm, bias_hbm, gain_hbm, cot_hbm, _, cot_ref, vis_ref, bias_ref, gain_ref,
-    normed_ref, inv_ref, rows_ref, sems,
-):
-    pairs = [(cot_hbm, cot_ref), (vis_hbm, vis_ref), (bias_hbm, bias_ref), (gain_hbm, gain_ref)]
-    copies = [pltpu.make_async_copy(a, b, sems.at[i]) for i, (a, b) in enumerate(pairs)]
-    for copy in copies:
-        copy.start()
-    for copy in copies:
-        copy.wait()
+def first_kernel(*refs):
+    token_ref = refs[-1]
+    token_ref[...] = jnp.zeros(token_ref.shape, F32)
+
+
+def project_kernel(vis_ref, bias_ref, gain_ref, weight_ref, _, projected_ref, inv_ref, rows_ref, normed_ref):
     buckets, capacity, features = vis_ref.shape
     for q in range(buckets):
         rows_ref[q * capacity : (q + 1) * capacity, :] = vis_ref[q].astype(F32) + bias_ref[...]
@@ -50,9 +46,6 @@
     inv_rms = lax.rsqrt(mean + 1e-06)
     normed_ref[...] = (inputs * inv_rms * gain_ref[...]).astype(BF16)
     inv_ref[...] = jnp.broadcast_to(inv_rms, inv_ref.shape)
-
-
-def project_kernel(normed_ref, weight_ref, projected_ref):
     projected_ref[...] = jnp.dot(normed_ref[...], weight_ref[...], preferred_element_type=F32)
 
 
@@ -262,22 +255,20 @@
     run = part(call, 2 * kv_weight.size * 2 + 16 * rows * features)
 
     vis, bias, gain, cot = visual[0, 0], merger_bias[None], norm_gain[None], kv_cotangent[0, 0]
-    own_cot, vis, bias, gain, normed, inv_rms = run(
-        norm_kernel,
-        (
-            *[struct(a.shape, a.dtype) for a in (cot, vis, bias, gain)],
-            struct((rows, features), BF16),
-            struct((rows, LANES), F32),
-        ),
-        [
-            pltpu.with_memory_space_constraint(a, pltpu.HBM)
-            for a in (vis, bias, gain, cot, kv_weight)
-        ],
-        scratch=[pltpu.VMEM((rows, features), F32), pltpu.SemaphoreType.DMA((4,))],
-        specs=[HBM] * 5,
-    )
+    (token,) = run(
+        first_kernel,
+        (struct((8, LANES), F32),),
+        [pltpu.with_memory_space_constraint(a, pltpu.HBM) for a in (kv_weight, vis, bias, gain)],
+        specs=[HBM] * 4,
+    )
+    projected, inv_rms = run(
+        project_kernel,
+        (struct((rows, columns), F32), struct((rows, LANES), F32)),
+        (vis, bias, gain, kv_weight, token),
+        scratch=[pltpu.VMEM((rows, features), F32), pltpu.VMEM((rows, features), BF16)],
+    )
+    own_cot = cot
     cots = [own_cot] + [swap(cot, "enc", k) for k in range(1, enc)]
-    (projected,) = run(project_kernel, (struct((rows, columns), F32),), (normed, kv_weight))
     kv, dots, lhs, send = run(
         part(sent_kernel, enc, tp),
         (

time: 28.7 us -> 28.1 us (0.979)
  Pallas kernels: 7.05 us -> 5.99 us
  waiting for transfers between devices: 6.93 us -> 7.4 us
    pallas_call x8, Pallas kernels: 7.05 us -> 5.99 us  [call(): pl.pallas_call(kernel, out_shape=tuple(outs), in_specs=specs or [VMEM] *...]
    ppermute x10, waiting for transfers between devices: 6.93 us -> 7.4 us  [swap(): return lax.ppermute(x, axis, [(i, i ^ k) for i in range(n)])]
  transfers between devices with their start and end apart: 10 -> 10, of which waited for: 6 -> 6; matrix products, arithmetic and copies ran while one was open for 0% -> 0% of each run, Pallas kernels for 15% -> 12%
where the time goes in v5:
time: 28.1 us; the launch traced here: 28 us
  starting transfers between devices  13.8 us (49%)
  waiting for transfers between devices  7.4 us (26%)
  Pallas kernels  5.99 us (21%)
  between operations  0.73 us (3%)
    ppermute x10, starting transfers between devices, swap(): return lax.ppermute(x, axis, [(i, i ^ k) for i in range(n)])  13.8 us
    ppermute x10, waiting for transfers between devices, swap(): return lax.ppermute(x, axis, [(i, i ^ k) for i in range(n)])  7.4 us
    pallas_call x8, Pallas kernels, call(): pl.pallas_call(kernel, out_shape=tuple(outs), in_specs=specs or [VMEM] *...  5.99 us
  transfers between devices with their start and end apart: 10, of which 6 were waited for; matrix products, arithmetic and copies ran while one was open for 0% of the time, Pallas kernels for 12%

profile of v5, /device:TPU:0, one launch (start us, length us, event | category | flops | bytes accessed | tf_op | source)
XLA Modules:
  0.0 28.0 jit_solution(6611341886072722010)
XLA Ops:
  0.6 0.0 copy-start.1
  0.6 0.0 copy-start.2
  0.7 0.0 copy-start.3
  0.7 0.0 copy-start
  0.7 5.1 %collective-permute-start = (bf16[4,4,512]{2,1,0:T(4,128)(2,1)}, bf16[4,4,512]{2,1,0:T(4,128)(2,1)S(1)}, u32[]{:S(2)}, u32[]{:S(2)}) collective-permute-start(bf16[4,4,512]{2,1,0:T(4,128)(2,1)} %bitcast.23), channel_id=1, source_target_pairs={{0,24},{8,16},{16,8},{24,0},{1,25},{9,17},{17,9},{25,1},{2,26},{10... | collective-permute-start | bytes 49160 | tf_op jit(solution)/shard_map/ppermute | solution.py:21
  5.8 0.0 collective-permute-start.1
  5.8 0.6 %collective-permute-start.2 = (bf16[4,4,512]{2,1,0:T(4,128)(2,1)}, bf16[4,4,512]{2,1,0:T(4,128)(2,1)S(1)}, u32[]{:S(2)}, u32[]{:S(2)}) collective-permute-start(bf16[4,4,512]{2,1,0:T(4,128)(2,1)} %bitcast.25), channel_id=1, source_target_pairs={{0,8},{8,0},{16,24},{24,16},{1,9},{9,1},{17,25},{25,17},{2,10},{10... | collective-permute-start | bytes 49160 | tf_op jit(solution)/shard_map/ppermute | solution.py:21
  6.4 0.0 copy-start.4
  6.4 0.0 copy-start.5
  6.4 0.0 copy-done.1
  6.4 0.0 copy-done.2
  6.5 0.0 copy-done.3
  6.5 0.0 copy-done
  6.5 1.4 %shard_map.86 = (f32[16,512]{1,0:T(8,128)S(1)}, f32[16,128]{1,0:T(8,128)S(1)}) custom-call(bf16[4,4,8192]{2,1,0:T(4,128)(2,1)S(1)} %bitcast.9, f32[1,8192]{1,0:T(1,128)S(1)} %bitcast.14, f32[1,8192]{1,0:T(1,128)S(1)} %bitcast.19, bf16[8192,512]{1,0:T(8,128)(2,1)S(1)} %copy-done, f32[8,128]{1,0:T(8,128)S(1)} %shard_map.85._), custom_call_target="tpu_custom_call" | custom-call | tf_op jit(solution)/shard_map/pallas_call | solution.py:25
  7.9 0.0 collective-permute-done.refs_0_
  7.9 2.7 %collective-permute-done.1.refs_1_ = bf16[4,4,512]{2,1,0:T(4,128)(2,1)S(1)} collective-permute-done((bf16[4,4,512]{2,1,0:T(4,128)(2,1)}, bf16[4,4,512]{2,1,0:T(4,128)(2,1)S(1)}, u32[]{:S(2)}, u32[]{:S(2)}) %collective-permute-start.1) | collective-permute-done | bytes 16416 | tf_op jit(solution)/shard_map/ppermute | solution.py:21
  10.6 0.0 collective-permute-done.2.refs_2_
  10.6 0.0 copy-done.4
  10.6 0.0 copy-done.5
  10.6 1.8 %shard_map.87 = (f32[4,4,512]{2,1,0:T(4,128)S(1)}, f32[16,128]{1,0:T(8,128)S(1)}, bf16[16,512]{1,0:T(8,128)(2,1)S(1)}, f32[16,4480]{1,0:T(8,128)S(1)}) custom-call(s32[1,4]{1,0:T(1,128)S(1)} %bitcast.27, f32[16,512]{1,0:T(8,128)S(1)} %get-tuple-element.24.projected_ref, bf16[8192,512]{1,0:T(8,128)(2,1)S(1)} %copy-done, bf16[4,4,8192]{2,1,0:T(4,128)(2,1)S(1)} %bitcast.10, ...), custom_call_target="tpu_custom_call" | custom-call | tf_op jit(solution)/shard_map/pallas_call | solution.py:25
  12.4 0.1 collective-permute-start.3
  12.5 1.2 %shard_map.88 = (f32[16,4096]{1,0:T(8,128)S(1)}, f32[32,128]{1,0:T(8,128)S(1)}) custom-call(bf16[16,512]{1,0:T(8,128)(2,1)S(1)} %get-tuple-element.27.lhs_ref, bf16[8192,512]{1,0:T(8,128)(2,1)S(1)} %copy-done, bf16[4,4,8192]{2,1,0:T(4,128)(2,1)S(1)} %bitcast.11, f32[1,8192]{1,0:T(1,128)S(1)} %bitcast.16, f32[1,8192]{1,0:T(1,128)S(1)} %bitcast.21, ...), custom_call_target="tpu_custom_call" | custom-call | tf_op jit(solution)/shard_map/pallas_call | solution.py:25
  13.8 0.3 %collective-permute-done.3.got_ref = f32[16,4480]{1,0:T(8,128)S(1)} collective-permute-done((f32[16,4480]{1,0:T(8,128)S(1)}, f32[16,4480]{1,0:T(8,128)S(1)}, u32[]{:S(2)}, u32[]{:S(2)}) %collective-permute-start.3) | collective-permute-done | bytes 286752 | tf_op jit(solution)/shard_map/ppermute | solution.py:21
  14.1 0.1 shard_map.89
  14.2 1.6 %collective-permute-start.4 = (bf16[16,2560]{1,0:T(8,128)(2,1)S(1)}, bf16[16,2560]{1,0:T(8,128)(2,1)S(1)}, u32[]{:S(2)}, u32[]{:S(2)}) collective-permute-start(bf16[16,2560]{1,0:T(8,128)(2,1)S(1)} %get-tuple-element.34), channel_id=1, source_target_pairs={{0,2},{1,3},{2,0},{3,1},{4,6},{5,7},{6,4},{7,5},{8,10},{9,11},{10,... | collective-permute-start | bytes 245768 | tf_op jit(solution)/shard_map/ppermute | solution.py:21
  15.7 1.4 %collective-permute-start.5 = (f32[16,128]{1,0:T(8,128)S(1)}, f32[16,128]{1,0:T(8,128)S(1)}, u32[]{:S(2)}, u32[]{:S(2)}) collective-permute-start(f32[16,128]{1,0:T(8,128)S(1)} %get-tuple-element.35), channel_id=1, source_target_pairs={{0,6},{1,7},{2,4},{3,5},{4,2},{5,3},{6,0},{7,1},{8,14},{9,15},{10,... | collective-permute-start | bytes 24584 | tf_op jit(solution)/shard_map/ppermute | solution.py:21
  17.2 0.5 %collective-permute-start.6 = (f32[16,128]{1,0:T(8,128)S(1)}, f32[16,128]{1,0:T(8,128)S(1)}, u32[]{:S(2)}, u32[]{:S(2)}) collective-permute-start(f32[16,128]{1,0:T(8,128)S(1)} %get-tuple-element.33.sum_ref), channel_id=1, source_target_pairs={{0,4},{1,5},{2,6},{3,7},{4,0},{5,1},{6,2},{7,3},{8,12},{9,13},{10,... | collective-permute-start | bytes 24584 | tf_op jit(solution)/shard_map/ppermute | solution.py:21
  17.7 2.6 %collective-permute-done.5.refs_1_ = f32[16,128]{1,0:T(8,128)S(1)} collective-permute-done((f32[16,128]{1,0:T(8,128)S(1)}, f32[16,128]{1,0:T(8,128)S(1)}, u32[]{:S(2)}, u32[]{:S(2)}) %collective-permute-start.5) | collective-permute-done | bytes 8224 | tf_op jit(solution)/shard_map/ppermute | solution.py:21
  20.3 0.5 %collective-permute-done.6.refs_2_ = f32[16,128]{1,0:T(8,128)S(1)} collective-permute-done((f32[16,128]{1,0:T(8,128)S(1)}, f32[16,128]{1,0:T(8,128)S(1)}, u32[]{:S(2)}, u32[]{:S(2)}) %collective-permute-start.6) | collective-permute-done | bytes 8224 | tf_op jit(solution)/shard_map/ppermute | solution.py:21
  20.8 0.0 collective-permute-done.4.refs_0_
  20.8 0.2 shard_map.90
  21.0 1.6 %collective-permute-start.7 = (f32[32,128]{1,0:T(8,128)S(1)}, f32[32,128]{1,0:T(8,128)S(1)}, u32[]{:S(2)}, u32[]{:S(2)}) collective-permute-start(f32[32,128]{1,0:T(8,128)S(1)} %get-tuple-element.37), channel_id=1, source_target_pairs={{0,24},{8,16},{16,8},{24,0},{1,25},{9,17},{17,9},{25,1},{2,26},{10... | collective-permute-start | bytes 49160 | tf_op jit(solution)/shard_map/ppermute | solution.py:21
  22.6 0.6 %collective-permute-start.8 = (f32[32,128]{1,0:T(8,128)S(1)}, f32[32,128]{1,0:T(8,128)S(1)}, u32[]{:S(2)}, u32[]{:S(2)}) collective-permute-start(f32[32,128]{1,0:T(8,128)S(1)} %get-tuple-element.38), channel_id=1, source_target_pairs={{0,16},{8,24},{16,0},{24,8},{1,17},{9,25},{17,1},{25,9},{2,18},{10... | collective-permute-start | bytes 49160 | tf_op jit(solution)/shard_map/ppermute | solution.py:21
  23.2 2.3 %collective-permute-start.9 = (f32[32,128]{1,0:T(8,128)S(1)}, f32[32,128]{1,0:T(8,128)S(1)}, u32[]{:S(2)}, u32[]{:S(2)}) collective-permute-start(f32[32,128]{1,0:T(8,128)S(1)} %get-tuple-element.39), channel_id=1, source_target_pairs={{0,8},{8,0},{16,24},{24,16},{1,9},{9,1},{17,25},{25,17},{2,10},{10... | collective-permute-start | bytes 49160 | tf_op jit(solution)/shard_map/ppermute | solution.py:21
  25.5 0.6 %shard_map.92 = bf16[4,4,2048]{2,1,0:T(4,128)(2,1)} custom-call(f32[16,2048]{1,0:T(8,128)S(1)} %get-tuple-element.41.grad_ref), custom_call_target="tpu_custom_call" | custom-call | tf_op jit(solution)/shard_map/pallas_call | solution.py:25
  26.1 0.5 %collective-permute-done.7.refs_0_ = f32[32,128]{1,0:T(8,128)S(1)} collective-permute-done((f32[32,128]{1,0:T(8,128)S(1)}, f32[32,128]{1,0:T(8,128)S(1)}, u32[]{:S(2)}, u32[]{:S(2)}) %collective-permute-start.7) | collective-permute-done | bytes 16416 | tf_op jit(solution)/shard_map/ppermute | solution.py:21
  26.6 0.7 %collective-permute-done.8.refs_1_ = f32[32,128]{1,0:T(8,128)S(1)} collective-permute-done((f32[32,128]{1,0:T(8,128)S(1)}, f32[32,128]{1,0:T(8,128)S(1)}, u32[]{:S(2)}, u32[]{:S(2)}) %collective-permute-start.8) | collective-permute-done | bytes 16416 | tf_op jit(solution)/shard_map/ppermute | solution.py:21
  27.3 0.0 collective-permute-done.9.refs_2_
  27.4 0.6 %shard_map.91 = (f32[16,128]{1,0:T(8,128)}, bf16[4,4,512]{2,1,0:T(4,128)(2,1)}) custom-call(f32[16,128]{1,0:T(8,128)S(1)} %get-tuple-element.36.total_ref, f32[4,4,512]{2,1,0:T(4,128)S(1)} %get-tuple-element.25.kv_ref, f32[32,128]{1,0:T(8,128)S(1)} %collective-permute-done.7.refs_0_, f32[32,128]{1,0:T(8,128)S(1)} %collective-permute-done.8.refs_1_, ...), custom_call_target="tpu_custom_call" | custom-call | tf_op jit(solution)/shard_map/pallas_call | solution.py:25
  (1 shorter events, 0.0 us)
Async XLA Ops:
  0.6 5.8 %copy-start.1 = (bf16[1,1,4,4,8192]{4,3,2,1,0:T(4,128)(2,1)S(1)}, bf16[1,1,4,4,8192]{4,3,2,1,0:T(4,128)(2,1)}, u32[]{:S(2)}) copy-start(bf16[1,1,4,4,8192]{4,3,2,1,0:T(4,128)(2,1)} %param.6) | copy-start | bytes 786436
  0.6 5.8 %copy-start.2 = (f32[8192]{0:T(1024)S(1)}, f32[8192]{0:T(1024)}, u32[]{:S(2)}) copy-start(f32[8192]{0:T(1024)} %param.8) | copy-start | bytes 98308
  0.7 5.8 %copy-start.3 = (f32[8192]{0:T(1024)S(1)}, f32[8192]{0:T(1024)}, u32[]{:S(2)}) copy-start(f32[8192]{0:T(1024)} %param.9) | copy-start | bytes 98308
  0.7 5.8 %copy-start = (bf16[8192,512]{1,0:T(8,128)(2,1)S(1)}, bf16[8192,512]{1,0:T(8,128)(2,1)}, u32[]{:S(2)}) copy-start(bf16[8192,512]{1,0:T(8,128)(2,1)} %weight_ref.5) | copy-start | bytes 25165828
  0.7 7.2 %collective-permute-start = (bf16[4,4,512]{2,1,0:T(4,128)(2,1)}, bf16[4,4,512]{2,1,0:T(4,128)(2,1)S(1)}, u32[]{:S(2)}, u32[]{:S(2)}) collective-permute-start(bf16[4,4,512]{2,1,0:T(4,128)(2,1)} %bitcast.23), channel_id=1, source_target_pairs={{0,24},{8,16},{16,8},{24,0},{1,25},{9,17},{17,9},{25,1},{2,26},{10... | collective-permute-start | bytes 49160 | tf_op jit(solution)/shard_map/ppermute | solution.py:21
  5.8 4.8 %collective-permute-start.1 = (bf16[4,4,512]{2,1,0:T(4,128)(2,1)}, bf16[4,4,512]{2,1,0:T(4,128)(2,1)S(1)}, u32[]{:S(2)}, u32[]{:S(2)}) collective-permute-start(bf16[4,4,512]{2,1,0:T(4,128)(2,1)} %bitcast.24), channel_id=1, source_target_pairs={{0,16},{8,24},{16,0},{24,8},{1,17},{9,25},{17,1},{25,9},{2,18},{10... | collective-permute-start | bytes 49160 | tf_op jit(solution)/shard_map/ppermute | solution.py:21
  5.8 4.8 %collective-permute-start.2 = (bf16[4,4,512]{2,1,0:T(4,128)(2,1)}, bf16[4,4,512]{2,1,0:T(4,128)(2,1)S(1)}, u32[]{:S(2)}, u32[]{:S(2)}) collective-permute-start(bf16[4,4,512]{2,1,0:T(4,128)(2,1)} %bitcast.25), channel_id=1, source_target_pairs={{0,8},{8,0},{16,24},{24,16},{1,9},{9,1},{17,25},{25,17},{2,10},{10... | collective-permute-start | bytes 49160 | tf_op jit(solution)/shard_map/ppermute | solution.py:21
  6.4 4.2 %copy-start.4 = (bf16[1,1,4,4,512]{4,3,2,1,0:T(4,128)(2,1)S(1)}, bf16[1,1,4,4,512]{4,3,2,1,0:T(4,128)(2,1)}, u32[]{:S(2)}) copy-start(bf16[1,1,4,4,512]{4,3,2,1,0:T(4,128)(2,1)} %param.11) | copy-start | bytes 49156
  6.4 4.2 %copy-start.5 = (s32[1,1,4]{2,1,0:T(1,128)S(1)}, s32[1,1,4]{2,1,0:T(1,128)}, u32[]{:S(2)}) copy-start(s32[1,1,4]{2,1,0:T(1,128)} %param.7) | copy-start | bytes 52
  12.4 1.6 %collective-permute-start.3 = (f32[16,4480]{1,0:T(8,128)S(1)}, f32[16,4480]{1,0:T(8,128)S(1)}, u32[]{:S(2)}, u32[]{:S(2)}) collective-permute-start(f32[16,4480]{1,0:T(8,128)S(1)} %get-tuple-element.26), channel_id=1, source_target_pairs={{0,1},{1,0},{2,3},{3,2},{4,5},{5,4},{6,7},{7,6},{8,9},{9,8},{10,11... | collective-permute-start | bytes 860168 | tf_op jit(solution)/shard_map/ppermute | solution.py:21
  14.2 6.7 %collective-permute-start.4 = (bf16[16,2560]{1,0:T(8,128)(2,1)S(1)}, bf16[16,2560]{1,0:T(8,128)(2,1)S(1)}, u32[]{:S(2)}, u32[]{:S(2)}) collective-permute-start(bf16[16,2560]{1,0:T(8,128)(2,1)S(1)} %get-tuple-element.34), channel_id=1, source_target_pairs={{0,2},{1,3},{2,0},{3,1},{4,6},{5,7},{6,4},{7,5},{8,10},{9,11},{10,... | collective-permute-start | bytes 245768 | tf_op jit(solution)/shard_map/ppermute | solution.py:21
  15.7 4.5 %collective-permute-start.5 = (f32[16,128]{1,0:T(8,128)S(1)}, f32[16,128]{1,0:T(8,128)S(1)}, u32[]{:S(2)}, u32[]{:S(2)}) collective-permute-start(f32[16,128]{1,0:T(8,128)S(1)} %get-tuple-element.35), channel_id=1, source_target_pairs={{0,6},{1,7},{2,4},{3,5},{4,2},{5,3},{6,0},{7,1},{8,14},{9,15},{10,... | collective-permute-start | bytes 24584 | tf_op jit(solution)/shard_map/ppermute | solution.py:21
  17.2 3.7 %collective-permute-start.6 = (f32[16,128]{1,0:T(8,128)S(1)}, f32[16,128]{1,0:T(8,128)S(1)}, u32[]{:S(2)}, u32[]{:S(2)}) collective-permute-start(f32[16,128]{1,0:T(8,128)S(1)} %get-tuple-element.33.sum_ref), channel_id=1, source_target_pairs={{0,4},{1,5},{2,6},{3,7},{4,0},{5,1},{6,2},{7,3},{8,12},{9,13},{10,... | collective-permute-start | bytes 24584 | tf_op jit(solution)/shard_map/ppermute | solution.py:21
  21.0 5.6 %collective-permute-start.7 = (f32[32,128]{1,0:T(8,128)S(1)}, f32[32,128]{1,0:T(8,128)S(1)}, u32[]{:S(2)}, u32[]{:S(2)}) collective-permute-start(f32[32,128]{1,0:T(8,128)S(1)} %get-tuple-element.37), channel_id=1, source_target_pairs={{0,24},{8,16},{16,8},{24,0},{1,25},{9,17},{17,9},{25,1},{2,26},{10... | collective-permute-start | bytes 49160 | tf_op jit(solution)/shard_map/ppermute | solution.py:21
  22.6 4.7 %collective-permute-start.8 = (f32[32,128]{1,0:T(8,128)S(1)}, f32[32,128]{1,0:T(8,128)S(1)}, u32[]{:S(2)}, u32[]{:S(2)}) collective-permute-start(f32[32,128]{1,0:T(8,128)S(1)} %get-tuple-element.38), channel_id=1, source_target_pairs={{0,16},{8,24},{16,0},{24,8},{1,17},{9,25},{17,1},{25,9},{2,18},{10... | collective-permute-start | bytes 49160 | tf_op jit(solution)/shard_map/ppermute | solution.py:21
  23.2 4.2 %collective-permute-start.9 = (f32[32,128]{1,0:T(8,128)S(1)}, f32[32,128]{1,0:T(8,128)S(1)}, u32[]{:S(2)}, u32[]{:S(2)}) collective-permute-start(f32[32,128]{1,0:T(8,128)S(1)} %get-tuple-element.39), channel_id=1, source_target_pairs={{0,8},{8,0},{16,24},{24,16},{1,9},{9,1},{17,25},{25,17},{2,10},{10... | collective-permute-start | bytes 49160 | tf_op jit(solution)/shard_map/ppermute | solution.py:21

commit v6 on v5

--- a/solution.py
+++ b/solution.py
@@ -10,7 +10,6 @@
 LANES = 128
 PIECES = 3
 VMEM = pl.BlockSpec(memory_space=pltpu.VMEM)
-SMEM = pl.BlockSpec(memory_space=pltpu.SMEM)
 HBM = pl.BlockSpec(memory_space=pltpu.HBM)
 F32 = jnp.float32
 BF16 = jnp.bfloat16
@@ -47,6 +46,10 @@
     normed_ref[...] = (inputs * inv_rms * gain_ref[...]).astype(BF16)
     inv_ref[...] = jnp.broadcast_to(inv_rms, inv_ref.shape)
     projected_ref[...] = jnp.dot(normed_ref[...], weight_ref[...], preferred_element_type=F32)
+
+
+def kept(j):
+    return 2 * j + (1 if j else 0)
 
 
 def split(value, dtype):
@@ -103,61 +106,70 @@
     return out
 
 
-def products(k, tp, lhs_ref, weight_ref, vis_ref, bias_ref, gain_ref, inv_ref, dots_ref, rows_ref):
+def products(steps, tp, lhs, weight_ref, out_ref):
+    width = weight_ref.shape[0] // tp
+    place = lax.axis_index("tp")
+    for j, k in enumerate(steps):
+        cols = pl.ds(pl.multiple_of((place ^ k) * width, width), width)
+        out_ref[:, j * width : (j + 1) * width] = lax.dot_general(
+            lhs, weight_ref[cols, :], (((1,), (1,)), ((), ())), preferred_element_type=F32
+        )
+
+
+def row_sum(k, tp, term, vis_ref, bias_ref, gain_ref, inv_rms, dots):
     buckets, capacity, features = vis_ref.shape
     width = features // tp
     place = lax.axis_index("tp")
     cols = pl.ds(pl.multiple_of((place ^ k) * width, width), width)
-    term = lax.dot_general(
-        lhs_ref[...], weight_ref[cols, :], (((1,), (1,)), ((), ())), preferred_element_type=F32
-    )
-    for q in range(buckets):
-        rows_ref[q * capacity : (q + 1) * capacity, :] = (
-            vis_ref[q, :, cols].astype(F32) + bias_ref[:, cols]
-        )
-    inv_rms = inv_ref[:, :1]
-    scale = inv_rms * inv_rms * dots_ref[:, :1] / features
+    scale = inv_rms * inv_rms * dots * (1.0 / features)
     row = gain_ref[:, cols] * jnp.sum(inv_rms * term, axis=0, keepdims=True)
-    return term, row - jnp.sum(rows_ref[...] * scale, axis=0, keepdims=True)
+    for q in range(buckets):
+        part = scale[q * capacity : (q + 1) * capacity]
+        inputs = vis_ref[q, :, cols].astype(F32) + bias_ref[:, cols]
+        row = row - jnp.sum(inputs * part, axis=0, keepdims=True)
+    return row
 
 
 def sent_kernel(enc, tp, counts_ref, projected_ref, weight_ref, vis_ref, bias_ref, gain_ref, inv_ref, *refs):
     cots = refs[:enc]
-    kv_ref, dots_ref, lhs_ref, send_ref, picked_ref, masked_ref, rows_ref = refs[enc:]
+    kv_ref, dots_ref, lhs_ref, send_ref = refs[enc:]
     buckets, capacity, columns = kv_ref.shape
     me = lax.axis_index("enc")
     cots = cots[::-1]
-    for k in range(enc):
-        picked_ref[me ^ k] = cots[k][me].astype(F32)
     slot = lax.broadcasted_iota(jnp.int32, (capacity, columns), 0)
-    for q in range(buckets):
-        rows = slice(q * capacity, (q + 1) * capacity)
-        live = slot < counts_ref[0, q]
-        masked_ref[rows, :] = jnp.where(live, picked_ref[q], 0.0)
-        kv_ref[q] = jnp.where(live, projected_ref[rows, :], 0.0)
-    masked = masked_ref[...]
+    blocks = [cot[me].astype(F32) for cot in cots]
+    parts = []
+    for q in range(buckets):
+        block = blocks[0]
+        for k in range(1, enc):
+            block = jnp.where((me ^ k) == q, blocks[k], block)
+        live = slot < counts_ref[:, q : q + 1]
+        parts.append(jnp.where(live, block, 0.0))
+        kv_ref[q] = jnp.where(live, projected_ref[q * capacity : (q + 1) * capacity, :], 0.0)
+    masked = jnp.concatenate(parts, axis=0)
+    lhs = masked.astype(BF16)
+    lhs_ref[...] = lhs
+    steps = [kept(j) ^ 1 for j in range(tp // 2)]
+    products(steps, tp, lhs, weight_ref, send_ref)
     dots = jnp.sum(masked * projected_ref[...], axis=1, keepdims=True)
-    dots = jnp.broadcast_to(dots, dots_ref.shape)
-    dots_ref[...] = dots
-    lhs_ref[...] = masked.astype(BF16)
+    dots_ref[...] = jnp.broadcast_to(dots, dots_ref.shape)
     width = vis_ref.shape[2] // tp
     chunks, half = width // LANES, tp // 2 * width
-    for j in range(tp // 2):
-        term, row = products(
-            2 * j + 1, tp, lhs_ref, weight_ref, vis_ref, bias_ref, gain_ref, inv_ref, dots_ref, rows_ref
-        )
-        send_ref[:, j * width : (j + 1) * width] = term
-        put_side(send_ref, half, None if j else dots, row, j * chunks, chunks)
-
-
-def kept_kernel(tp, lhs_ref, weight_ref, vis_ref, bias_ref, gain_ref, inv_ref, dots_ref, kept_ref, sums_ref, rows_ref):
+    inv_rms = inv_ref[:, :1]
+    for j, k in enumerate(steps):
+        term = send_ref[:, j * width : (j + 1) * width]
+        row = row_sum(k, tp, term, vis_ref, bias_ref, gain_ref, inv_rms, dots)
+        put_side(send_ref, half, None if j else dots_ref[...], row, j * chunks, chunks)
+
+
+def kept_kernel(tp, lhs_ref, weight_ref, vis_ref, bias_ref, gain_ref, inv_ref, dots_ref, kept_ref, sums_ref):
     width = vis_ref.shape[2] // tp
     chunks = width // LANES
-    for j in range(tp // 2):
-        term, row = products(
-            2 * j, tp, lhs_ref, weight_ref, vis_ref, bias_ref, gain_ref, inv_ref, dots_ref, rows_ref
-        )
-        kept_ref[:, j * width : (j + 1) * width] = term
+    steps = [kept(j) for j in range(tp // 2)]
+    products(steps, tp, lhs_ref[...], weight_ref, kept_ref)
+    for j, k in enumerate(steps):
+        term = kept_ref[:, j * width : (j + 1) * width]
+        row = row_sum(k, tp, term, vis_ref, bias_ref, gain_ref, inv_ref[:, :1], dots_ref[:, :1])
         for i in range(chunks):
             sums_ref[j * chunks + i : j * chunks + i + 1, :] = row[:, i * LANES : (i + 1) * LANES]
 
@@ -278,19 +290,12 @@
             struct((rows, half + side(pairs * chunks, rows, F32)), F32),
         ),
         (counts[0], projected, kv_weight, vis, bias, gain, inv_rms, *cots[::-1]),
-        scratch=[
-            pltpu.VMEM((buckets, capacity, columns), F32),
-            pltpu.VMEM((rows, columns), F32),
-            pltpu.VMEM((rows, width), F32),
-        ],
-        specs=[SMEM, *[VMEM] * (6 + enc)],
     )
     got = swap(send, "tp", 1)
-    kept, sums = run(
+    terms, sums = run(
         part(kept_kernel, tp),
         (struct((rows, half), F32), struct((pairs * chunks, LANES), F32)),
         (lhs, kv_weight, vis, bias, gain, inv_rms, dots),
-        scratch=[pltpu.VMEM((rows, width), F32)],
     )
     dots, own, *refs = run(
         part(fold_kernel, width),
@@ -300,12 +305,12 @@
             *[struct((rows, width + side(chunks, rows, BF16)), BF16)] * (pairs - 1),
             *[struct((chunks, LANES), F32)] * pairs,
         ),
-        (got, kept, dots, sums),
+        (got, terms, dots, sums),
     )
     sends, totals = refs[: pairs - 1], refs[pairs - 1 :]
-    gots = [swap(s, "tp", 2 * (j + 1)) for j, s in enumerate(sends)]
+    gots = [swap(s, "tp", kept(j + 1)) for j, s in enumerate(sends)]
     others = [
-        swap(t, ("llm", "tp"), tp * g + 2 * j) for g in range(1, llm) for j, t in enumerate(totals)
+        swap(t, ("llm", "tp"), tp * g + kept(j)) for g in range(1, llm) for j, t in enumerate(totals)
     ]
     grad, total, *sends = run(
         part(combine_kernel, enc, pairs),

time: 28.1 us -> 27.3 us (0.972)
  Pallas kernels: 5.99 us -> 5.45 us
  starting transfers between devices: 13.8 us -> 13.5 us
    pallas_call x8, Pallas kernels: 5.99 us -> 5.45 us  [call(): pl.pallas_call(kernel, out_shape=tuple(outs), in_specs=specs or [VMEM] *...]
where the time goes in v6:
time: 27.3 us; the launch traced here: 27.2 us
  starting transfers between devices  13.5 us (49%)
  waiting for transfers between devices  7.4 us (27%)
  Pallas kernels  5.45 us (20%)
  between operations  0.73 us (3%)
    ppermute x10, starting transfers between devices, swap(): return lax.ppermute(x, axis, [(i, i ^ k) for i in range(n)])  13.5 us
    ppermute x10, waiting for transfers between devices, swap(): return lax.ppermute(x, axis, [(i, i ^ k) for i in range(n)])  7.4 us
    pallas_call x8, Pallas kernels, call(): pl.pallas_call(kernel, out_shape=tuple(outs), in_specs=specs or [VMEM] *...  5.45 us
  transfers between devices with their start and end apart: 10, of which 6 were waited for; matrix products, arithmetic and copies ran while one was open for 0% of the time, Pallas kernels for 12%

profile of v6, /device:TPU:0, one launch (start us, length us, event | category | flops | bytes accessed | tf_op | source)
XLA Modules:
  0.0 27.2 jit_solution(17888042089795157013)
XLA Ops:
  0.6 0.0 copy-start.1
  0.6 0.0 copy-start.2
  0.7 0.0 copy-start.3
  0.7 0.0 copy-start
  0.7 5.1 %collective-permute-start = (bf16[4,4,512]{2,1,0:T(4,128)(2,1)}, bf16[4,4,512]{2,1,0:T(4,128)(2,1)S(1)}, u32[]{:S(2)}, u32[]{:S(2)}) collective-permute-start(bf16[4,4,512]{2,1,0:T(4,128)(2,1)} %bitcast.23), channel_id=1, source_target_pairs={{0,24},{8,16},{16,8},{24,0},{1,25},{9,17},{17,9},{25,1},{2,26},{10... | collective-permute-start | bytes 49160 | tf_op jit(solution)/shard_map/ppermute | solution.py:20
  5.8 0.0 collective-permute-start.1
  5.8 0.6 %collective-permute-start.2 = (bf16[4,4,512]{2,1,0:T(4,128)(2,1)}, bf16[4,4,512]{2,1,0:T(4,128)(2,1)S(1)}, u32[]{:S(2)}, u32[]{:S(2)}) collective-permute-start(bf16[4,4,512]{2,1,0:T(4,128)(2,1)} %bitcast.25), channel_id=1, source_target_pairs={{0,8},{8,0},{16,24},{24,16},{1,9},{9,1},{17,25},{25,17},{2,10},{10... | collective-permute-start | bytes 49160 | tf_op jit(solution)/shard_map/ppermute | solution.py:20
  6.4 0.0 copy-start.4
  6.4 0.0 copy-start.5
  6.4 0.0 copy-done.1
  6.4 0.0 copy-done.2
  6.5 0.0 copy-done.3
  6.5 0.0 copy-done
  6.5 1.4 %shard_map.86 = (f32[16,512]{1,0:T(8,128)S(1)}, f32[16,128]{1,0:T(8,128)S(1)}) custom-call(bf16[4,4,8192]{2,1,0:T(4,128)(2,1)S(1)} %bitcast.9, f32[1,8192]{1,0:T(1,128)S(1)} %bitcast.14, f32[1,8192]{1,0:T(1,128)S(1)} %bitcast.19, bf16[8192,512]{1,0:T(8,128)(2,1)S(1)} %copy-done, f32[8,128]{1,0:T(8,128)S(1)} %shard_map.85._), custom_call_target="tpu_custom_call" | custom-call | tf_op jit(solution)/shard_map/pallas_call | solution.py:24
  7.9 0.0 collective-permute-done.refs_0_
  7.9 2.7 %collective-permute-done.1.refs_1_ = bf16[4,4,512]{2,1,0:T(4,128)(2,1)S(1)} collective-permute-done((bf16[4,4,512]{2,1,0:T(4,128)(2,1)}, bf16[4,4,512]{2,1,0:T(4,128)(2,1)S(1)}, u32[]{:S(2)}, u32[]{:S(2)}) %collective-permute-start.1) | collective-permute-done | bytes 16416 | tf_op jit(solution)/shard_map/ppermute | solution.py:20
  10.6 0.0 collective-permute-done.2.refs_2_
  10.6 0.0 copy-done.4
  10.6 0.0 copy-done.5
  10.6 1.2 %shard_map.87 = (f32[4,4,512]{2,1,0:T(4,128)S(1)}, f32[16,128]{1,0:T(8,128)S(1)}, bf16[16,512]{1,0:T(8,128)(2,1)S(1)}, f32[16,4480]{1,0:T(8,128)S(1)}) custom-call(s32[1,4]{1,0:T(1,128)S(1)} %bitcast.27, f32[16,512]{1,0:T(8,128)S(1)} %get-tuple-element.24.projected_ref, bf16[8192,512]{1,0:T(8,128)(2,1)S(1)} %copy-done, bf16[4,4,8192]{2,1,0:T(4,128)(2,1)S(1)} %bitcast.10, ...), custom_call_target="tpu_custom_call" | custom-call | tf_op jit(solution)/shard_map/pallas_call | solution.py:24
  11.9 0.1 collective-permute-start.3
  12.0 1.2 %shard_map.88 = (f32[16,4096]{1,0:T(8,128)S(1)}, f32[32,128]{1,0:T(8,128)S(1)}) custom-call(bf16[16,512]{1,0:T(8,128)(2,1)S(1)} %get-tuple-element.27.lhs_ref, bf16[8192,512]{1,0:T(8,128)(2,1)S(1)} %copy-done, bf16[4,4,8192]{2,1,0:T(4,128)(2,1)S(1)} %bitcast.11, f32[1,8192]{1,0:T(1,128)S(1)} %bitcast.16, f32[1,8192]{1,0:T(1,128)S(1)} %bitcast.21, ...), custom_call_target="tpu_custom_call" | custom-call | tf_op jit(solution)/shard_map/pallas_call | solution.py:24
  13.2 0.3 %collective-permute-done.3.got_ref = f32[16,4480]{1,0:T(8,128)S(1)} collective-permute-done((f32[16,4480]{1,0:T(8,128)S(1)}, f32[16,4480]{1,0:T(8,128)S(1)}, u32[]{:S(2)}, u32[]{:S(2)}) %collective-permute-start.3) | collective-permute-done | bytes 286752 | tf_op jit(solution)/shard_map/ppermute | solution.py:20
  13.5 0.1 shard_map.89
  13.6 1.4 %collective-permute-start.4 = (bf16[16,2560]{1,0:T(8,128)(2,1)S(1)}, bf16[16,2560]{1,0:T(8,128)(2,1)S(1)}, u32[]{:S(2)}, u32[]{:S(2)}) collective-permute-start(bf16[16,2560]{1,0:T(8,128)(2,1)S(1)} %get-tuple-element.34), channel_id=1, source_target_pairs={{0,3},{1,2},{2,1},{3,0},{4,7},{5,6},{6,5},{7,4},{8,11},{9,10},{10,... | collective-permute-start | bytes 245768 | tf_op jit(solution)/shard_map/ppermute | solution.py:20
  15.0 1.4 %collective-permute-start.5 = (f32[16,128]{1,0:T(8,128)S(1)}, f32[16,128]{1,0:T(8,128)S(1)}, u32[]{:S(2)}, u32[]{:S(2)}) collective-permute-start(f32[16,128]{1,0:T(8,128)S(1)} %get-tuple-element.35), channel_id=1, source_target_pairs={{0,7},{1,6},{2,5},{3,4},{4,3},{5,2},{6,1},{7,0},{8,15},{9,14},{10,... | collective-permute-start | bytes 24584 | tf_op jit(solution)/shard_map/ppermute | solution.py:20
  16.4 0.5 %collective-permute-start.6 = (f32[16,128]{1,0:T(8,128)S(1)}, f32[16,128]{1,0:T(8,128)S(1)}, u32[]{:S(2)}, u32[]{:S(2)}) collective-permute-start(f32[16,128]{1,0:T(8,128)S(1)} %get-tuple-element.33.sum_ref), channel_id=1, source_target_pairs={{0,4},{1,5},{2,6},{3,7},{4,0},{5,1},{6,2},{7,3},{8,12},{9,13},{10,... | collective-permute-start | bytes 24584 | tf_op jit(solution)/shard_map/ppermute | solution.py:20
  16.9 2.1 %collective-permute-done.5.refs_1_ = f32[16,128]{1,0:T(8,128)S(1)} collective-permute-done((f32[16,128]{1,0:T(8,128)S(1)}, f32[16,128]{1,0:T(8,128)S(1)}, u32[]{:S(2)}, u32[]{:S(2)}) %collective-permute-start.5) | collective-permute-done | bytes 8224 | tf_op jit(solution)/shard_map/ppermute | solution.py:20
  19.0 1.0 %collective-permute-done.6.refs_2_ = f32[16,128]{1,0:T(8,128)S(1)} collective-permute-done((f32[16,128]{1,0:T(8,128)S(1)}, f32[16,128]{1,0:T(8,128)S(1)}, u32[]{:S(2)}, u32[]{:S(2)}) %collective-permute-start.6) | collective-permute-done | bytes 8224 | tf_op jit(solution)/shard_map/ppermute | solution.py:20
  20.0 0.0 collective-permute-done.4.refs_0_
  20.0 0.2 shard_map.90
  20.2 1.6 %collective-permute-start.7 = (f32[32,128]{1,0:T(8,128)S(1)}, f32[32,128]{1,0:T(8,128)S(1)}, u32[]{:S(2)}, u32[]{:S(2)}) collective-permute-start(f32[32,128]{1,0:T(8,128)S(1)} %get-tuple-element.37), channel_id=1, source_target_pairs={{0,24},{8,16},{16,8},{24,0},{1,25},{9,17},{17,9},{25,1},{2,26},{10... | collective-permute-start | bytes 49160 | tf_op jit(solution)/shard_map/ppermute | solution.py:20
  21.7 0.6 %collective-permute-start.8 = (f32[32,128]{1,0:T(8,128)S(1)}, f32[32,128]{1,0:T(8,128)S(1)}, u32[]{:S(2)}, u32[]{:S(2)}) collective-permute-start(f32[32,128]{1,0:T(8,128)S(1)} %get-tuple-element.38), channel_id=1, source_target_pairs={{0,16},{8,24},{16,0},{24,8},{1,17},{9,25},{17,1},{25,9},{2,18},{10... | collective-permute-start | bytes 49160 | tf_op jit(solution)/shard_map/ppermute | solution.py:20
  22.3 2.3 %collective-permute-start.9 = (f32[32,128]{1,0:T(8,128)S(1)}, f32[32,128]{1,0:T(8,128)S(1)}, u32[]{:S(2)}, u32[]{:S(2)}) collective-permute-start(f32[32,128]{1,0:T(8,128)S(1)} %get-tuple-element.39), channel_id=1, source_target_pairs={{0,8},{8,0},{16,24},{24,16},{1,9},{9,1},{17,25},{25,17},{2,10},{10... | collective-permute-start | bytes 49160 | tf_op jit(solution)/shard_map/ppermute | solution.py:20
  24.6 0.6 %shard_map.92 = bf16[4,4,2048]{2,1,0:T(4,128)(2,1)} custom-call(f32[16,2048]{1,0:T(8,128)S(1)} %get-tuple-element.41.grad_ref), custom_call_target="tpu_custom_call" | custom-call | tf_op jit(solution)/shard_map/pallas_call | solution.py:24
  25.3 0.5 %collective-permute-done.7.refs_0_ = f32[32,128]{1,0:T(8,128)S(1)} collective-permute-done((f32[32,128]{1,0:T(8,128)S(1)}, f32[32,128]{1,0:T(8,128)S(1)}, u32[]{:S(2)}, u32[]{:S(2)}) %collective-permute-start.7) | collective-permute-done | bytes 16416 | tf_op jit(solution)/shard_map/ppermute | solution.py:20
  25.8 0.7 %collective-permute-done.8.refs_1_ = f32[32,128]{1,0:T(8,128)S(1)} collective-permute-done((f32[32,128]{1,0:T(8,128)S(1)}, f32[32,128]{1,0:T(8,128)S(1)}, u32[]{:S(2)}, u32[]{:S(2)}) %collective-permute-start.8) | collective-permute-done | bytes 16416 | tf_op jit(solution)/shard_map/ppermute | solution.py:20
  26.5 0.0 collective-permute-done.9.refs_2_
  26.5 0.6 %shard_map.91 = (f32[16,128]{1,0:T(8,128)}, bf16[4,4,512]{2,1,0:T(4,128)(2,1)}) custom-call(f32[16,128]{1,0:T(8,128)S(1)} %get-tuple-element.36.total_ref, f32[4,4,512]{2,1,0:T(4,128)S(1)} %get-tuple-element.25.kv_ref, f32[32,128]{1,0:T(8,128)S(1)} %collective-permute-done.7.refs_0_, f32[32,128]{1,0:T(8,128)S(1)} %collective-permute-done.8.refs_1_, ...), custom_call_target="tpu_custom_call" | custom-call | tf_op jit(solution)/shard_map/pallas_call | solution.py:24
  (1 shorter events, 0.0 us)
Async XLA Ops:
  0.6 5.8 %copy-start.1 = (bf16[1,1,4,4,8192]{4,3,2,1,0:T(4,128)(2,1)S(1)}, bf16[1,1,4,4,8192]{4,3,2,1,0:T(4,128)(2,1)}, u32[]{:S(2)}) copy-start(bf16[1,1,4,4,8192]{4,3,2,1,0:T(4,128)(2,1)} %param.6) | copy-start | bytes 786436
  0.6 5.8 %copy-start.2 = (f32[8192]{0:T(1024)S(1)}, f32[8192]{0:T(1024)}, u32[]{:S(2)}) copy-start(f32[8192]{0:T(1024)} %param.8) | copy-start | bytes 98308
  0.7 5.8 %copy-start.3 = (f32[8192]{0:T(1024)S(1)}, f32[8192]{0:T(1024)}, u32[]{:S(2)}) copy-start(f32[8192]{0:T(1024)} %param.9) | copy-start | bytes 98308
  0.7 5.8 %copy-start = (bf16[8192,512]{1,0:T(8,128)(2,1)S(1)}, bf16[8192,512]{1,0:T(8,128)(2,1)}, u32[]{:S(2)}) copy-start(bf16[8192,512]{1,0:T(8,128)(2,1)} %weight_ref.5) | copy-start | bytes 25165828
  0.7 7.2 %collective-permute-start = (bf16[4,4,512]{2,1,0:T(4,128)(2,1)}, bf16[4,4,512]{2,1,0:T(4,128)(2,1)S(1)}, u32[]{:S(2)}, u32[]{:S(2)}) collective-permute-start(bf16[4,4,512]{2,1,0:T(4,128)(2,1)} %bitcast.23), channel_id=1, source_target_pairs={{0,24},{8,16},{16,8},{24,0},{1,25},{9,17},{17,9},{25,1},{2,26},{10... | collective-permute-start | bytes 49160 | tf_op jit(solution)/shard_map/ppermute | solution.py:20
  5.8 4.8 %collective-permute-start.1 = (bf16[4,4,512]{2,1,0:T(4,128)(2,1)}, bf16[4,4,512]{2,1,0:T(4,128)(2,1)S(1)}, u32[]{:S(2)}, u32[]{:S(2)}) collective-permute-start(bf16[4,4,512]{2,1,0:T(4,128)(2,1)} %bitcast.24), channel_id=1, source_target_pairs={{0,16},{8,24},{16,0},{24,8},{1,17},{9,25},{17,1},{25,9},{2,18},{10... | collective-permute-start | bytes 49160 | tf_op jit(solution)/shard_map/ppermute | solution.py:20
  5.8 4.8 %collective-permute-start.2 = (bf16[4,4,512]{2,1,0:T(4,128)(2,1)}, bf16[4,4,512]{2,1,0:T(4,128)(2,1)S(1)}, u32[]{:S(2)}, u32[]{:S(2)}) collective-permute-start(bf16[4,4,512]{2,1,0:T(4,128)(2,1)} %bitcast.25), channel_id=1, source_target_pairs={{0,8},{8,0},{16,24},{24,16},{1,9},{9,1},{17,25},{25,17},{2,10},{10... | collective-permute-start | bytes 49160 | tf_op jit(solution)/shard_map/ppermute | solution.py:20
  6.4 4.2 %copy-start.4 = (bf16[1,1,4,4,512]{4,3,2,1,0:T(4,128)(2,1)S(1)}, bf16[1,1,4,4,512]{4,3,2,1,0:T(4,128)(2,1)}, u32[]{:S(2)}) copy-start(bf16[1,1,4,4,512]{4,3,2,1,0:T(4,128)(2,1)} %param.11) | copy-start | bytes 49156
  6.4 4.2 %copy-start.5 = (s32[1,1,4]{2,1,0:T(1,128)S(1)}, s32[1,1,4]{2,1,0:T(1,128)}, u32[]{:S(2)}) copy-start(s32[1,1,4]{2,1,0:T(1,128)} %param.7) | copy-start | bytes 52
  11.9 1.6 %collective-permute-start.3 = (f32[16,4480]{1,0:T(8,128)S(1)}, f32[16,4480]{1,0:T(8,128)S(1)}, u32[]{:S(2)}, u32[]{:S(2)}) collective-permute-start(f32[16,4480]{1,0:T(8,128)S(1)} %get-tuple-element.26), channel_id=1, source_target_pairs={{0,1},{1,0},{2,3},{3,2},{4,5},{5,4},{6,7},{7,6},{8,9},{9,8},{10,11... | collective-permute-start | bytes 860168 | tf_op jit(solution)/shard_map/ppermute | solution.py:20
  13.6 6.4 %collective-permute-start.4 = (bf16[16,2560]{1,0:T(8,128)(2,1)S(1)}, bf16[16,2560]{1,0:T(8,128)(2,1)S(1)}, u32[]{:S(2)}, u32[]{:S(2)}) collective-permute-start(bf16[16,2560]{1,0:T(8,128)(2,1)S(1)} %get-tuple-element.34), channel_id=1, source_target_pairs={{0,3},{1,2},{2,1},{3,0},{4,7},{5,6},{6,5},{7,4},{8,11},{9,10},{10,... | collective-permute-start | bytes 245768 | tf_op jit(solution)/shard_map/ppermute | solution.py:20
  15.0 4.0 %collective-permute-start.5 = (f32[16,128]{1,0:T(8,128)S(1)}, f32[16,128]{1,0:T(8,128)S(1)}, u32[]{:S(2)}, u32[]{:S(2)}) collective-permute-start(f32[16,128]{1,0:T(8,128)S(1)} %get-tuple-element.35), channel_id=1, source_target_pairs={{0,7},{1,6},{2,5},{3,4},{4,3},{5,2},{6,1},{7,0},{8,15},{9,14},{10,... | collective-permute-start | bytes 24584 | tf_op jit(solution)/shard_map/ppermute | solution.py:20
  16.4 3.7 %collective-permute-start.6 = (f32[16,128]{1,0:T(8,128)S(1)}, f32[16,128]{1,0:T(8,128)S(1)}, u32[]{:S(2)}, u32[]{:S(2)}) collective-permute-start(f32[16,128]{1,0:T(8,128)S(1)} %get-tuple-element.33.sum_ref), channel_id=1, source_target_pairs={{0,4},{1,5},{2,6},{3,7},{4,0},{5,1},{6,2},{7,3},{8,12},{9,13},{10,... | collective-permute-start | bytes 24584 | tf_op jit(solution)/shard_map/ppermute | solution.py:20
  20.2 5.6 %collective-permute-start.7 = (f32[32,128]{1,0:T(8,128)S(1)}, f32[32,128]{1,0:T(8,128)S(1)}, u32[]{:S(2)}, u32[]{:S(2)}) collective-permute-start(f32[32,128]{1,0:T(8,128)S(1)} %get-tuple-element.37), channel_id=1, source_target_pairs={{0,24},{8,16},{16,8},{24,0},{1,25},{9,17},{17,9},{25,1},{2,26},{10... | collective-permute-start | bytes 49160 | tf_op jit(solution)/shard_map/ppermute | solution.py:20
  21.7 4.7 %collective-permute-start.8 = (f32[32,128]{1,0:T(8,128)S(1)}, f32[32,128]{1,0:T(8,128)S(1)}, u32[]{:S(2)}, u32[]{:S(2)}) collective-permute-start(f32[32,128]{1,0:T(8,128)S(1)} %get-tuple-element.38), channel_id=1, source_target_pairs={{0,16},{8,24},{16,0},{24,8},{1,17},{9,25},{17,1},{25,9},{2,18},{10... | collective-permute-start | bytes 49160 | tf_op jit(solution)/shard_map/ppermute | solution.py:20
  22.3 4.2 %collective-permute-start.9 = (f32[32,128]{1,0:T(8,128)S(1)}, f32[32,128]{1,0:T(8,128)S(1)}, u32[]{:S(2)}, u32[]{:S(2)}) collective-permute-start(f32[32,128]{1,0:T(8,128)S(1)} %get-tuple-element.39), channel_id=1, source_target_pairs={{0,8},{8,0},{16,24},{24,16},{1,9},{9,1},{17,25},{25,17},{2,10},{10... | collective-permute-start | bytes 49160 | tf_op jit(solution)/shard_map/ppermute | solution.py:20

commit v7 on v6

--- a/solution.py
+++ b/solution.py
@@ -63,47 +63,38 @@
 
 
 def side(count, rows, dtype):
-    return LANES + len(split_shape(dtype)) * -(-count // rows) * LANES
-
-
-def split_shape(dtype):
-    return range(1 if dtype == F32 else PIECES)
-
-
-def put_side(send_ref, start, dots, row, at, count):
+    return LANES * (1 + (1 if dtype == F32 else PIECES) * -(-count // rows))
+
+
+def put_side(send_ref, start, dots, lines):
     rows, dtype = send_ref.shape[0], send_ref.dtype
-    if dots is not None:
-        lane = lax.broadcasted_iota(jnp.int32, dots.shape, 1)
-        block = jnp.zeros(dots.shape, F32)
-        for i, piece in enumerate(split(dots, dtype)):
-            block = jnp.where(lane == i, piece.astype(F32), block)
-        send_ref[:, start : start + LANES] = block.astype(dtype)
-    blocks = (send_ref.shape[1] - start) // LANES - 1
-    blocks //= len(split_shape(dtype))
-    for i, piece in enumerate(split(row, dtype)):
-        for j in range(count):
-            line, col = (at + j) % rows, start + LANES * (1 + i * blocks + (at + j) // rows)
-            send_ref[line : line + 1, col : col + LANES] = piece[:, j * LANES : (j + 1) * LANES]
+    lane = lax.broadcasted_iota(jnp.int32, dots.shape, 1)
+    block = jnp.zeros(dots.shape, F32)
+    for i, piece in enumerate(split(dots, dtype)):
+        block = jnp.where(lane == i, piece.astype(F32), block)
+    blocks = [block.astype(dtype)]
+    spare = -lines.shape[0] % rows
+    if spare:
+        lines = jnp.concatenate([lines, jnp.zeros((spare, LANES), F32)], axis=0)
+    for piece in split(lines, dtype):
+        blocks += [piece[i : i + rows] for i in range(0, piece.shape[0], rows)]
+    for i, block in enumerate(blocks):
+        send_ref[:, start + i * LANES : start + (i + 1) * LANES] = block
 
 
 def get_dots(got_ref, start):
     return jnp.sum(got_ref[:, start : start + LANES].astype(F32), axis=1, keepdims=True)
 
 
-def get_side(got_ref, start, at, count):
-    rows, dtype = got_ref.shape[0], got_ref.dtype
-    blocks = (got_ref.shape[1] - start) // LANES - 1
-    blocks //= len(split_shape(dtype))
-    out = []
-    for j in range(0, count):
-        line = (at + j) % rows
-        total = None
-        for i in split_shape(dtype):
-            col = start + LANES * (1 + i * blocks + (at + j) // rows)
-            piece = got_ref[line : line + 1, col : col + LANES].astype(F32)
-            total = piece if total is None else total + piece
-        out.append(total)
-    return out
+def get_lines(got_ref, start, count):
+    rows = got_ref.shape[0]
+    each = -(-count // rows)
+    blocks = [got_ref[:, i : i + LANES].astype(F32) for i in range(start + LANES, got_ref.shape[1], LANES)]
+    total = None
+    for i in range(0, len(blocks), each):
+        piece = blocks[i] if each == 1 else jnp.concatenate(blocks[i : i + each], axis=0)
+        total = piece if total is None else total + piece
+    return total[:count]
 
 
 def products(steps, tp, lhs, weight_ref, out_ref):
@@ -132,7 +123,7 @@
 
 def sent_kernel(enc, tp, counts_ref, projected_ref, weight_ref, vis_ref, bias_ref, gain_ref, inv_ref, *refs):
     cots = refs[:enc]
-    kv_ref, dots_ref, lhs_ref, send_ref = refs[enc:]
+    kv_ref, dots_ref, lhs_ref, send_ref, sums_ref = refs[enc:]
     buckets, capacity, columns = kv_ref.shape
     me = lax.axis_index("enc")
     cots = cots[::-1]
@@ -159,7 +150,9 @@
     for j, k in enumerate(steps):
         term = send_ref[:, j * width : (j + 1) * width]
         row = row_sum(k, tp, term, vis_ref, bias_ref, gain_ref, inv_rms, dots)
-        put_side(send_ref, half, None if j else dots_ref[...], row, j * chunks, chunks)
+        for i in range(chunks):
+            sums_ref[j * chunks + i : j * chunks + i + 1, :] = row[:, i * LANES : (i + 1) * LANES]
+    put_side(send_ref, half, dots_ref[...], sums_ref[...])
 
 
 def kept_kernel(tp, lhs_ref, weight_ref, vis_ref, bias_ref, gain_ref, inv_ref, dots_ref, kept_ref, sums_ref):
@@ -180,16 +173,15 @@
     sends, totals = refs[: pairs - 1], refs[pairs - 1 :]
     dots = dots_ref[...] + get_dots(got_ref, half)
     all_ref[...] = dots
+    sums = sums_ref[...] + get_lines(got_ref, half, pairs * chunks)
     for j in range(pairs):
         cols = slice(j * width, (j + 1) * width)
         term = kept_ref[:, cols] + got_ref[:, cols]
-        for i, line in enumerate(get_side(got_ref, half, j * chunks, chunks)):
-            row = sums_ref[j * chunks + i : j * chunks + i + 1, :] + line
-            totals[j][i : i + 1, :] = row
-            if j:
-                put_side(sends[j - 1], width, None if i else dots, row, i, 1)
+        lines = sums[j * chunks : (j + 1) * chunks]
+        totals[j][...] = lines
         if j:
             sends[j - 1][:, :width] = term.astype(BF16)
+            put_side(sends[j - 1], width, dots, lines)
         else:
             own_ref[...] = term
 
@@ -207,12 +199,11 @@
     total = sum_ref[...]
     for got in sums:
         total = total + got[...]
+    for got in gots:
+        total = total + get_lines(got, width, chunks)
     total_ref[...] = total
-    for got in gots:
-        for i, line in enumerate(get_side(got, width, 0, chunks)):
-            total_ref[i : i + 1, :] = total_ref[i : i + 1, :] + line
     for k in range(1, enc):
-        sends[k - 1][:chunks, :] = total_ref[...]
+        sends[k - 1][:chunks, :] = total
         block = kv_ref[me ^ k]
         for j in range(block.shape[1] // LANES):
             at = chunks + j * capacity
@@ -290,6 +281,7 @@
             struct((rows, half + side(pairs * chunks, rows, F32)), F32),
         ),
         (counts[0], projected, kv_weight, vis, bias, gain, inv_rms, *cots[::-1]),
+        scratch=[pltpu.VMEM((pairs * chunks, LANES), F32)],
     )
     got = swap(send, "tp", 1)
     terms, sums = run(

time: 27.3 us -> 27.3 us (level)
  no operation moved by 1% of the time
where the time goes in v7:
time: 27.3 us; the launch traced here: 27.1 us
  starting transfers between devices  13.5 us (49%)
  waiting for transfers between devices  7.4 us (27%)
  Pallas kernels  5.46 us (20%)
  between operations  0.73 us (3%)
    ppermute x10, starting transfers between devices, swap(): return lax.ppermute(x, axis, [(i, i ^ k) for i in range(n)])  13.5 us
    ppermute x10, waiting for transfers between devices, swap(): return lax.ppermute(x, axis, [(i, i ^ k) for i in range(n)])  7.4 us
    pallas_call x8, Pallas kernels, call(): pl.pallas_call(kernel, out_shape=tuple(outs), in_specs=specs or [VMEM] *...  5.46 us
  transfers between devices with their start and end apart: 10, of which 6 were waited for; matrix products, arithmetic and copies ran while one was open for 0% of the time, Pallas kernels for 12%

profile of v7, /device:TPU:0, one launch (start us, length us, event | category | flops | bytes accessed | tf_op | source)
XLA Modules:
  0.0 27.1 jit_solution(1063943614612103531)
XLA Ops:
  0.6 0.0 copy-start.1
  0.6 0.0 copy-start.2
  0.7 0.0 copy-start.3
  0.7 0.0 copy-start
  0.7 5.1 %collective-permute-start = (bf16[4,4,512]{2,1,0:T(4,128)(2,1)}, bf16[4,4,512]{2,1,0:T(4,128)(2,1)S(1)}, u32[]{:S(2)}, u32[]{:S(2)}) collective-permute-start(bf16[4,4,512]{2,1,0:T(4,128)(2,1)} %bitcast.23), channel_id=1, source_target_pairs={{0,24},{8,16},{16,8},{24,0},{1,25},{9,17},{17,9},{25,1},{2,26},{10... | collective-permute-start | bytes 49160 | tf_op jit(solution)/shard_map/ppermute | solution.py:20
  5.8 0.0 collective-permute-start.1
  5.8 0.6 %collective-permute-start.2 = (bf16[4,4,512]{2,1,0:T(4,128)(2,1)}, bf16[4,4,512]{2,1,0:T(4,128)(2,1)S(1)}, u32[]{:S(2)}, u32[]{:S(2)}) collective-permute-start(bf16[4,4,512]{2,1,0:T(4,128)(2,1)} %bitcast.25), channel_id=1, source_target_pairs={{0,8},{8,0},{16,24},{24,16},{1,9},{9,1},{17,25},{25,17},{2,10},{10... | collective-permute-start | bytes 49160 | tf_op jit(solution)/shard_map/ppermute | solution.py:20
  6.4 0.0 copy-start.4
  6.4 0.0 copy-start.5
  6.4 0.0 copy-done.1
  6.4 0.0 copy-done.2
  6.5 0.0 copy-done.3
  6.5 0.0 copy-done
  6.5 1.4 %shard_map.86 = (f32[16,512]{1,0:T(8,128)S(1)}, f32[16,128]{1,0:T(8,128)S(1)}) custom-call(bf16[4,4,8192]{2,1,0:T(4,128)(2,1)S(1)} %bitcast.9, f32[1,8192]{1,0:T(1,128)S(1)} %bitcast.14, f32[1,8192]{1,0:T(1,128)S(1)} %bitcast.19, bf16[8192,512]{1,0:T(8,128)(2,1)S(1)} %copy-done, f32[8,128]{1,0:T(8,128)S(1)} %shard_map.85._), custom_call_target="tpu_custom_call" | custom-call | tf_op jit(solution)/shard_map/pallas_call | solution.py:24
  7.9 0.0 collective-permute-done.refs_0_
  7.9 2.7 %collective-permute-done.1.refs_1_ = bf16[4,4,512]{2,1,0:T(4,128)(2,1)S(1)} collective-permute-done((bf16[4,4,512]{2,1,0:T(4,128)(2,1)}, bf16[4,4,512]{2,1,0:T(4,128)(2,1)S(1)}, u32[]{:S(2)}, u32[]{:S(2)}) %collective-permute-start.1) | collective-permute-done | bytes 16416 | tf_op jit(solution)/shard_map/ppermute | solution.py:20
  10.6 0.0 collective-permute-done.2.refs_2_
  10.6 0.0 copy-done.4
  10.6 0.0 copy-done.5
  10.6 1.2 %shard_map.87 = (f32[4,4,512]{2,1,0:T(4,128)S(1)}, f32[16,128]{1,0:T(8,128)S(1)}, bf16[16,512]{1,0:T(8,128)(2,1)S(1)}, f32[16,4480]{1,0:T(8,128)S(1)}) custom-call(s32[1,4]{1,0:T(1,128)S(1)} %bitcast.27, f32[16,512]{1,0:T(8,128)S(1)} %get-tuple-element.24.projected_ref, bf16[8192,512]{1,0:T(8,128)(2,1)S(1)} %copy-done, bf16[4,4,8192]{2,1,0:T(4,128)(2,1)S(1)} %bitcast.10, ...), custom_call_target="tpu_custom_call" | custom-call | tf_op jit(solution)/shard_map/pallas_call | solution.py:24
  11.9 0.1 collective-permute-start.3
  12.0 1.2 %shard_map.88 = (f32[16,4096]{1,0:T(8,128)S(1)}, f32[32,128]{1,0:T(8,128)S(1)}) custom-call(bf16[16,512]{1,0:T(8,128)(2,1)S(1)} %get-tuple-element.27.lhs_ref, bf16[8192,512]{1,0:T(8,128)(2,1)S(1)} %copy-done, bf16[4,4,8192]{2,1,0:T(4,128)(2,1)S(1)} %bitcast.11, f32[1,8192]{1,0:T(1,128)S(1)} %bitcast.16, f32[1,8192]{1,0:T(1,128)S(1)} %bitcast.21, ...), custom_call_target="tpu_custom_call" | custom-call | tf_op jit(solution)/shard_map/pallas_call | solution.py:24
  13.2 0.3 %collective-permute-done.3.got_ref = f32[16,4480]{1,0:T(8,128)S(1)} collective-permute-done((f32[16,4480]{1,0:T(8,128)S(1)}, f32[16,4480]{1,0:T(8,128)S(1)}, u32[]{:S(2)}, u32[]{:S(2)}) %collective-permute-start.3) | collective-permute-done | bytes 286752 | tf_op jit(solution)/shard_map/ppermute | solution.py:20
  13.5 0.1 shard_map.89
  13.6 1.3 %collective-permute-start.4 = (bf16[16,2560]{1,0:T(8,128)(2,1)S(1)}, bf16[16,2560]{1,0:T(8,128)(2,1)S(1)}, u32[]{:S(2)}, u32[]{:S(2)}) collective-permute-start(bf16[16,2560]{1,0:T(8,128)(2,1)S(1)} %get-tuple-element.34), channel_id=1, source_target_pairs={{0,3},{1,2},{2,1},{3,0},{4,7},{5,6},{6,5},{7,4},{8,11},{9,10},{10,... | collective-permute-start | bytes 245768 | tf_op jit(solution)/shard_map/ppermute | solution.py:20
  15.0 1.4 %collective-permute-start.5 = (f32[16,128]{1,0:T(8,128)S(1)}, f32[16,128]{1,0:T(8,128)S(1)}, u32[]{:S(2)}, u32[]{:S(2)}) collective-permute-start(f32[16,128]{1,0:T(8,128)S(1)} %get-tuple-element.35), channel_id=1, source_target_pairs={{0,7},{1,6},{2,5},{3,4},{4,3},{5,2},{6,1},{7,0},{8,15},{9,14},{10,... | collective-permute-start | bytes 24584 | tf_op jit(solution)/shard_map/ppermute | solution.py:20
  16.3 0.5 %collective-permute-start.6 = (f32[16,128]{1,0:T(8,128)S(1)}, f32[16,128]{1,0:T(8,128)S(1)}, u32[]{:S(2)}, u32[]{:S(2)}) collective-permute-start(f32[16,128]{1,0:T(8,128)S(1)} %get-tuple-element.33.sum_ref), channel_id=1, source_target_pairs={{0,4},{1,5},{2,6},{3,7},{4,0},{5,1},{6,2},{7,3},{8,12},{9,13},{10,... | collective-permute-start | bytes 24584 | tf_op jit(solution)/shard_map/ppermute | solution.py:20
  16.8 2.1 %collective-permute-done.5.refs_1_ = f32[16,128]{1,0:T(8,128)S(1)} collective-permute-done((f32[16,128]{1,0:T(8,128)S(1)}, f32[16,128]{1,0:T(8,128)S(1)}, u32[]{:S(2)}, u32[]{:S(2)}) %collective-permute-start.5) | collective-permute-done | bytes 8224 | tf_op jit(solution)/shard_map/ppermute | solution.py:20
  18.9 1.0 %collective-permute-done.6.refs_2_ = f32[16,128]{1,0:T(8,128)S(1)} collective-permute-done((f32[16,128]{1,0:T(8,128)S(1)}, f32[16,128]{1,0:T(8,128)S(1)}, u32[]{:S(2)}, u32[]{:S(2)}) %collective-permute-start.6) | collective-permute-done | bytes 8224 | tf_op jit(solution)/shard_map/ppermute | solution.py:20
  20.0 0.0 collective-permute-done.4.refs_0_
  20.0 0.2 shard_map.90
  20.1 1.6 %collective-permute-start.7 = (f32[32,128]{1,0:T(8,128)S(1)}, f32[32,128]{1,0:T(8,128)S(1)}, u32[]{:S(2)}, u32[]{:S(2)}) collective-permute-start(f32[32,128]{1,0:T(8,128)S(1)} %get-tuple-element.37), channel_id=1, source_target_pairs={{0,24},{8,16},{16,8},{24,0},{1,25},{9,17},{17,9},{25,1},{2,26},{10... | collective-permute-start | bytes 49160 | tf_op jit(solution)/shard_map/ppermute | solution.py:20
  21.7 0.6 %collective-permute-start.8 = (f32[32,128]{1,0:T(8,128)S(1)}, f32[32,128]{1,0:T(8,128)S(1)}, u32[]{:S(2)}, u32[]{:S(2)}) collective-permute-start(f32[32,128]{1,0:T(8,128)S(1)} %get-tuple-element.38), channel_id=1, source_target_pairs={{0,16},{8,24},{16,0},{24,8},{1,17},{9,25},{17,1},{25,9},{2,18},{10... | collective-permute-start | bytes 49160 | tf_op jit(solution)/shard_map/ppermute | solution.py:20
  22.3 2.3 %collective-permute-start.9 = (f32[32,128]{1,0:T(8,128)S(1)}, f32[32,128]{1,0:T(8,128)S(1)}, u32[]{:S(2)}, u32[]{:S(2)}) collective-permute-start(f32[32,128]{1,0:T(8,128)S(1)} %get-tuple-element.39), channel_id=1, source_target_pairs={{0,8},{8,0},{16,24},{24,16},{1,9},{9,1},{17,25},{25,17},{2,10},{10... | collective-permute-start | bytes 49160 | tf_op jit(solution)/shard_map/ppermute | solution.py:20
  24.6 0.6 %shard_map.92 = bf16[4,4,2048]{2,1,0:T(4,128)(2,1)} custom-call(f32[16,2048]{1,0:T(8,128)S(1)} %get-tuple-element.41.grad_ref), custom_call_target="tpu_custom_call" | custom-call | tf_op jit(solution)/shard_map/pallas_call | solution.py:24
  25.2 0.5 %collective-permute-done.7.refs_0_ = f32[32,128]{1,0:T(8,128)S(1)} collective-permute-done((f32[32,128]{1,0:T(8,128)S(1)}, f32[32,128]{1,0:T(8,128)S(1)}, u32[]{:S(2)}, u32[]{:S(2)}) %collective-permute-start.7) | collective-permute-done | bytes 16416 | tf_op jit(solution)/shard_map/ppermute | solution.py:20
  25.8 0.7 %collective-permute-done.8.refs_1_ = f32[32,128]{1,0:T(8,128)S(1)} collective-permute-done((f32[32,128]{1,0:T(8,128)S(1)}, f32[32,128]{1,0:T(8,128)S(1)}, u32[]{:S(2)}, u32[]{:S(2)}) %collective-permute-start.8) | collective-permute-done | bytes 16416 | tf_op jit(solution)/shard_map/ppermute | solution.py:20
  26.5 0.0 collective-permute-done.9.refs_2_
  26.5 0.6 %shard_map.91 = (f32[16,128]{1,0:T(8,128)}, bf16[4,4,512]{2,1,0:T(4,128)(2,1)}) custom-call(f32[16,128]{1,0:T(8,128)S(1)} %get-tuple-element.36.total_ref, f32[4,4,512]{2,1,0:T(4,128)S(1)} %get-tuple-element.25.kv_ref, f32[32,128]{1,0:T(8,128)S(1)} %collective-permute-done.7.refs_0_, f32[32,128]{1,0:T(8,128)S(1)} %collective-permute-done.8.refs_1_, ...), custom_call_target="tpu_custom_call" | custom-call | tf_op jit(solution)/shard_map/pallas_call | solution.py:24
  (1 shorter events, 0.0 us)
Async XLA Ops:
  0.6 5.8 %copy-start.1 = (bf16[1,1,4,4,8192]{4,3,2,1,0:T(4,128)(2,1)S(1)}, bf16[1,1,4,4,8192]{4,3,2,1,0:T(4,128)(2,1)}, u32[]{:S(2)}) copy-start(bf16[1,1,4,4,8192]{4,3,2,1,0:T(4,128)(2,1)} %param.6) | copy-start | bytes 786436
  0.6 5.8 %copy-start.2 = (f32[8192]{0:T(1024)S(1)}, f32[8192]{0:T(1024)}, u32[]{:S(2)}) copy-start(f32[8192]{0:T(1024)} %param.8) | copy-start | bytes 98308
  0.7 5.8 %copy-start.3 = (f32[8192]{0:T(1024)S(1)}, f32[8192]{0:T(1024)}, u32[]{:S(2)}) copy-start(f32[8192]{0:T(1024)} %param.9) | copy-start | bytes 98308
  0.7 5.8 %copy-start = (bf16[8192,512]{1,0:T(8,128)(2,1)S(1)}, bf16[8192,512]{1,0:T(8,128)(2,1)}, u32[]{:S(2)}) copy-start(bf16[8192,512]{1,0:T(8,128)(2,1)} %weight_ref.5) | copy-start | bytes 25165828
  0.7 7.2 %collective-permute-start = (bf16[4,4,512]{2,1,0:T(4,128)(2,1)}, bf16[4,4,512]{2,1,0:T(4,128)(2,1)S(1)}, u32[]{:S(2)}, u32[]{:S(2)}) collective-permute-start(bf16[4,4,512]{2,1,0:T(4,128)(2,1)} %bitcast.23), channel_id=1, source_target_pairs={{0,24},{8,16},{16,8},{24,0},{1,25},{9,17},{17,9},{25,1},{2,26},{10... | collective-permute-start | bytes 49160 | tf_op jit(solution)/shard_map/ppermute | solution.py:20
  5.8 4.8 %collective-permute-start.1 = (bf16[4,4,512]{2,1,0:T(4,128)(2,1)}, bf16[4,4,512]{2,1,0:T(4,128)(2,1)S(1)}, u32[]{:S(2)}, u32[]{:S(2)}) collective-permute-start(bf16[4,4,512]{2,1,0:T(4,128)(2,1)} %bitcast.24), channel_id=1, source_target_pairs={{0,16},{8,24},{16,0},{24,8},{1,17},{9,25},{17,1},{25,9},{2,18},{10... | collective-permute-start | bytes 49160 | tf_op jit(solution)/shard_map/ppermute | solution.py:20
  5.8 4.8 %collective-permute-start.2 = (bf16[4,4,512]{2,1,0:T(4,128)(2,1)}, bf16[4,4,512]{2,1,0:T(4,128)(2,1)S(1)}, u32[]{:S(2)}, u32[]{:S(2)}) collective-permute-start(bf16[4,4,512]{2,1,0:T(4,128)(2,1)} %bitcast.25), channel_id=1, source_target_pairs={{0,8},{8,0},{16,24},{24,16},{1,9},{9,1},{17,25},{25,17},{2,10},{10... | collective-permute-start | bytes 49160 | tf_op jit(solution)/shard_map/ppermute | solution.py:20
  6.4 4.2 %copy-start.4 = (bf16[1,1,4,4,512]{4,3,2,1,0:T(4,128)(2,1)S(1)}, bf16[1,1,4,4,512]{4,3,2,1,0:T(4,128)(2,1)}, u32[]{:S(2)}) copy-start(bf16[1,1,4,4,512]{4,3,2,1,0:T(4,128)(2,1)} %param.11) | copy-start | bytes 49156
  6.4 4.2 %copy-start.5 = (s32[1,1,4]{2,1,0:T(1,128)S(1)}, s32[1,1,4]{2,1,0:T(1,128)}, u32[]{:S(2)}) copy-start(s32[1,1,4]{2,1,0:T(1,128)} %param.7) | copy-start | bytes 52
  11.9 1.6 %collective-permute-start.3 = (f32[16,4480]{1,0:T(8,128)S(1)}, f32[16,4480]{1,0:T(8,128)S(1)}, u32[]{:S(2)}, u32[]{:S(2)}) collective-permute-start(f32[16,4480]{1,0:T(8,128)S(1)} %get-tuple-element.26), channel_id=1, source_target_pairs={{0,1},{1,0},{2,3},{3,2},{4,5},{5,4},{6,7},{7,6},{8,9},{9,8},{10,11... | collective-permute-start | bytes 860168 | tf_op jit(solution)/shard_map/ppermute | solution.py:20
  13.6 6.3 %collective-permute-start.4 = (bf16[16,2560]{1,0:T(8,128)(2,1)S(1)}, bf16[16,2560]{1,0:T(8,128)(2,1)S(1)}, u32[]{:S(2)}, u32[]{:S(2)}) collective-permute-start(bf16[16,2560]{1,0:T(8,128)(2,1)S(1)} %get-tuple-element.34), channel_id=1, source_target_pairs={{0,3},{1,2},{2,1},{3,0},{4,7},{5,6},{6,5},{7,4},{8,11},{9,10},{10,... | collective-permute-start | bytes 245768 | tf_op jit(solution)/shard_map/ppermute | solution.py:20
  15.0 4.0 %collective-permute-start.5 = (f32[16,128]{1,0:T(8,128)S(1)}, f32[16,128]{1,0:T(8,128)S(1)}, u32[]{:S(2)}, u32[]{:S(2)}) collective-permute-start(f32[16,128]{1,0:T(8,128)S(1)} %get-tuple-element.35), channel_id=1, source_target_pairs={{0,7},{1,6},{2,5},{3,4},{4,3},{5,2},{6,1},{7,0},{8,15},{9,14},{10,... | collective-permute-start | bytes 24584 | tf_op jit(solution)/shard_map/ppermute | solution.py:20
  16.3 3.7 %collective-permute-start.6 = (f32[16,128]{1,0:T(8,128)S(1)}, f32[16,128]{1,0:T(8,128)S(1)}, u32[]{:S(2)}, u32[]{:S(2)}) collective-permute-start(f32[16,128]{1,0:T(8,128)S(1)} %get-tuple-element.33.sum_ref), channel_id=1, source_target_pairs={{0,4},{1,5},{2,6},{3,7},{4,0},{5,1},{6,2},{7,3},{8,12},{9,13},{10,... | collective-permute-start | bytes 24584 | tf_op jit(solution)/shard_map/ppermute | solution.py:20
  20.1 5.6 %collective-permute-start.7 = (f32[32,128]{1,0:T(8,128)S(1)}, f32[32,128]{1,0:T(8,128)S(1)}, u32[]{:S(2)}, u32[]{:S(2)}) collective-permute-start(f32[32,128]{1,0:T(8,128)S(1)} %get-tuple-element.37), channel_id=1, source_target_pairs={{0,24},{8,16},{16,8},{24,0},{1,25},{9,17},{17,9},{25,1},{2,26},{10... | collective-permute-start | bytes 49160 | tf_op jit(solution)/shard_map/ppermute | solution.py:20
  21.7 4.7 %collective-permute-start.8 = (f32[32,128]{1,0:T(8,128)S(1)}, f32[32,128]{1,0:T(8,128)S(1)}, u32[]{:S(2)}, u32[]{:S(2)}) collective-permute-start(f32[32,128]{1,0:T(8,128)S(1)} %get-tuple-element.38), channel_id=1, source_target_pairs={{0,16},{8,24},{16,0},{24,8},{1,17},{9,25},{17,1},{25,9},{2,18},{10... | collective-permute-start | bytes 49160 | tf_op jit(solution)/shard_map/ppermute | solution.py:20
  22.3 4.2 %collective-permute-start.9 = (f32[32,128]{1,0:T(8,128)S(1)}, f32[32,128]{1,0:T(8,128)S(1)}, u32[]{:S(2)}, u32[]{:S(2)}) collective-permute-start(f32[32,128]{1,0:T(8,128)S(1)} %get-tuple-element.39), channel_id=1, source_target_pairs={{0,8},{8,0},{16,24},{24,16},{1,9},{9,1},{17,25},{25,17},{2,10},{10... | collective-permute-start | bytes 49160 | tf_op jit(solution)/shard_map/ppermute | solution.py:20

commit v8 on v7

--- a/solution.py
+++ b/solution.py
@@ -9,6 +9,7 @@
 
 LANES = 128
 PIECES = 3
+TERMS = 2
 VMEM = pl.BlockSpec(memory_space=pltpu.VMEM)
 HBM = pl.BlockSpec(memory_space=pltpu.HBM)
 F32 = jnp.float32
@@ -126,7 +127,6 @@
     kv_ref, dots_ref, lhs_ref, send_ref, sums_ref = refs[enc:]
     buckets, capacity, columns = kv_ref.shape
     me = lax.axis_index("enc")
-    cots = cots[::-1]
     slot = lax.broadcasted_iota(jnp.int32, (capacity, columns), 0)
     blocks = [cot[me].astype(F32) for cot in cots]
     parts = []
@@ -180,8 +180,11 @@
         lines = sums[j * chunks : (j + 1) * chunks]
         totals[j][...] = lines
         if j:
-            sends[j - 1][:, :width] = term.astype(BF16)
-            put_side(sends[j - 1], width, dots, lines)
+            for i in range(TERMS):
+                piece = term.astype(BF16)
+                sends[j - 1][:, i * width : (i + 1) * width] = piece
+                term = term - piece.astype(F32)
+            put_side(sends[j - 1], TERMS * width, dots, lines)
         else:
             own_ref[...] = term
 
@@ -200,7 +203,7 @@
     for got in sums:
         total = total + got[...]
     for got in gots:
-        total = total + get_lines(got, width, chunks)
+        total = total + get_lines(got, TERMS * width, chunks)
     total_ref[...] = total
     for k in range(1, enc):
         sends[k - 1][:chunks, :] = total
@@ -214,8 +217,9 @@
         )
     grad_normed, row_dot = own_ref[...], dots_ref[:, :1]
     for got in gots:
-        grad_normed = grad_normed + got[:, :width].astype(F32)
-        row_dot = row_dot + get_dots(got, width)
+        for i in range(TERMS):
+            grad_normed = grad_normed + got[:, i * width : (i + 1) * width].astype(F32)
+        row_dot = row_dot + get_dots(got, TERMS * width)
     inv_rms = inv_ref[:, :1]
     grad_ref[...] = (
         inv_rms * gain_ref[:, own] * grad_normed
@@ -280,7 +284,7 @@
             struct((rows, columns), BF16),
             struct((rows, half + side(pairs * chunks, rows, F32)), F32),
         ),
-        (counts[0], projected, kv_weight, vis, bias, gain, inv_rms, *cots[::-1]),
+        (counts[0], projected, kv_weight, vis, bias, gain, inv_rms, *cots),
         scratch=[pltpu.VMEM((pairs * chunks, LANES), F32)],
     )
     got = swap(send, "tp", 1)
@@ -294,7 +298,7 @@
         (
             struct((rows, LANES), F32),
             struct((rows, width), F32),
-            *[struct((rows, width + side(chunks, rows, BF16)), BF16)] * (pairs - 1),
+            *[struct((rows, TERMS * width + side(chunks, rows, BF16)), BF16)] * (pairs - 1),
             *[struct((chunks, LANES), F32)] * pairs,
         ),
         (got, terms, dots, sums),

time: 27.3 us -> 27.3 us (level)
  transfers between devices with their start and end apart: 10 -> 10, of which waited for: 6 -> 7; matrix products, arithmetic and copies ran while one was open for 0% -> 0% of each run, Pallas kernels for 12% -> 12%
where the time goes in v8:
time: 27.3 us; the launch traced here: 27.1 us
  starting transfers between devices  13.5 us (49%)
  waiting for transfers between devices  7.4 us (27%)
  Pallas kernels  5.46 us (20%)
  between operations  0.73 us (3%)
    ppermute x10, starting transfers between devices, swap(): return lax.ppermute(x, axis, [(i, i ^ k) for i in range(n)])  13.5 us
    ppermute x10, waiting for transfers between devices, swap(): return lax.ppermute(x, axis, [(i, i ^ k) for i in range(n)])  7.4 us
    pallas_call x8, Pallas kernels, call(): pl.pallas_call(kernel, out_shape=tuple(outs), in_specs=specs or [VMEM] *...  5.46 us
  transfers between devices with their start and end apart: 10, of which 7 were waited for; matrix products, arithmetic and copies ran while one was open for 0% of the time, Pallas kernels for 12%

profile of v8, /device:TPU:0, one launch (start us, length us, event | category | flops | bytes accessed | tf_op | source)
XLA Modules:
  0.0 27.1 jit_solution(12294623675503726524)
XLA Ops:
  0.6 0.0 copy-start
  0.6 0.0 copy-start.3
  0.7 0.0 copy-start.2
  0.7 0.0 copy-start.1
  0.7 5.1 %collective-permute-start.2 = (bf16[4,4,512]{2,1,0:T(4,128)(2,1)}, bf16[4,4,512]{2,1,0:T(4,128)(2,1)S(1)}, u32[]{:S(2)}, u32[]{:S(2)}) collective-permute-start(bf16[4,4,512]{2,1,0:T(4,128)(2,1)} %bitcast.23), channel_id=1, source_target_pairs={{0,24},{8,16},{16,8},{24,0},{1,25},{9,17},{17,9},{25,1},{2,26},{10... | collective-permute-start | bytes 49160 | tf_op jit(solution)/shard_map/ppermute | solution.py:21
  5.8 0.0 collective-permute-start.1
  5.8 0.6 %collective-permute-start = (bf16[4,4,512]{2,1,0:T(4,128)(2,1)}, bf16[4,4,512]{2,1,0:T(4,128)(2,1)S(1)}, u32[]{:S(2)}, u32[]{:S(2)}) collective-permute-start(bf16[4,4,512]{2,1,0:T(4,128)(2,1)} %bitcast.25), channel_id=1, source_target_pairs={{0,8},{8,0},{16,24},{24,16},{1,9},{9,1},{17,25},{25,17},{2,10},{10... | collective-permute-start | bytes 49160 | tf_op jit(solution)/shard_map/ppermute | solution.py:21
  6.4 0.0 copy-start.4
  6.4 0.0 copy-start.5
  6.4 0.0 copy-done
  6.4 0.0 copy-done.3
  6.5 0.0 copy-done.2
  6.5 0.0 copy-done.1
  6.5 1.4 %shard_map.86 = (f32[16,512]{1,0:T(8,128)S(1)}, f32[16,128]{1,0:T(8,128)S(1)}) custom-call(bf16[4,4,8192]{2,1,0:T(4,128)(2,1)S(1)} %bitcast.9, f32[1,8192]{1,0:T(1,128)S(1)} %bitcast.14, f32[1,8192]{1,0:T(1,128)S(1)} %bitcast.19, bf16[8192,512]{1,0:T(8,128)(2,1)S(1)} %copy-done, f32[8,128]{1,0:T(8,128)S(1)} %shard_map.85._), custom_call_target="tpu_custom_call" | custom-call | tf_op jit(solution)/shard_map/pallas_call | solution.py:25
  7.9 0.0 collective-permute-done.2.refs_3_
  7.9 2.7 %collective-permute-done.1.refs_2_ = bf16[4,4,512]{2,1,0:T(4,128)(2,1)S(1)} collective-permute-done((bf16[4,4,512]{2,1,0:T(4,128)(2,1)}, bf16[4,4,512]{2,1,0:T(4,128)(2,1)S(1)}, u32[]{:S(2)}, u32[]{:S(2)}) %collective-permute-start.1) | collective-permute-done | bytes 16416 | tf_op jit(solution)/shard_map/ppermute | solution.py:21
  10.6 0.0 collective-permute-done.refs_1_
  10.6 0.0 copy-done.4
  10.6 0.0 copy-done.5
  10.6 1.2 %shard_map.87 = (f32[4,4,512]{2,1,0:T(4,128)S(1)}, f32[16,128]{1,0:T(8,128)S(1)}, bf16[16,512]{1,0:T(8,128)(2,1)S(1)}, f32[16,4480]{1,0:T(8,128)S(1)}) custom-call(s32[1,4]{1,0:T(1,128)S(1)} %bitcast.27, f32[16,512]{1,0:T(8,128)S(1)} %get-tuple-element.24.projected_ref, bf16[8192,512]{1,0:T(8,128)(2,1)S(1)} %copy-done, bf16[4,4,8192]{2,1,0:T(4,128)(2,1)S(1)} %bitcast.10, ...), custom_call_target="tpu_custom_call" | custom-call | tf_op jit(solution)/shard_map/pallas_call | solution.py:25
  11.9 0.1 collective-permute-start.3
  12.0 1.2 %shard_map.88 = (f32[16,4096]{1,0:T(8,128)S(1)}, f32[32,128]{1,0:T(8,128)S(1)}) custom-call(bf16[16,512]{1,0:T(8,128)(2,1)S(1)} %get-tuple-element.27.lhs_ref, bf16[8192,512]{1,0:T(8,128)(2,1)S(1)} %copy-done, bf16[4,4,8192]{2,1,0:T(4,128)(2,1)S(1)} %bitcast.11, f32[1,8192]{1,0:T(1,128)S(1)} %bitcast.16, f32[1,8192]{1,0:T(1,128)S(1)} %bitcast.21, ...), custom_call_target="tpu_custom_call" | custom-call | tf_op jit(solution)/shard_map/pallas_call | solution.py:25
  13.2 0.3 %collective-permute-done.3.got_ref = f32[16,4480]{1,0:T(8,128)S(1)} collective-permute-done((f32[16,4480]{1,0:T(8,128)S(1)}, f32[16,4480]{1,0:T(8,128)S(1)}, u32[]{:S(2)}, u32[]{:S(2)}) %collective-permute-start.3) | collective-permute-done | bytes 286752 | tf_op jit(solution)/shard_map/ppermute | solution.py:21
  13.5 0.1 shard_map.89
  13.6 1.3 %collective-permute-start.4 = (bf16[16,4608]{1,0:T(8,128)(2,1)S(1)}, bf16[16,4608]{1,0:T(8,128)(2,1)S(1)}, u32[]{:S(2)}, u32[]{:S(2)}) collective-permute-start(bf16[16,4608]{1,0:T(8,128)(2,1)S(1)} %get-tuple-element.34), channel_id=1, source_target_pairs={{0,3},{1,2},{2,1},{3,0},{4,7},{5,6},{6,5},{7,4},{8,11},{9,10},{10,... | collective-permute-start | bytes 442376 | tf_op jit(solution)/shard_map/ppermute | solution.py:21
  15.0 1.4 %collective-permute-start.5 = (f32[16,128]{1,0:T(8,128)S(1)}, f32[16,128]{1,0:T(8,128)S(1)}, u32[]{:S(2)}, u32[]{:S(2)}) collective-permute-start(f32[16,128]{1,0:T(8,128)S(1)} %get-tuple-element.35), channel_id=1, source_target_pairs={{0,7},{1,6},{2,5},{3,4},{4,3},{5,2},{6,1},{7,0},{8,15},{9,14},{10,... | collective-permute-start | bytes 24584 | tf_op jit(solution)/shard_map/ppermute | solution.py:21
  16.3 0.5 %collective-permute-start.6 = (f32[16,128]{1,0:T(8,128)S(1)}, f32[16,128]{1,0:T(8,128)S(1)}, u32[]{:S(2)}, u32[]{:S(2)}) collective-permute-start(f32[16,128]{1,0:T(8,128)S(1)} %get-tuple-element.33.sum_ref), channel_id=1, source_target_pairs={{0,4},{1,5},{2,6},{3,7},{4,0},{5,1},{6,2},{7,3},{8,12},{9,13},{10,... | collective-permute-start | bytes 24584 | tf_op jit(solution)/shard_map/ppermute | solution.py:21
  16.9 2.2 %collective-permute-done.5.refs_1_ = f32[16,128]{1,0:T(8,128)S(1)} collective-permute-done((f32[16,128]{1,0:T(8,128)S(1)}, f32[16,128]{1,0:T(8,128)S(1)}, u32[]{:S(2)}, u32[]{:S(2)}) %collective-permute-start.5) | collective-permute-done | bytes 8224 | tf_op jit(solution)/shard_map/ppermute | solution.py:21
  19.0 0.9 %collective-permute-done.6.refs_2_ = f32[16,128]{1,0:T(8,128)S(1)} collective-permute-done((f32[16,128]{1,0:T(8,128)S(1)}, f32[16,128]{1,0:T(8,128)S(1)}, u32[]{:S(2)}, u32[]{:S(2)}) %collective-permute-start.6) | collective-permute-done | bytes 8224 | tf_op jit(solution)/shard_map/ppermute | solution.py:21
  20.0 0.0 collective-permute-done.4.refs_0_
  20.0 0.2 shard_map.90
  20.2 1.6 %collective-permute-start.7 = (f32[32,128]{1,0:T(8,128)S(1)}, f32[32,128]{1,0:T(8,128)S(1)}, u32[]{:S(2)}, u32[]{:S(2)}) collective-permute-start(f32[32,128]{1,0:T(8,128)S(1)} %get-tuple-element.37), channel_id=1, source_target_pairs={{0,24},{8,16},{16,8},{24,0},{1,25},{9,17},{17,9},{25,1},{2,26},{10... | collective-permute-start | bytes 49160 | tf_op jit(solution)/shard_map/ppermute | solution.py:21
  21.7 0.6 %collective-permute-start.8 = (f32[32,128]{1,0:T(8,128)S(1)}, f32[32,128]{1,0:T(8,128)S(1)}, u32[]{:S(2)}, u32[]{:S(2)}) collective-permute-start(f32[32,128]{1,0:T(8,128)S(1)} %get-tuple-element.38), channel_id=1, source_target_pairs={{0,16},{8,24},{16,0},{24,8},{1,17},{9,25},{17,1},{25,9},{2,18},{10... | collective-permute-start | bytes 49160 | tf_op jit(solution)/shard_map/ppermute | solution.py:21
  22.3 2.3 %collective-permute-start.9 = (f32[32,128]{1,0:T(8,128)S(1)}, f32[32,128]{1,0:T(8,128)S(1)}, u32[]{:S(2)}, u32[]{:S(2)}) collective-permute-start(f32[32,128]{1,0:T(8,128)S(1)} %get-tuple-element.39), channel_id=1, source_target_pairs={{0,8},{8,0},{16,24},{24,16},{1,9},{9,1},{17,25},{25,17},{2,10},{10... | collective-permute-start | bytes 49160 | tf_op jit(solution)/shard_map/ppermute | solution.py:21
  24.6 0.6 %shard_map.92 = bf16[4,4,2048]{2,1,0:T(4,128)(2,1)} custom-call(f32[16,2048]{1,0:T(8,128)S(1)} %get-tuple-element.41.grad_ref), custom_call_target="tpu_custom_call" | custom-call | tf_op jit(solution)/shard_map/pallas_call | solution.py:25
  25.3 0.7 %collective-permute-done.7.refs_0_ = f32[32,128]{1,0:T(8,128)S(1)} collective-permute-done((f32[32,128]{1,0:T(8,128)S(1)}, f32[32,128]{1,0:T(8,128)S(1)}, u32[]{:S(2)}, u32[]{:S(2)}) %collective-permute-start.7) | collective-permute-done | bytes 16416 | tf_op jit(solution)/shard_map/ppermute | solution.py:21
  25.9 0.5 %collective-permute-done.8.refs_1_ = f32[32,128]{1,0:T(8,128)S(1)} collective-permute-done((f32[32,128]{1,0:T(8,128)S(1)}, f32[32,128]{1,0:T(8,128)S(1)}, u32[]{:S(2)}, u32[]{:S(2)}) %collective-permute-start.8) | collective-permute-done | bytes 16416 | tf_op jit(solution)/shard_map/ppermute | solution.py:21
  26.4 0.1 collective-permute-done.9.refs_2_
  26.5 0.6 %shard_map.91 = (f32[16,128]{1,0:T(8,128)}, bf16[4,4,512]{2,1,0:T(4,128)(2,1)}) custom-call(f32[16,128]{1,0:T(8,128)S(1)} %get-tuple-element.36.total_ref, f32[4,4,512]{2,1,0:T(4,128)S(1)} %get-tuple-element.25.kv_ref, f32[32,128]{1,0:T(8,128)S(1)} %collective-permute-done.7.refs_0_, f32[32,128]{1,0:T(8,128)S(1)} %collective-permute-done.8.refs_1_, ...), custom_call_target="tpu_custom_call" | custom-call | tf_op jit(solution)/shard_map/pallas_call | solution.py:25
  (1 shorter events, 0.0 us)
Async XLA Ops:
  0.6 5.8 %copy-start = (bf16[8192,512]{1,0:T(8,128)(2,1)S(1)}, bf16[8192,512]{1,0:T(8,128)(2,1)}, u32[]{:S(2)}) copy-start(bf16[8192,512]{1,0:T(8,128)(2,1)} %weight_ref.5) | copy-start | bytes 25165828
  0.6 5.8 %copy-start.3 = (f32[8192]{0:T(1024)S(1)}, f32[8192]{0:T(1024)}, u32[]{:S(2)}) copy-start(f32[8192]{0:T(1024)} %param.9) | copy-start | bytes 98308
  0.7 5.8 %copy-start.2 = (f32[8192]{0:T(1024)S(1)}, f32[8192]{0:T(1024)}, u32[]{:S(2)}) copy-start(f32[8192]{0:T(1024)} %param.8) | copy-start | bytes 98308
  0.7 5.8 %copy-start.1 = (bf16[1,1,4,4,8192]{4,3,2,1,0:T(4,128)(2,1)S(1)}, bf16[1,1,4,4,8192]{4,3,2,1,0:T(4,128)(2,1)}, u32[]{:S(2)}) copy-start(bf16[1,1,4,4,8192]{4,3,2,1,0:T(4,128)(2,1)} %param.6) | copy-start | bytes 786436
  0.7 7.2 %collective-permute-start.2 = (bf16[4,4,512]{2,1,0:T(4,128)(2,1)}, bf16[4,4,512]{2,1,0:T(4,128)(2,1)S(1)}, u32[]{:S(2)}, u32[]{:S(2)}) collective-permute-start(bf16[4,4,512]{2,1,0:T(4,128)(2,1)} %bitcast.23), channel_id=1, source_target_pairs={{0,24},{8,16},{16,8},{24,0},{1,25},{9,17},{17,9},{25,1},{2,26},{10... | collective-permute-start | bytes 49160 | tf_op jit(solution)/shard_map/ppermute | solution.py:21
  5.8 4.8 %collective-permute-start.1 = (bf16[4,4,512]{2,1,0:T(4,128)(2,1)}, bf16[4,4,512]{2,1,0:T(4,128)(2,1)S(1)}, u32[]{:S(2)}, u32[]{:S(2)}) collective-permute-start(bf16[4,4,512]{2,1,0:T(4,128)(2,1)} %bitcast.24), channel_id=1, source_target_pairs={{0,16},{8,24},{16,0},{24,8},{1,17},{9,25},{17,1},{25,9},{2,18},{10... | collective-permute-start | bytes 49160 | tf_op jit(solution)/shard_map/ppermute | solution.py:21
  5.8 4.8 %collective-permute-start = (bf16[4,4,512]{2,1,0:T(4,128)(2,1)}, bf16[4,4,512]{2,1,0:T(4,128)(2,1)S(1)}, u32[]{:S(2)}, u32[]{:S(2)}) collective-permute-start(bf16[4,4,512]{2,1,0:T(4,128)(2,1)} %bitcast.25), channel_id=1, source_target_pairs={{0,8},{8,0},{16,24},{24,16},{1,9},{9,1},{17,25},{25,17},{2,10},{10... | collective-permute-start | bytes 49160 | tf_op jit(solution)/shard_map/ppermute | solution.py:21
  6.4 4.2 %copy-start.4 = (bf16[1,1,4,4,512]{4,3,2,1,0:T(4,128)(2,1)S(1)}, bf16[1,1,4,4,512]{4,3,2,1,0:T(4,128)(2,1)}, u32[]{:S(2)}) copy-start(bf16[1,1,4,4,512]{4,3,2,1,0:T(4,128)(2,1)} %param.11) | copy-start | bytes 49156
  6.4 4.2 %copy-start.5 = (s32[1,1,4]{2,1,0:T(1,128)S(1)}, s32[1,1,4]{2,1,0:T(1,128)}, u32[]{:S(2)}) copy-start(s32[1,1,4]{2,1,0:T(1,128)} %param.7) | copy-start | bytes 52
  11.9 1.6 %collective-permute-start.3 = (f32[16,4480]{1,0:T(8,128)S(1)}, f32[16,4480]{1,0:T(8,128)S(1)}, u32[]{:S(2)}, u32[]{:S(2)}) collective-permute-start(f32[16,4480]{1,0:T(8,128)S(1)} %get-tuple-element.26), channel_id=1, source_target_pairs={{0,1},{1,0},{2,3},{3,2},{4,5},{5,4},{6,7},{7,6},{8,9},{9,8},{10,11... | collective-permute-start | bytes 860168 | tf_op jit(solution)/shard_map/ppermute | solution.py:21
  13.6 6.4 %collective-permute-start.4 = (bf16[16,4608]{1,0:T(8,128)(2,1)S(1)}, bf16[16,4608]{1,0:T(8,128)(2,1)S(1)}, u32[]{:S(2)}, u32[]{:S(2)}) collective-permute-start(bf16[16,4608]{1,0:T(8,128)(2,1)S(1)} %get-tuple-element.34), channel_id=1, source_target_pairs={{0,3},{1,2},{2,1},{3,0},{4,7},{5,6},{6,5},{7,4},{8,11},{9,10},{10,... | collective-permute-start | bytes 442376 | tf_op jit(solution)/shard_map/ppermute | solution.py:21
  15.0 4.1 %collective-permute-start.5 = (f32[16,128]{1,0:T(8,128)S(1)}, f32[16,128]{1,0:T(8,128)S(1)}, u32[]{:S(2)}, u32[]{:S(2)}) collective-permute-start(f32[16,128]{1,0:T(8,128)S(1)} %get-tuple-element.35), channel_id=1, source_target_pairs={{0,7},{1,6},{2,5},{3,4},{4,3},{5,2},{6,1},{7,0},{8,15},{9,14},{10,... | collective-permute-start | bytes 24584 | tf_op jit(solution)/shard_map/ppermute | solution.py:21
  16.3 3.7 %collective-permute-start.6 = (f32[16,128]{1,0:T(8,128)S(1)}, f32[16,128]{1,0:T(8,128)S(1)}, u32[]{:S(2)}, u32[]{:S(2)}) collective-permute-start(f32[16,128]{1,0:T(8,128)S(1)} %get-tuple-element.33.sum_ref), channel_id=1, source_target_pairs={{0,4},{1,5},{2,6},{3,7},{4,0},{5,1},{6,2},{7,3},{8,12},{9,13},{10,... | collective-permute-start | bytes 24584 | tf_op jit(solution)/shard_map/ppermute | solution.py:21
  20.2 5.8 %collective-permute-start.7 = (f32[32,128]{1,0:T(8,128)S(1)}, f32[32,128]{1,0:T(8,128)S(1)}, u32[]{:S(2)}, u32[]{:S(2)}) collective-permute-start(f32[32,128]{1,0:T(8,128)S(1)} %get-tuple-element.37), channel_id=1, source_target_pairs={{0,24},{8,16},{16,8},{24,0},{1,25},{9,17},{17,9},{25,1},{2,26},{10... | collective-permute-start | bytes 49160 | tf_op jit(solution)/shard_map/ppermute | solution.py:21
  21.7 4.7 %collective-permute-start.8 = (f32[32,128]{1,0:T(8,128)S(1)}, f32[32,128]{1,0:T(8,128)S(1)}, u32[]{:S(2)}, u32[]{:S(2)}) collective-permute-start(f32[32,128]{1,0:T(8,128)S(1)} %get-tuple-element.38), channel_id=1, source_target_pairs={{0,16},{8,24},{16,0},{24,8},{1,17},{9,25},{17,1},{25,9},{2,18},{10... | collective-permute-start | bytes 49160 | tf_op jit(solution)/shard_map/ppermute | solution.py:21
  22.3 4.2 %collective-permute-start.9 = (f32[32,128]{1,0:T(8,128)S(1)}, f32[32,128]{1,0:T(8,128)S(1)}, u32[]{:S(2)}, u32[]{:S(2)}) collective-permute-start(f32[32,128]{1,0:T(8,128)S(1)} %get-tuple-element.39), channel_id=1, source_target_pairs={{0,8},{8,0},{16,24},{24,16},{1,9},{9,1},{17,25},{25,17},{2,10},{10... | collective-permute-start | bytes 49160 | tf_op jit(solution)/shard_map/ppermute | solution.py:21

commit v9 on v8

--- a/solution.py
+++ b/solution.py
@@ -189,21 +189,17 @@
             own_ref[...] = term
 
 
-def combine_kernel(enc, pairs, vis_ref, bias_ref, gain_ref, inv_ref, kv_ref, dots_ref, own_ref, sum_ref, *refs):
+def pack_kernel(enc, pairs, kv_ref, sum_ref, *refs):
     gots, refs = refs[: pairs - 1], refs[pairs - 1 :]
-    sums, refs = refs[: -enc - 2], refs[-enc - 2 :]
-    grad_ref, total_ref = refs[:2]
-    sends, rows_ref = refs[2:-1], refs[-1]
-    buckets, capacity, features = vis_ref.shape
-    width = own_ref.shape[1]
-    chunks = width // LANES
-    me, place = lax.axis_index("enc"), lax.axis_index("tp")
-    own = pl.ds(pl.multiple_of(place * width, width), width)
+    sums, (total_ref, *sends) = refs[:-enc], refs[-enc:]
+    chunks, capacity = sum_ref.shape[0], kv_ref.shape[1]
+    me = lax.axis_index("enc")
     total = sum_ref[...]
     for got in sums:
         total = total + got[...]
     for got in gots:
-        total = total + get_lines(got, TERMS * width, chunks)
+        start = got.shape[1] - side(chunks, got.shape[0], BF16)
+        total = total + get_lines(got, start, chunks)
     total_ref[...] = total
     for k in range(1, enc):
         sends[k - 1][:chunks, :] = total
@@ -211,29 +207,30 @@
         for j in range(block.shape[1] // LANES):
             at = chunks + j * capacity
             sends[k - 1][at : at + capacity, :] = block[:, j * LANES : (j + 1) * LANES]
-    for q in range(buckets):
-        rows_ref[q * capacity : (q + 1) * capacity, :] = (
-            vis_ref[q, :, own].astype(F32) + bias_ref[:, own]
-        )
+
+
+def combine_kernel(vis_ref, bias_ref, gain_ref, inv_ref, dots_ref, own_ref, *refs):
+    gots, (out_ref, token_ref) = refs[:-2], refs[-2:]
+    buckets, capacity, features = vis_ref.shape
+    width = own_ref.shape[1]
+    place = lax.axis_index("tp")
+    own = pl.ds(pl.multiple_of(place * width, width), width)
     grad_normed, row_dot = own_ref[...], dots_ref[:, :1]
     for got in gots:
         for i in range(TERMS):
             grad_normed = grad_normed + got[:, i * width : (i + 1) * width].astype(F32)
         row_dot = row_dot + get_dots(got, TERMS * width)
     inv_rms = inv_ref[:, :1]
-    grad_ref[...] = (
-        inv_rms * gain_ref[:, own] * grad_normed
-        - rows_ref[...] * (inv_rms * inv_rms) * row_dot / features
-    )
-
-
-def round_kernel(grad_ref, out_ref):
-    buckets, capacity, _ = out_ref.shape
+    first = inv_rms * gain_ref[:, own] * grad_normed
+    scale = inv_rms * inv_rms * row_dot * (1.0 / features)
     for q in range(buckets):
-        out_ref[q] = grad_ref[q * capacity : (q + 1) * capacity, :].astype(BF16)
-
-
-def final_kernel(enc, total_ref, kv_ref, *refs):
+        rows = slice(q * capacity, (q + 1) * capacity)
+        inputs = vis_ref[q, :, own].astype(F32) + bias_ref[:, own]
+        out_ref[q] = (first[rows] - inputs * scale[rows]).astype(BF16)
+    token_ref[...] = jnp.zeros(token_ref.shape, F32)
+
+
+def final_kernel(enc, total_ref, kv_ref, _, *refs):
     gots, (sum_ref, out_ref) = refs[: enc - 1][::-1], refs[enc - 1 :]
     buckets, capacity, columns = kv_ref.shape
     chunks = total_ref.shape[0]
@@ -308,22 +305,24 @@
     others = [
         swap(t, ("llm", "tp"), tp * g + kept(j)) for g in range(1, llm) for j, t in enumerate(totals)
     ]
-    grad, total, *sends = run(
-        part(combine_kernel, enc, pairs),
+    total, *sends = run(
+        part(pack_kernel, enc, pairs),
         (
-            struct((rows, width), F32),
             struct((chunks, LANES), F32),
             *[struct((chunks + capacity * columns // LANES, LANES), F32)] * (enc - 1),
         ),
-        (vis, bias, gain, inv_rms, kv, dots, own, totals[0], *gots, *others[::-1]),
-        scratch=[pltpu.VMEM((rows, width), F32)],
+        (kv, totals[0], *gots, *others[::-1]),
+    )
+    visual_grad, token = run(
+        combine_kernel,
+        (struct((buckets, capacity, width), BF16), struct((8, LANES), F32)),
+        (vis, bias, gain, inv_rms, dots, own, *gots),
     )
     gots = [swap(s, "enc", k + 1) for k, s in enumerate(sends)]
-    (visual_grad,) = run(round_kernel, (struct((buckets, capacity, width), BF16),), (grad,))
     bias_grad, key_values = run(
         part(final_kernel, enc),
         (struct((chunks, LANES), F32), struct((buckets, capacity, columns), BF16)),
-        (total, kv, *gots[::-1]),
+        (total, kv, token, *gots[::-1]),
     )
     return (key_values[None, None], visual_grad[None, None], bias_grad.reshape(width))
 

time: 27.3 us -> 27.1 us (level)
  transfers between devices with their start and end apart: 10 -> 10, of which waited for: 7 -> 7; matrix products, arithmetic and copies ran while one was open for 0% -> 0% of each run, Pallas kernels for 12% -> 13%
where the time goes in v9:
time: 27.1 us; the launch traced here: 27 us
  starting transfers between devices  13.5 us (50%)
  waiting for transfers between devices  7.22 us (27%)
  Pallas kernels  5.48 us (20%)
  between operations  0.72 us (3%)
    ppermute x10, starting transfers between devices, swap(): return lax.ppermute(x, axis, [(i, i ^ k) for i in range(n)])  13.5 us
    ppermute x10, waiting for transfers between devices, swap(): return lax.ppermute(x, axis, [(i, i ^ k) for i in range(n)])  7.22 us
    pallas_call x8, Pallas kernels, call(): pl.pallas_call(kernel, out_shape=tuple(outs), in_specs=specs or [VMEM] *...  5.48 us
  transfers between devices with their start and end apart: 10, of which 7 were waited for; matrix products, arithmetic and copies ran while one was open for 0% of the time, Pallas kernels for 13%

profile of v9, /device:TPU:0, one launch (start us, length us, event | category | flops | bytes accessed | tf_op | source)
XLA Modules:
  0.0 27.0 jit_solution(5822548832484353289)
XLA Ops:
  0.6 0.0 copy-start
  0.6 0.0 copy-start.3
  0.7 0.0 copy-start.2
  0.7 0.0 copy-start.1
  0.7 5.1 %collective-permute-start.2 = (bf16[4,4,512]{2,1,0:T(4,128)(2,1)}, bf16[4,4,512]{2,1,0:T(4,128)(2,1)S(1)}, u32[]{:S(2)}, u32[]{:S(2)}) collective-permute-start(bf16[4,4,512]{2,1,0:T(4,128)(2,1)} %bitcast.23), channel_id=1, source_target_pairs={{0,24},{8,16},{16,8},{24,0},{1,25},{9,17},{17,9},{25,1},{2,26},{10... | collective-permute-start | bytes 49160 | tf_op jit(solution)/shard_map/ppermute | solution.py:21
  5.8 0.0 collective-permute-start.1
  5.8 0.6 %collective-permute-start = (bf16[4,4,512]{2,1,0:T(4,128)(2,1)}, bf16[4,4,512]{2,1,0:T(4,128)(2,1)S(1)}, u32[]{:S(2)}, u32[]{:S(2)}) collective-permute-start(bf16[4,4,512]{2,1,0:T(4,128)(2,1)} %bitcast.25), channel_id=1, source_target_pairs={{0,8},{8,0},{16,24},{24,16},{1,9},{9,1},{17,25},{25,17},{2,10},{10... | collective-permute-start | bytes 49160 | tf_op jit(solution)/shard_map/ppermute | solution.py:21
  6.4 0.0 copy-start.4
  6.4 0.0 copy-start.5
  6.4 0.0 copy-done
  6.4 0.0 copy-done.3
  6.5 0.0 copy-done.2
  6.5 0.0 copy-done.1
  6.5 1.4 %shard_map.86 = (f32[16,512]{1,0:T(8,128)S(1)}, f32[16,128]{1,0:T(8,128)S(1)}) custom-call(bf16[4,4,8192]{2,1,0:T(4,128)(2,1)S(1)} %bitcast.9, f32[1,8192]{1,0:T(1,128)S(1)} %bitcast.14, f32[1,8192]{1,0:T(1,128)S(1)} %bitcast.19, bf16[8192,512]{1,0:T(8,128)(2,1)S(1)} %copy-done, f32[8,128]{1,0:T(8,128)S(1)} %shard_map.85._), custom_call_target="tpu_custom_call" | custom-call | tf_op jit(solution)/shard_map/pallas_call | solution.py:25
  7.9 0.0 collective-permute-done.2.refs_3_
  7.9 2.7 %collective-permute-done.1.refs_2_ = bf16[4,4,512]{2,1,0:T(4,128)(2,1)S(1)} collective-permute-done((bf16[4,4,512]{2,1,0:T(4,128)(2,1)}, bf16[4,4,512]{2,1,0:T(4,128)(2,1)S(1)}, u32[]{:S(2)}, u32[]{:S(2)}) %collective-permute-start.1) | collective-permute-done | bytes 16416 | tf_op jit(solution)/shard_map/ppermute | solution.py:21
  10.6 0.0 collective-permute-done.refs_1_
  10.6 0.0 copy-done.4
  10.6 0.0 copy-done.5
  10.6 1.2 %shard_map.87 = (f32[4,4,512]{2,1,0:T(4,128)S(1)}, f32[16,128]{1,0:T(8,128)S(1)}, bf16[16,512]{1,0:T(8,128)(2,1)S(1)}, f32[16,4480]{1,0:T(8,128)S(1)}) custom-call(s32[1,4]{1,0:T(1,128)S(1)} %bitcast.27, f32[16,512]{1,0:T(8,128)S(1)} %get-tuple-element.24.projected_ref, bf16[8192,512]{1,0:T(8,128)(2,1)S(1)} %copy-done, bf16[4,4,8192]{2,1,0:T(4,128)(2,1)S(1)} %bitcast.10, ...), custom_call_target="tpu_custom_call" | custom-call | tf_op jit(solution)/shard_map/pallas_call | solution.py:25
  11.9 0.1 collective-permute-start.3
  12.0 1.2 %shard_map.88 = (f32[16,4096]{1,0:T(8,128)S(1)}, f32[32,128]{1,0:T(8,128)S(1)}) custom-call(bf16[16,512]{1,0:T(8,128)(2,1)S(1)} %get-tuple-element.28.lhs_ref, bf16[8192,512]{1,0:T(8,128)(2,1)S(1)} %copy-done, bf16[4,4,8192]{2,1,0:T(4,128)(2,1)S(1)} %bitcast.11, f32[1,8192]{1,0:T(1,128)S(1)} %bitcast.16, f32[1,8192]{1,0:T(1,128)S(1)} %bitcast.21, ...), custom_call_target="tpu_custom_call" | custom-call | tf_op jit(solution)/shard_map/pallas_call | solution.py:25
  13.2 0.3 %collective-permute-done.3.got_ref = f32[16,4480]{1,0:T(8,128)S(1)} collective-permute-done((f32[16,4480]{1,0:T(8,128)S(1)}, f32[16,4480]{1,0:T(8,128)S(1)}, u32[]{:S(2)}, u32[]{:S(2)}) %collective-permute-start.3) | collective-permute-done | bytes 286752 | tf_op jit(solution)/shard_map/ppermute | solution.py:21
  13.5 0.1 shard_map.89
  13.6 1.3 %collective-permute-start.4 = (bf16[16,4608]{1,0:T(8,128)(2,1)S(1)}, bf16[16,4608]{1,0:T(8,128)(2,1)S(1)}, u32[]{:S(2)}, u32[]{:S(2)}) collective-permute-start(bf16[16,4608]{1,0:T(8,128)(2,1)S(1)} %get-tuple-element.33), channel_id=1, source_target_pairs={{0,3},{1,2},{2,1},{3,0},{4,7},{5,6},{6,5},{7,4},{8,11},{9,10},{10,... | collective-permute-start | bytes 442376 | tf_op jit(solution)/shard_map/ppermute | solution.py:21
  15.0 1.4 %collective-permute-start.5 = (f32[16,128]{1,0:T(8,128)S(1)}, f32[16,128]{1,0:T(8,128)S(1)}, u32[]{:S(2)}, u32[]{:S(2)}) collective-permute-start(f32[16,128]{1,0:T(8,128)S(1)} %get-tuple-element.34), channel_id=1, source_target_pairs={{0,7},{1,6},{2,5},{3,4},{4,3},{5,2},{6,1},{7,0},{8,15},{9,14},{10,... | collective-permute-start | bytes 24584 | tf_op jit(solution)/shard_map/ppermute | solution.py:21
  16.3 0.5 %collective-permute-start.6 = (f32[16,128]{1,0:T(8,128)S(1)}, f32[16,128]{1,0:T(8,128)S(1)}, u32[]{:S(2)}, u32[]{:S(2)}) collective-permute-start(f32[16,128]{1,0:T(8,128)S(1)} %get-tuple-element.32.sum_ref), channel_id=1, source_target_pairs={{0,4},{1,5},{2,6},{3,7},{4,0},{5,1},{6,2},{7,3},{8,12},{9,13},{10,... | collective-permute-start | bytes 24584 | tf_op jit(solution)/shard_map/ppermute | solution.py:21
  16.9 2.2 %collective-permute-done.5.refs_1_ = f32[16,128]{1,0:T(8,128)S(1)} collective-permute-done((f32[16,128]{1,0:T(8,128)S(1)}, f32[16,128]{1,0:T(8,128)S(1)}, u32[]{:S(2)}, u32[]{:S(2)}) %collective-permute-start.5) | collective-permute-done | bytes 8224 | tf_op jit(solution)/shard_map/ppermute | solution.py:21
  19.1 0.9 %collective-permute-done.6.refs_2_ = f32[16,128]{1,0:T(8,128)S(1)} collective-permute-done((f32[16,128]{1,0:T(8,128)S(1)}, f32[16,128]{1,0:T(8,128)S(1)}, u32[]{:S(2)}, u32[]{:S(2)}) %collective-permute-start.6) | collective-permute-done | bytes 8224 | tf_op jit(solution)/shard_map/ppermute | solution.py:21
  20.0 0.0 collective-permute-done.4.refs_0_
  20.0 1.6 %collective-permute-start.7 = (f32[32,128]{1,0:T(8,128)S(1)}, f32[32,128]{1,0:T(8,128)S(1)}, u32[]{:S(2)}, u32[]{:S(2)}) collective-permute-start(f32[32,128]{1,0:T(8,128)S(1)} %get-tuple-element.39), channel_id=1, source_target_pairs={{0,24},{8,16},{16,8},{24,0},{1,25},{9,17},{17,9},{25,1},{2,26},{10... | collective-permute-start | bytes 49160 | tf_op jit(solution)/shard_map/ppermute | solution.py:21
  21.6 0.6 %collective-permute-start.8 = (f32[32,128]{1,0:T(8,128)S(1)}, f32[32,128]{1,0:T(8,128)S(1)}, u32[]{:S(2)}, u32[]{:S(2)}) collective-permute-start(f32[32,128]{1,0:T(8,128)S(1)} %get-tuple-element.40), channel_id=1, source_target_pairs={{0,16},{8,24},{16,0},{24,8},{1,17},{9,25},{17,1},{25,9},{2,18},{10... | collective-permute-start | bytes 49160 | tf_op jit(solution)/shard_map/ppermute | solution.py:21
  22.2 2.3 %collective-permute-start.9 = (f32[32,128]{1,0:T(8,128)S(1)}, f32[32,128]{1,0:T(8,128)S(1)}, u32[]{:S(2)}, u32[]{:S(2)}) collective-permute-start(f32[32,128]{1,0:T(8,128)S(1)} %get-tuple-element.41), channel_id=1, source_target_pairs={{0,8},{8,0},{16,24},{24,16},{1,9},{9,1},{17,25},{25,17},{2,10},{10... | collective-permute-start | bytes 49160 | tf_op jit(solution)/shard_map/ppermute | solution.py:21
  24.5 0.8 %shard_map.91 = (bf16[4,4,2048]{2,1,0:T(4,128)(2,1)}, f32[8,128]{1,0:T(8,128)S(1)}) custom-call(bf16[4,4,8192]{2,1,0:T(4,128)(2,1)S(1)} %bitcast.12, f32[1,8192]{1,0:T(1,128)S(1)} %bitcast.17, f32[1,8192]{1,0:T(1,128)S(1)} %bitcast.22, f32[16,128]{1,0:T(8,128)S(1)} %get-tuple-element.25.inv_ref, f32[16,128]{1,0:T(8,128)S(1)} %get-tuple-element.36.dots_ref, ...), custom_call_target="tpu_custom_call" | custom-call | tf_op jit(solution)/shard_map/pallas_call | solution.py:25
  25.3 0.5 %collective-permute-done.7.refs_0_ = f32[32,128]{1,0:T(8,128)S(1)} collective-permute-done((f32[32,128]{1,0:T(8,128)S(1)}, f32[32,128]{1,0:T(8,128)S(1)}, u32[]{:S(2)}, u32[]{:S(2)}) %collective-permute-start.7) | collective-permute-done | bytes 16416 | tf_op jit(solution)/shard_map/ppermute | solution.py:21
  25.8 0.5 %collective-permute-done.8.refs_1_ = f32[32,128]{1,0:T(8,128)S(1)} collective-permute-done((f32[32,128]{1,0:T(8,128)S(1)}, f32[32,128]{1,0:T(8,128)S(1)}, u32[]{:S(2)}, u32[]{:S(2)}) %collective-permute-start.8) | collective-permute-done | bytes 16416 | tf_op jit(solution)/shard_map/ppermute | solution.py:21
  26.2 0.1 collective-permute-done.9.refs_2_
  26.3 0.6 %shard_map.92 = (f32[16,128]{1,0:T(8,128)}, bf16[4,4,512]{2,1,0:T(4,128)(2,1)}) custom-call(f32[16,128]{1,0:T(8,128)S(1)} %get-tuple-element.35.total_ref, f32[4,4,512]{2,1,0:T(4,128)S(1)} %get-tuple-element.26.kv_ref, f32[8,128]{1,0:T(8,128)S(1)} %get-tuple-element.38._, f32[32,128]{1,0:T(8,128)S(1)} %collective-permute-done.7.refs_0_, ...), custom_call_target="tpu_custom_call" | custom-call | tf_op jit(solution)/shard_map/pallas_call | solution.py:25
  (2 shorter events, 0.0 us)
Async XLA Ops:
  0.6 5.8 %copy-start = (bf16[8192,512]{1,0:T(8,128)(2,1)S(1)}, bf16[8192,512]{1,0:T(8,128)(2,1)}, u32[]{:S(2)}) copy-start(bf16[8192,512]{1,0:T(8,128)(2,1)} %weight_ref.5) | copy-start | bytes 25165828
  0.6 5.8 %copy-start.3 = (f32[8192]{0:T(1024)S(1)}, f32[8192]{0:T(1024)}, u32[]{:S(2)}) copy-start(f32[8192]{0:T(1024)} %param.9) | copy-start | bytes 98308
  0.7 5.8 %copy-start.2 = (f32[8192]{0:T(1024)S(1)}, f32[8192]{0:T(1024)}, u32[]{:S(2)}) copy-start(f32[8192]{0:T(1024)} %param.8) | copy-start | bytes 98308
  0.7 5.8 %copy-start.1 = (bf16[1,1,4,4,8192]{4,3,2,1,0:T(4,128)(2,1)S(1)}, bf16[1,1,4,4,8192]{4,3,2,1,0:T(4,128)(2,1)}, u32[]{:S(2)}) copy-start(bf16[1,1,4,4,8192]{4,3,2,1,0:T(4,128)(2,1)} %param.6) | copy-start | bytes 786436
  0.7 7.2 %collective-permute-start.2 = (bf16[4,4,512]{2,1,0:T(4,128)(2,1)}, bf16[4,4,512]{2,1,0:T(4,128)(2,1)S(1)}, u32[]{:S(2)}, u32[]{:S(2)}) collective-permute-start(bf16[4,4,512]{2,1,0:T(4,128)(2,1)} %bitcast.23), channel_id=1, source_target_pairs={{0,24},{8,16},{16,8},{24,0},{1,25},{9,17},{17,9},{25,1},{2,26},{10... | collective-permute-start | bytes 49160 | tf_op jit(solution)/shard_map/ppermute | solution.py:21
  5.8 4.8 %collective-permute-start.1 = (bf16[4,4,512]{2,1,0:T(4,128)(2,1)}, bf16[4,4,512]{2,1,0:T(4,128)(2,1)S(1)}, u32[]{:S(2)}, u32[]{:S(2)}) collective-permute-start(bf16[4,4,512]{2,1,0:T(4,128)(2,1)} %bitcast.24), channel_id=1, source_target_pairs={{0,16},{8,24},{16,0},{24,8},{1,17},{9,25},{17,1},{25,9},{2,18},{10... | collective-permute-start | bytes 49160 | tf_op jit(solution)/shard_map/ppermute | solution.py:21
  5.8 4.8 %collective-permute-start = (bf16[4,4,512]{2,1,0:T(4,128)(2,1)}, bf16[4,4,512]{2,1,0:T(4,128)(2,1)S(1)}, u32[]{:S(2)}, u32[]{:S(2)}) collective-permute-start(bf16[4,4,512]{2,1,0:T(4,128)(2,1)} %bitcast.25), channel_id=1, source_target_pairs={{0,8},{8,0},{16,24},{24,16},{1,9},{9,1},{17,25},{25,17},{2,10},{10... | collective-permute-start | bytes 49160 | tf_op jit(solution)/shard_map/ppermute | solution.py:21
  6.4 4.2 %copy-start.4 = (bf16[1,1,4,4,512]{4,3,2,1,0:T(4,128)(2,1)S(1)}, bf16[1,1,4,4,512]{4,3,2,1,0:T(4,128)(2,1)}, u32[]{:S(2)}) copy-start(bf16[1,1,4,4,512]{4,3,2,1,0:T(4,128)(2,1)} %param.11) | copy-start | bytes 49156
  6.4 4.2 %copy-start.5 = (s32[1,1,4]{2,1,0:T(1,128)S(1)}, s32[1,1,4]{2,1,0:T(1,128)}, u32[]{:S(2)}) copy-start(s32[1,1,4]{2,1,0:T(1,128)} %param.7) | copy-start | bytes 52
  11.9 1.6 %collective-permute-start.3 = (f32[16,4480]{1,0:T(8,128)S(1)}, f32[16,4480]{1,0:T(8,128)S(1)}, u32[]{:S(2)}, u32[]{:S(2)}) collective-permute-start(f32[16,4480]{1,0:T(8,128)S(1)} %get-tuple-element.27), channel_id=1, source_target_pairs={{0,1},{1,0},{2,3},{3,2},{4,5},{5,4},{6,7},{7,6},{8,9},{9,8},{10,11... | collective-permute-start | bytes 860168 | tf_op jit(solution)/shard_map/ppermute | solution.py:21
  13.6 6.4 %collective-permute-start.4 = (bf16[16,4608]{1,0:T(8,128)(2,1)S(1)}, bf16[16,4608]{1,0:T(8,128)(2,1)S(1)}, u32[]{:S(2)}, u32[]{:S(2)}) collective-permute-start(bf16[16,4608]{1,0:T(8,128)(2,1)S(1)} %get-tuple-element.33), channel_id=1, source_target_pairs={{0,3},{1,2},{2,1},{3,0},{4,7},{5,6},{6,5},{7,4},{8,11},{9,10},{10,... | collective-permute-start | bytes 442376 | tf_op jit(solution)/shard_map/ppermute | solution.py:21
  15.0 4.1 %collective-permute-start.5 = (f32[16,128]{1,0:T(8,128)S(1)}, f32[16,128]{1,0:T(8,128)S(1)}, u32[]{:S(2)}, u32[]{:S(2)}) collective-permute-start(f32[16,128]{1,0:T(8,128)S(1)} %get-tuple-element.34), channel_id=1, source_target_pairs={{0,7},{1,6},{2,5},{3,4},{4,3},{5,2},{6,1},{7,0},{8,15},{9,14},{10,... | collective-permute-start | bytes 24584 | tf_op jit(solution)/shard_map/ppermute | solution.py:21
  16.3 3.7 %collective-permute-start.6 = (f32[16,128]{1,0:T(8,128)S(1)}, f32[16,128]{1,0:T(8,128)S(1)}, u32[]{:S(2)}, u32[]{:S(2)}) collective-permute-start(f32[16,128]{1,0:T(8,128)S(1)} %get-tuple-element.32.sum_ref), channel_id=1, source_target_pairs={{0,4},{1,5},{2,6},{3,7},{4,0},{5,1},{6,2},{7,3},{8,12},{9,13},{10,... | collective-permute-start | bytes 24584 | tf_op jit(solution)/shard_map/ppermute | solution.py:21
  20.0 5.8 %collective-permute-start.7 = (f32[32,128]{1,0:T(8,128)S(1)}, f32[32,128]{1,0:T(8,128)S(1)}, u32[]{:S(2)}, u32[]{:S(2)}) collective-permute-start(f32[32,128]{1,0:T(8,128)S(1)} %get-tuple-element.39), channel_id=1, source_target_pairs={{0,24},{8,16},{16,8},{24,0},{1,25},{9,17},{17,9},{25,1},{2,26},{10... | collective-permute-start | bytes 49160 | tf_op jit(solution)/shard_map/ppermute | solution.py:21
  21.6 4.7 %collective-permute-start.8 = (f32[32,128]{1,0:T(8,128)S(1)}, f32[32,128]{1,0:T(8,128)S(1)}, u32[]{:S(2)}, u32[]{:S(2)}) collective-permute-start(f32[32,128]{1,0:T(8,128)S(1)} %get-tuple-element.40), channel_id=1, source_target_pairs={{0,16},{8,24},{16,0},{24,8},{1,17},{9,25},{17,1},{25,9},{2,18},{10... | collective-permute-start | bytes 49160 | tf_op jit(solution)/shard_map/ppermute | solution.py:21
  22.2 4.2 %collective-permute-start.9 = (f32[32,128]{1,0:T(8,128)S(1)}, f32[32,128]{1,0:T(8,128)S(1)}, u32[]{:S(2)}, u32[]{:S(2)}) collective-permute-start(f32[32,128]{1,0:T(8,128)S(1)} %get-tuple-element.41), channel_id=1, source_target_pairs={{0,8},{8,0},{16,24},{24,16},{1,9},{9,1},{17,25},{25,17},{2,10},{10... | collective-permute-start | bytes 49160 | tf_op jit(solution)/shard_map/ppermute | solution.py:21

commit v10 on v9

--- a/solution.py
+++ b/solution.py
@@ -10,6 +10,8 @@
 LANES = 128
 PIECES = 3
 TERMS = 2
+STEPS = 8
+TURNED = 2
 VMEM = pl.BlockSpec(memory_space=pltpu.VMEM)
 HBM = pl.BlockSpec(memory_space=pltpu.HBM)
 F32 = jnp.float32
@@ -37,7 +39,9 @@
     token_ref[...] = jnp.zeros(token_ref.shape, F32)
 
 
-def project_kernel(vis_ref, bias_ref, gain_ref, weight_ref, _, projected_ref, inv_ref, rows_ref, normed_ref):
+def project_kernel(
+    tp, vis_ref, bias_ref, gain_ref, weight_ref, _, projected_ref, inv_ref, turned_ref, rows_ref, normed_ref
+):
     buckets, capacity, features = vis_ref.shape
     for q in range(buckets):
         rows_ref[q * capacity : (q + 1) * capacity, :] = vis_ref[q].astype(F32) + bias_ref[...]
@@ -46,7 +50,20 @@
     inv_rms = lax.rsqrt(mean + 1e-06)
     normed_ref[...] = (inputs * inv_rms * gain_ref[...]).astype(BF16)
     inv_ref[...] = jnp.broadcast_to(inv_rms, inv_ref.shape)
-    projected_ref[...] = jnp.dot(normed_ref[...], weight_ref[...], preferred_element_type=F32)
+    count, width = turned_ref.shape[0], features // tp
+    place, step = lax.axis_index("tp"), features // STEPS
+    projected = jnp.zeros(projected_ref.shape, F32)
+    for i in range(STEPS):
+        part = slice(i * step, (i + 1) * step)
+        projected = projected + jnp.dot(
+            normed_ref[:, part], weight_ref[part, :], preferred_element_type=F32
+        )
+        size = width // STEPS
+        for j in range(count):
+            start = pl.multiple_of((place ^ kept(j) ^ 1) * width, width)
+            block = weight_ref[pl.ds(start + i * size, size), :]
+            turned_ref[j, :, i * size : (i + 1) * size] = block.T
+    projected_ref[...] = projected
 
 
 def kept(j):
@@ -98,10 +115,10 @@
     return total[:count]
 
 
-def products(steps, tp, lhs, weight_ref, out_ref):
+def products(steps, tp, lhs, weight_ref, out_ref, first=0):
     width = weight_ref.shape[0] // tp
     place = lax.axis_index("tp")
-    for j, k in enumerate(steps):
+    for j, k in enumerate(steps, first):
         cols = pl.ds(pl.multiple_of((place ^ k) * width, width), width)
         out_ref[:, j * width : (j + 1) * width] = lax.dot_general(
             lhs, weight_ref[cols, :], (((1,), (1,)), ((), ())), preferred_element_type=F32
@@ -122,7 +139,7 @@
     return row
 
 
-def sent_kernel(enc, tp, counts_ref, projected_ref, weight_ref, vis_ref, bias_ref, gain_ref, inv_ref, *refs):
+def sent_kernel(enc, tp, counts_ref, projected_ref, turned_ref, weight_ref, vis_ref, bias_ref, gain_ref, inv_ref, *refs):
     cots = refs[:enc]
     kv_ref, dots_ref, lhs_ref, send_ref, sums_ref = refs[enc:]
     buckets, capacity, columns = kv_ref.shape
@@ -141,7 +158,12 @@
     lhs = masked.astype(BF16)
     lhs_ref[...] = lhs
     steps = [kept(j) ^ 1 for j in range(tp // 2)]
-    products(steps, tp, lhs, weight_ref, send_ref)
+    count, _, width = turned_ref.shape
+    for j in range(count):
+        send_ref[:, j * width : (j + 1) * width] = jnp.dot(
+            lhs, turned_ref[j], preferred_element_type=F32
+        )
+    products(steps[count:], tp, lhs, weight_ref, send_ref, count)
     dots = jnp.sum(masked * projected_ref[...], axis=1, keepdims=True)
     dots_ref[...] = jnp.broadcast_to(dots, dots_ref.shape)
     width = vis_ref.shape[2] // tp
@@ -265,9 +287,13 @@
         [pltpu.with_memory_space_constraint(a, pltpu.HBM) for a in (kv_weight, vis, bias, gain)],
         specs=[HBM] * 4,
     )
-    projected, inv_rms = run(
-        project_kernel,
-        (struct((rows, columns), F32), struct((rows, LANES), F32)),
+    projected, inv_rms, turned = run(
+        part(project_kernel, tp),
+        (
+            struct((rows, columns), F32),
+            struct((rows, LANES), F32),
+            struct((min(TURNED, pairs), columns, width), BF16),
+        ),
         (vis, bias, gain, kv_weight, token),
         scratch=[pltpu.VMEM((rows, features), F32), pltpu.VMEM((rows, features), BF16)],
     )
@@ -281,7 +307,7 @@
             struct((rows, columns), BF16),
             struct((rows, half + side(pairs * chunks, rows, F32)), F32),
         ),
-        (counts[0], projected, kv_weight, vis, bias, gain, inv_rms, *cots),
+        (counts[0], projected, turned, kv_weight, vis, bias, gain, inv_rms, *cots),
         scratch=[pltpu.VMEM((pairs * chunks, LANES), F32)],
     )
     got = swap(send, "tp", 1)

time: 27.1 us -> 26.6 us (0.982)
  Pallas kernels: 5.48 us -> 5.1 us
    pallas_call x8, Pallas kernels: 5.48 us -> 5.1 us  [call(): pl.pallas_call(kernel, out_shape=tuple(outs), in_specs=specs or [VMEM] *...]
  transfers between devices with their start and end apart: 10 -> 10, of which waited for: 7 -> 7; matrix products, arithmetic and copies ran while one was open for 0% -> 0% of each run, Pallas kernels for 13% -> 14%
where the time goes in v10:
time: 26.6 us; the launch traced here: 26.5 us
  starting transfers between devices  13.5 us (51%)
  waiting for transfers between devices  7.09 us (27%)
  Pallas kernels  5.1 us (19%)
  between operations  0.72 us (3%)
    ppermute x10, starting transfers between devices, swap(): return lax.ppermute(x, axis, [(i, i ^ k) for i in range(n)])  13.5 us
    ppermute x10, waiting for transfers between devices, swap(): return lax.ppermute(x, axis, [(i, i ^ k) for i in range(n)])  7.09 us
    pallas_call x8, Pallas kernels, call(): pl.pallas_call(kernel, out_shape=tuple(outs), in_specs=specs or [VMEM] *...  5.1 us
  transfers between devices with their start and end apart: 10, of which 7 were waited for; matrix products, arithmetic and copies ran while one was open for 0% of the time, Pallas kernels for 14%

profile of v10, /device:TPU:0, one launch (start us, length us, event | category | flops | bytes accessed | tf_op | source)
XLA Modules:
  0.0 26.5 jit_solution(16441243339117721160)
XLA Ops:
  0.6 0.0 copy-start
  0.6 0.0 copy-start.3
  0.7 0.0 copy-start.2
  0.7 0.0 copy-start.1
  0.7 5.1 %collective-permute-start.2 = (bf16[4,4,512]{2,1,0:T(4,128)(2,1)}, bf16[4,4,512]{2,1,0:T(4,128)(2,1)S(1)}, u32[]{:S(2)}, u32[]{:S(2)}) collective-permute-start(bf16[4,4,512]{2,1,0:T(4,128)(2,1)} %bitcast.23), channel_id=1, source_target_pairs={{0,24},{8,16},{16,8},{24,0},{1,25},{9,17},{17,9},{25,1},{2,26},{10... | collective-permute-start | bytes 49160 | tf_op jit(solution)/shard_map/ppermute | solution.py:23
  5.8 0.0 collective-permute-start.1
  5.8 0.6 %collective-permute-start = (bf16[4,4,512]{2,1,0:T(4,128)(2,1)}, bf16[4,4,512]{2,1,0:T(4,128)(2,1)S(1)}, u32[]{:S(2)}, u32[]{:S(2)}) collective-permute-start(bf16[4,4,512]{2,1,0:T(4,128)(2,1)} %bitcast.25), channel_id=1, source_target_pairs={{0,8},{8,0},{16,24},{24,16},{1,9},{9,1},{17,25},{25,17},{2,10},{10... | collective-permute-start | bytes 49160 | tf_op jit(solution)/shard_map/ppermute | solution.py:23
  6.4 0.0 copy-start.4
  6.4 0.0 copy-start.5
  6.4 0.0 copy-done
  6.4 0.0 copy-done.3
  6.5 0.0 copy-done.2
  6.5 0.0 copy-done.1
  6.5 1.6 %shard_map.86 = (f32[16,512]{1,0:T(8,128)S(1)}, f32[16,128]{1,0:T(8,128)S(1)}, bf16[2,512,2048]{2,1,0:T(8,128)(2,1)S(1)}) custom-call(bf16[4,4,8192]{2,1,0:T(4,128)(2,1)S(1)} %bitcast.9, f32[1,8192]{1,0:T(1,128)S(1)} %bitcast.14, f32[1,8192]{1,0:T(1,128)S(1)} %bitcast.19, bf16[8192,512]{1,0:T(8,128)(2,1)S(1)} %copy-done, f32[8,128]{1,0:T(8,128)S(1)} %shard_map.85._), custom_call_target="tpu_custom_call" | custom-call | tf_op jit(solution)/shard_map/pallas_call | solution.py:27
  8.0 0.0 collective-permute-done.2.refs_3_
  8.0 2.6 %collective-permute-done.1.refs_2_ = bf16[4,4,512]{2,1,0:T(4,128)(2,1)S(1)} collective-permute-done((bf16[4,4,512]{2,1,0:T(4,128)(2,1)}, bf16[4,4,512]{2,1,0:T(4,128)(2,1)S(1)}, u32[]{:S(2)}, u32[]{:S(2)}) %collective-permute-start.1) | collective-permute-done | bytes 16416 | tf_op jit(solution)/shard_map/ppermute | solution.py:23
  10.6 0.0 collective-permute-done.refs_1_
  10.6 0.0 copy-done.4
  10.6 0.0 copy-done.5
  10.6 0.7 %shard_map.87 = (f32[4,4,512]{2,1,0:T(4,128)S(1)}, f32[16,128]{1,0:T(8,128)S(1)}, bf16[16,512]{1,0:T(8,128)(2,1)S(1)}, f32[16,4480]{1,0:T(8,128)S(1)}) custom-call(s32[1,4]{1,0:T(1,128)S(1)} %bitcast.27, f32[16,512]{1,0:T(8,128)S(1)} %get-tuple-element.25.projected_ref, bf16[2,512,2048]{2,1,0:T(8,128)(2,1)S(1)} %get-tuple-element.26.turned_ref, ...), custom_call_target="tpu_custom_call" | custom-call | tf_op jit(solution)/shard_map/pallas_call | solution.py:27
  11.4 0.1 collective-permute-start.3
  11.5 1.2 %shard_map.88 = (f32[16,4096]{1,0:T(8,128)S(1)}, f32[32,128]{1,0:T(8,128)S(1)}) custom-call(bf16[16,512]{1,0:T(8,128)(2,1)S(1)} %get-tuple-element.30.lhs_ref, bf16[8192,512]{1,0:T(8,128)(2,1)S(1)} %copy-done, bf16[4,4,8192]{2,1,0:T(4,128)(2,1)S(1)} %bitcast.11, f32[1,8192]{1,0:T(1,128)S(1)} %bitcast.16, f32[1,8192]{1,0:T(1,128)S(1)} %bitcast.21, ...), custom_call_target="tpu_custom_call" | custom-call | tf_op jit(solution)/shard_map/pallas_call | solution.py:27
  12.7 0.3 %collective-permute-done.3.got_ref = f32[16,4480]{1,0:T(8,128)S(1)} collective-permute-done((f32[16,4480]{1,0:T(8,128)S(1)}, f32[16,4480]{1,0:T(8,128)S(1)}, u32[]{:S(2)}, u32[]{:S(2)}) %collective-permute-start.3) | collective-permute-done | bytes 286752 | tf_op jit(solution)/shard_map/ppermute | solution.py:23
  13.0 0.1 shard_map.89
  13.1 1.3 %collective-permute-start.4 = (bf16[16,4608]{1,0:T(8,128)(2,1)S(1)}, bf16[16,4608]{1,0:T(8,128)(2,1)S(1)}, u32[]{:S(2)}, u32[]{:S(2)}) collective-permute-start(bf16[16,4608]{1,0:T(8,128)(2,1)S(1)} %get-tuple-element.35), channel_id=1, source_target_pairs={{0,3},{1,2},{2,1},{3,0},{4,7},{5,6},{6,5},{7,4},{8,11},{9,10},{10,... | collective-permute-start | bytes 442376 | tf_op jit(solution)/shard_map/ppermute | solution.py:23
  14.5 1.4 %collective-permute-start.5 = (f32[16,128]{1,0:T(8,128)S(1)}, f32[16,128]{1,0:T(8,128)S(1)}, u32[]{:S(2)}, u32[]{:S(2)}) collective-permute-start(f32[16,128]{1,0:T(8,128)S(1)} %get-tuple-element.36), channel_id=1, source_target_pairs={{0,7},{1,6},{2,5},{3,4},{4,3},{5,2},{6,1},{7,0},{8,15},{9,14},{10,... | collective-permute-start | bytes 24584 | tf_op jit(solution)/shard_map/ppermute | solution.py:23
  15.8 0.5 %collective-permute-start.6 = (f32[16,128]{1,0:T(8,128)S(1)}, f32[16,128]{1,0:T(8,128)S(1)}, u32[]{:S(2)}, u32[]{:S(2)}) collective-permute-start(f32[16,128]{1,0:T(8,128)S(1)} %get-tuple-element.34.sum_ref), channel_id=1, source_target_pairs={{0,4},{1,5},{2,6},{3,7},{4,0},{5,1},{6,2},{7,3},{8,12},{9,13},{10,... | collective-permute-start | bytes 24584 | tf_op jit(solution)/shard_map/ppermute | solution.py:23
  16.4 2.2 %collective-permute-done.5.refs_1_ = f32[16,128]{1,0:T(8,128)S(1)} collective-permute-done((f32[16,128]{1,0:T(8,128)S(1)}, f32[16,128]{1,0:T(8,128)S(1)}, u32[]{:S(2)}, u32[]{:S(2)}) %collective-permute-start.5) | collective-permute-done | bytes 8224 | tf_op jit(solution)/shard_map/ppermute | solution.py:23
  18.5 0.9 %collective-permute-done.6.refs_2_ = f32[16,128]{1,0:T(8,128)S(1)} collective-permute-done((f32[16,128]{1,0:T(8,128)S(1)}, f32[16,128]{1,0:T(8,128)S(1)}, u32[]{:S(2)}, u32[]{:S(2)}) %collective-permute-start.6) | collective-permute-done | bytes 8224 | tf_op jit(solution)/shard_map/ppermute | solution.py:23
  19.5 0.0 collective-permute-done.4.refs_0_
  19.5 1.6 %collective-permute-start.7 = (f32[32,128]{1,0:T(8,128)S(1)}, f32[32,128]{1,0:T(8,128)S(1)}, u32[]{:S(2)}, u32[]{:S(2)}) collective-permute-start(f32[32,128]{1,0:T(8,128)S(1)} %get-tuple-element.41), channel_id=1, source_target_pairs={{0,24},{8,16},{16,8},{24,0},{1,25},{9,17},{17,9},{25,1},{2,26},{10... | collective-permute-start | bytes 49160 | tf_op jit(solution)/shard_map/ppermute | solution.py:23
  21.0 0.6 %collective-permute-start.8 = (f32[32,128]{1,0:T(8,128)S(1)}, f32[32,128]{1,0:T(8,128)S(1)}, u32[]{:S(2)}, u32[]{:S(2)}) collective-permute-start(f32[32,128]{1,0:T(8,128)S(1)} %get-tuple-element.42), channel_id=1, source_target_pairs={{0,16},{8,24},{16,0},{24,8},{1,17},{9,25},{17,1},{25,9},{2,18},{10... | collective-permute-start | bytes 49160 | tf_op jit(solution)/shard_map/ppermute | solution.py:23
  21.7 2.3 %collective-permute-start.9 = (f32[32,128]{1,0:T(8,128)S(1)}, f32[32,128]{1,0:T(8,128)S(1)}, u32[]{:S(2)}, u32[]{:S(2)}) collective-permute-start(f32[32,128]{1,0:T(8,128)S(1)} %get-tuple-element.43), channel_id=1, source_target_pairs={{0,8},{8,0},{16,24},{24,16},{1,9},{9,1},{17,25},{25,17},{2,10},{10... | collective-permute-start | bytes 49160 | tf_op jit(solution)/shard_map/ppermute | solution.py:23
  23.9 0.8 %shard_map.91 = (bf16[4,4,2048]{2,1,0:T(4,128)(2,1)}, f32[8,128]{1,0:T(8,128)S(1)}) custom-call(bf16[4,4,8192]{2,1,0:T(4,128)(2,1)S(1)} %bitcast.12, f32[1,8192]{1,0:T(1,128)S(1)} %bitcast.17, f32[1,8192]{1,0:T(1,128)S(1)} %bitcast.22, f32[16,128]{1,0:T(8,128)S(1)} %get-tuple-element.27.inv_ref, f32[16,128]{1,0:T(8,128)S(1)} %get-tuple-element.38.dots_ref, ...), custom_call_target="tpu_custom_call" | custom-call | tf_op jit(solution)/shard_map/pallas_call | solution.py:27
  24.8 0.5 %collective-permute-done.7.refs_0_ = f32[32,128]{1,0:T(8,128)S(1)} collective-permute-done((f32[32,128]{1,0:T(8,128)S(1)}, f32[32,128]{1,0:T(8,128)S(1)}, u32[]{:S(2)}, u32[]{:S(2)}) %collective-permute-start.7) | collective-permute-done | bytes 16416 | tf_op jit(solution)/shard_map/ppermute | solution.py:23
  25.3 0.5 %collective-permute-done.8.refs_1_ = f32[32,128]{1,0:T(8,128)S(1)} collective-permute-done((f32[32,128]{1,0:T(8,128)S(1)}, f32[32,128]{1,0:T(8,128)S(1)}, u32[]{:S(2)}, u32[]{:S(2)}) %collective-permute-start.8) | collective-permute-done | bytes 16416 | tf_op jit(solution)/shard_map/ppermute | solution.py:23
  25.7 0.1 collective-permute-done.9.refs_2_
  25.8 0.6 %shard_map.92 = (f32[16,128]{1,0:T(8,128)}, bf16[4,4,512]{2,1,0:T(4,128)(2,1)}) custom-call(f32[16,128]{1,0:T(8,128)S(1)} %get-tuple-element.37.total_ref, f32[4,4,512]{2,1,0:T(4,128)S(1)} %get-tuple-element.28.kv_ref, f32[8,128]{1,0:T(8,128)S(1)} %get-tuple-element.40._, f32[32,128]{1,0:T(8,128)S(1)} %collective-permute-done.7.refs_0_, ...), custom_call_target="tpu_custom_call" | custom-call | tf_op jit(solution)/shard_map/pallas_call | solution.py:27
  (2 shorter events, 0.0 us)
Async XLA Ops:
  0.6 5.8 %copy-start = (bf16[8192,512]{1,0:T(8,128)(2,1)S(1)}, bf16[8192,512]{1,0:T(8,128)(2,1)}, u32[]{:S(2)}) copy-start(bf16[8192,512]{1,0:T(8,128)(2,1)} %weight_ref.5) | copy-start | bytes 25165828
  0.6 5.8 %copy-start.3 = (f32[8192]{0:T(1024)S(1)}, f32[8192]{0:T(1024)}, u32[]{:S(2)}) copy-start(f32[8192]{0:T(1024)} %param.9) | copy-start | bytes 98308
  0.7 5.8 %copy-start.2 = (f32[8192]{0:T(1024)S(1)}, f32[8192]{0:T(1024)}, u32[]{:S(2)}) copy-start(f32[8192]{0:T(1024)} %param.8) | copy-start | bytes 98308
  0.7 5.8 %copy-start.1 = (bf16[1,1,4,4,8192]{4,3,2,1,0:T(4,128)(2,1)S(1)}, bf16[1,1,4,4,8192]{4,3,2,1,0:T(4,128)(2,1)}, u32[]{:S(2)}) copy-start(bf16[1,1,4,4,8192]{4,3,2,1,0:T(4,128)(2,1)} %param.6) | copy-start | bytes 786436
  0.7 7.4 %collective-permute-start.2 = (bf16[4,4,512]{2,1,0:T(4,128)(2,1)}, bf16[4,4,512]{2,1,0:T(4,128)(2,1)S(1)}, u32[]{:S(2)}, u32[]{:S(2)}) collective-permute-start(bf16[4,4,512]{2,1,0:T(4,128)(2,1)} %bitcast.23), channel_id=1, source_target_pairs={{0,24},{8,16},{16,8},{24,0},{1,25},{9,17},{17,9},{25,1},{2,26},{10... | collective-permute-start | bytes 49160 | tf_op jit(solution)/shard_map/ppermute | solution.py:23
  5.8 4.8 %collective-permute-start.1 = (bf16[4,4,512]{2,1,0:T(4,128)(2,1)}, bf16[4,4,512]{2,1,0:T(4,128)(2,1)S(1)}, u32[]{:S(2)}, u32[]{:S(2)}) collective-permute-start(bf16[4,4,512]{2,1,0:T(4,128)(2,1)} %bitcast.24), channel_id=1, source_target_pairs={{0,16},{8,24},{16,0},{24,8},{1,17},{9,25},{17,1},{25,9},{2,18},{10... | collective-permute-start | bytes 49160 | tf_op jit(solution)/shard_map/ppermute | solution.py:23
  5.8 4.8 %collective-permute-start = (bf16[4,4,512]{2,1,0:T(4,128)(2,1)}, bf16[4,4,512]{2,1,0:T(4,128)(2,1)S(1)}, u32[]{:S(2)}, u32[]{:S(2)}) collective-permute-start(bf16[4,4,512]{2,1,0:T(4,128)(2,1)} %bitcast.25), channel_id=1, source_target_pairs={{0,8},{8,0},{16,24},{24,16},{1,9},{9,1},{17,25},{25,17},{2,10},{10... | collective-permute-start | bytes 49160 | tf_op jit(solution)/shard_map/ppermute | solution.py:23
  6.4 4.2 %copy-start.4 = (bf16[1,1,4,4,512]{4,3,2,1,0:T(4,128)(2,1)S(1)}, bf16[1,1,4,4,512]{4,3,2,1,0:T(4,128)(2,1)}, u32[]{:S(2)}) copy-start(bf16[1,1,4,4,512]{4,3,2,1,0:T(4,128)(2,1)} %param.11) | copy-start | bytes 49156
  6.4 4.2 %copy-start.5 = (s32[1,1,4]{2,1,0:T(1,128)S(1)}, s32[1,1,4]{2,1,0:T(1,128)}, u32[]{:S(2)}) copy-start(s32[1,1,4]{2,1,0:T(1,128)} %param.7) | copy-start | bytes 52
  11.4 1.6 %collective-permute-start.3 = (f32[16,4480]{1,0:T(8,128)S(1)}, f32[16,4480]{1,0:T(8,128)S(1)}, u32[]{:S(2)}, u32[]{:S(2)}) collective-permute-start(f32[16,4480]{1,0:T(8,128)S(1)} %get-tuple-element.29), channel_id=1, source_target_pairs={{0,1},{1,0},{2,3},{3,2},{4,5},{5,4},{6,7},{7,6},{8,9},{9,8},{10,11... | collective-permute-start | bytes 860168 | tf_op jit(solution)/shard_map/ppermute | solution.py:23
  13.1 6.4 %collective-permute-start.4 = (bf16[16,4608]{1,0:T(8,128)(2,1)S(1)}, bf16[16,4608]{1,0:T(8,128)(2,1)S(1)}, u32[]{:S(2)}, u32[]{:S(2)}) collective-permute-start(bf16[16,4608]{1,0:T(8,128)(2,1)S(1)} %get-tuple-element.35), channel_id=1, source_target_pairs={{0,3},{1,2},{2,1},{3,0},{4,7},{5,6},{6,5},{7,4},{8,11},{9,10},{10,... | collective-permute-start | bytes 442376 | tf_op jit(solution)/shard_map/ppermute | solution.py:23
  14.5 4.1 %collective-permute-start.5 = (f32[16,128]{1,0:T(8,128)S(1)}, f32[16,128]{1,0:T(8,128)S(1)}, u32[]{:S(2)}, u32[]{:S(2)}) collective-permute-start(f32[16,128]{1,0:T(8,128)S(1)} %get-tuple-element.36), channel_id=1, source_target_pairs={{0,7},{1,6},{2,5},{3,4},{4,3},{5,2},{6,1},{7,0},{8,15},{9,14},{10,... | collective-permute-start | bytes 24584 | tf_op jit(solution)/shard_map/ppermute | solution.py:23
  15.8 3.7 %collective-permute-start.6 = (f32[16,128]{1,0:T(8,128)S(1)}, f32[16,128]{1,0:T(8,128)S(1)}, u32[]{:S(2)}, u32[]{:S(2)}) collective-permute-start(f32[16,128]{1,0:T(8,128)S(1)} %get-tuple-element.34.sum_ref), channel_id=1, source_target_pairs={{0,4},{1,5},{2,6},{3,7},{4,0},{5,1},{6,2},{7,3},{8,12},{9,13},{10,... | collective-permute-start | bytes 24584 | tf_op jit(solution)/shard_map/ppermute | solution.py:23
  19.5 5.8 %collective-permute-start.7 = (f32[32,128]{1,0:T(8,128)S(1)}, f32[32,128]{1,0:T(8,128)S(1)}, u32[]{:S(2)}, u32[]{:S(2)}) collective-permute-start(f32[32,128]{1,0:T(8,128)S(1)} %get-tuple-element.41), channel_id=1, source_target_pairs={{0,24},{8,16},{16,8},{24,0},{1,25},{9,17},{17,9},{25,1},{2,26},{10... | collective-permute-start | bytes 49160 | tf_op jit(solution)/shard_map/ppermute | solution.py:23
  21.0 4.7 %collective-permute-start.8 = (f32[32,128]{1,0:T(8,128)S(1)}, f32[32,128]{1,0:T(8,128)S(1)}, u32[]{:S(2)}, u32[]{:S(2)}) collective-permute-start(f32[32,128]{1,0:T(8,128)S(1)} %get-tuple-element.42), channel_id=1, source_target_pairs={{0,16},{8,24},{16,0},{24,8},{1,17},{9,25},{17,1},{25,9},{2,18},{10... | collective-permute-start | bytes 49160 | tf_op jit(solution)/shard_map/ppermute | solution.py:23
  21.7 4.2 %collective-permute-start.9 = (f32[32,128]{1,0:T(8,128)S(1)}, f32[32,128]{1,0:T(8,128)S(1)}, u32[]{:S(2)}, u32[]{:S(2)}) collective-permute-start(f32[32,128]{1,0:T(8,128)S(1)} %get-tuple-element.43), channel_id=1, source_target_pairs={{0,8},{8,0},{16,24},{24,16},{1,9},{9,1},{17,25},{25,17},{2,10},{10... | collective-permute-start | bytes 49160 | tf_op jit(solution)/shard_map/ppermute | solution.py:23

commit v11 on v10

--- a/solution.py
+++ b/solution.py
@@ -125,21 +125,17 @@
         )
 
 
-def row_sum(k, tp, term, vis_ref, bias_ref, gain_ref, inv_rms, dots):
-    buckets, capacity, features = vis_ref.shape
+def row_sum(k, tp, term, rows_ref, gain_ref, inv_rms, dots):
+    features = rows_ref.shape[1]
     width = features // tp
     place = lax.axis_index("tp")
     cols = pl.ds(pl.multiple_of((place ^ k) * width, width), width)
     scale = inv_rms * inv_rms * dots * (1.0 / features)
     row = gain_ref[:, cols] * jnp.sum(inv_rms * term, axis=0, keepdims=True)
-    for q in range(buckets):
-        part = scale[q * capacity : (q + 1) * capacity]
-        inputs = vis_ref[q, :, cols].astype(F32) + bias_ref[:, cols]
-        row = row - jnp.sum(inputs * part, axis=0, keepdims=True)
-    return row
-
-
-def sent_kernel(enc, tp, counts_ref, projected_ref, turned_ref, weight_ref, vis_ref, bias_ref, gain_ref, inv_ref, *refs):
+    return row - jnp.sum(rows_ref[:, cols] * scale, axis=0, keepdims=True)
+
+
+def sent_kernel(enc, tp, counts_ref, projected_ref, turned_ref, weight_ref, rows_ref, gain_ref, inv_ref, *refs):
     cots = refs[:enc]
     kv_ref, dots_ref, lhs_ref, send_ref, sums_ref = refs[enc:]
     buckets, capacity, columns = kv_ref.shape
@@ -166,25 +162,25 @@
     products(steps[count:], tp, lhs, weight_ref, send_ref, count)
     dots = jnp.sum(masked * projected_ref[...], axis=1, keepdims=True)
     dots_ref[...] = jnp.broadcast_to(dots, dots_ref.shape)
-    width = vis_ref.shape[2] // tp
+    width = rows_ref.shape[1] // tp
     chunks, half = width // LANES, tp // 2 * width
     inv_rms = inv_ref[:, :1]
     for j, k in enumerate(steps):
         term = send_ref[:, j * width : (j + 1) * width]
-        row = row_sum(k, tp, term, vis_ref, bias_ref, gain_ref, inv_rms, dots)
+        row = row_sum(k, tp, term, rows_ref, gain_ref, inv_rms, dots)
         for i in range(chunks):
             sums_ref[j * chunks + i : j * chunks + i + 1, :] = row[:, i * LANES : (i + 1) * LANES]
     put_side(send_ref, half, dots_ref[...], sums_ref[...])
 
 
-def kept_kernel(tp, lhs_ref, weight_ref, vis_ref, bias_ref, gain_ref, inv_ref, dots_ref, kept_ref, sums_ref):
-    width = vis_ref.shape[2] // tp
+def kept_kernel(tp, lhs_ref, weight_ref, rows_ref, gain_ref, inv_ref, dots_ref, kept_ref, sums_ref):
+    width = rows_ref.shape[1] // tp
     chunks = width // LANES
     steps = [kept(j) for j in range(tp // 2)]
     products(steps, tp, lhs_ref[...], weight_ref, kept_ref)
     for j, k in enumerate(steps):
         term = kept_ref[:, j * width : (j + 1) * width]
-        row = row_sum(k, tp, term, vis_ref, bias_ref, gain_ref, inv_ref[:, :1], dots_ref[:, :1])
+        row = row_sum(k, tp, term, rows_ref, gain_ref, inv_ref[:, :1], dots_ref[:, :1])
         for i in range(chunks):
             sums_ref[j * chunks + i : j * chunks + i + 1, :] = row[:, i * LANES : (i + 1) * LANES]
 
@@ -231,10 +227,10 @@
             sends[k - 1][at : at + capacity, :] = block[:, j * LANES : (j + 1) * LANES]
 
 
-def combine_kernel(vis_ref, bias_ref, gain_ref, inv_ref, dots_ref, own_ref, *refs):
+def combine_kernel(rows_ref, gain_ref, inv_ref, dots_ref, own_ref, *refs):
     gots, (out_ref, token_ref) = refs[:-2], refs[-2:]
-    buckets, capacity, features = vis_ref.shape
-    width = own_ref.shape[1]
+    buckets, capacity, width = out_ref.shape
+    features = rows_ref.shape[1]
     place = lax.axis_index("tp")
     own = pl.ds(pl.multiple_of(place * width, width), width)
     grad_normed, row_dot = own_ref[...], dots_ref[:, :1]
@@ -245,10 +241,9 @@
     inv_rms = inv_ref[:, :1]
     first = inv_rms * gain_ref[:, own] * grad_normed
     scale = inv_rms * inv_rms * row_dot * (1.0 / features)
+    grad_rows = first - rows_ref[:, own] * scale
     for q in range(buckets):
-        rows = slice(q * capacity, (q + 1) * capacity)
-        inputs = vis_ref[q, :, own].astype(F32) + bias_ref[:, own]
-        out_ref[q] = (first[rows] - inputs * scale[rows]).astype(BF16)
+        out_ref[q] = grad_rows[q * capacity : (q + 1) * capacity].astype(BF16)
     token_ref[...] = jnp.zeros(token_ref.shape, F32)
 
 
@@ -287,15 +282,16 @@
         [pltpu.with_memory_space_constraint(a, pltpu.HBM) for a in (kv_weight, vis, bias, gain)],
         specs=[HBM] * 4,
     )
-    projected, inv_rms, turned = run(
+    projected, inv_rms, turned, inputs = run(
         part(project_kernel, tp),
         (
             struct((rows, columns), F32),
             struct((rows, LANES), F32),
             struct((min(TURNED, pairs), columns, width), BF16),
+            struct((rows, features), F32),
         ),
         (vis, bias, gain, kv_weight, token),
-        scratch=[pltpu.VMEM((rows, features), F32), pltpu.VMEM((rows, features), BF16)],
+        scratch=[pltpu.VMEM((rows, features), BF16)],
     )
     own_cot = cot
     cots = [own_cot] + [swap(cot, "enc", k) for k in range(1, enc)]
@@ -307,14 +303,14 @@
             struct((rows, columns), BF16),
             struct((rows, half + side(pairs * chunks, rows, F32)), F32),
         ),
-        (counts[0], projected, turned, kv_weight, vis, bias, gain, inv_rms, *cots),
+        (counts[0], projected, turned, kv_weight, inputs, gain, inv_rms, *cots),
         scratch=[pltpu.VMEM((pairs * chunks, LANES), F32)],
     )
     got = swap(send, "tp", 1)
     terms, sums = run(
         part(kept_kernel, tp),
         (struct((rows, half), F32), struct((pairs * chunks, LANES), F32)),
-        (lhs, kv_weight, vis, bias, gain, inv_rms, dots),
+        (lhs, kv_weight, inputs, gain, inv_rms, dots),
     )
     dots, own, *refs = run(
         part(fold_kernel, width),
@@ -342,7 +338,7 @@
     visual_grad, token = run(
         combine_kernel,
         (struct((buckets, capacity, width), BF16), struct((8, LANES), F32)),
-        (vis, bias, gain, inv_rms, dots, own, *gots),
+        (inputs, gain, inv_rms, dots, own, *gots),
     )
     gots = [swap(s, "enc", k + 1) for k, s in enumerate(sends)]
     bias_grad, key_values = run(

time: 26.6 us -> 26.6 us (level)
  no operation moved by 1% of the time
where the time goes in v11:
time: 26.6 us; the launch traced here: 26.5 us
  starting transfers between devices  13.5 us (51%)
  waiting for transfers between devices  7.12 us (27%)
  Pallas kernels  5.06 us (19%)
  between operations  0.73 us (3%)
    ppermute x10, starting transfers between devices, swap(): return lax.ppermute(x, axis, [(i, i ^ k) for i in range(n)])  13.5 us
    ppermute x10, waiting for transfers between devices, swap(): return lax.ppermute(x, axis, [(i, i ^ k) for i in range(n)])  7.12 us
    pallas_call x8, Pallas kernels, call(): pl.pallas_call(kernel, out_shape=tuple(outs), in_specs=specs or [VMEM] *...  5.06 us
  transfers between devices with their start and end apart: 10, of which 7 were waited for; matrix products, arithmetic and copies ran while one was open for 0% of the time, Pallas kernels for 14%

profile of v11, /device:TPU:0, one launch (start us, length us, event | category | flops | bytes accessed | tf_op | source)
XLA Modules:
  0.0 26.5 jit_solution(13038371767903461465)
XLA Ops:
  0.6 0.0 copy-start
  0.6 0.0 copy-start.2
  0.7 0.0 copy-start.3
  0.7 0.0 copy-start.1
  0.7 5.1 %collective-permute-start.2 = (bf16[4,4,512]{2,1,0:T(4,128)(2,1)}, bf16[4,4,512]{2,1,0:T(4,128)(2,1)S(1)}, u32[]{:S(2)}, u32[]{:S(2)}) collective-permute-start(bf16[4,4,512]{2,1,0:T(4,128)(2,1)} %bitcast.17), channel_id=1, source_target_pairs={{0,24},{8,16},{16,8},{24,0},{1,25},{9,17},{17,9},{25,1},{2,26},{10... | collective-permute-start | bytes 49160 | tf_op jit(solution)/shard_map/ppermute | solution.py:23
  5.8 0.0 collective-permute-start.1
  5.8 0.6 %collective-permute-start = (bf16[4,4,512]{2,1,0:T(4,128)(2,1)}, bf16[4,4,512]{2,1,0:T(4,128)(2,1)S(1)}, u32[]{:S(2)}, u32[]{:S(2)}) collective-permute-start(bf16[4,4,512]{2,1,0:T(4,128)(2,1)} %bitcast.19), channel_id=1, source_target_pairs={{0,8},{8,0},{16,24},{24,16},{1,9},{9,1},{17,25},{25,17},{2,10},{10... | collective-permute-start | bytes 49160 | tf_op jit(solution)/shard_map/ppermute | solution.py:23
  6.4 0.0 copy-start.4
  6.4 0.0 copy-start.5
  6.4 0.0 copy-done
  6.4 0.0 copy-done.2
  6.5 0.0 copy-done.3
  6.5 0.0 copy-done.1
  6.5 1.6 %shard_map.86 = (f32[16,512]{1,0:T(8,128)S(1)}, f32[16,128]{1,0:T(8,128)S(1)}, bf16[2,512,2048]{2,1,0:T(8,128)(2,1)S(1)}, f32[16,8192]{1,0:T(8,128)S(1)}) custom-call(bf16[4,4,8192]{2,1,0:T(4,128)(2,1)S(1)} %bitcast.9, f32[1,8192]{1,0:T(1,128)S(1)} %bitcast.16, f32[1,8192]{1,0:T(1,128)S(1)} %bitcast.11, bf16[8192,512]{1,0:T(8,128)(2,1)S(1)} %copy-done, ...), custom_call_target="tpu_custom_call" | custom-call | tf_op jit(solution)/shard_map/pallas_call | solution.py:27
  8.0 0.0 collective-permute-done.2.refs_3_
  8.0 2.6 %collective-permute-done.1.refs_2_ = bf16[4,4,512]{2,1,0:T(4,128)(2,1)S(1)} collective-permute-done((bf16[4,4,512]{2,1,0:T(4,128)(2,1)}, bf16[4,4,512]{2,1,0:T(4,128)(2,1)S(1)}, u32[]{:S(2)}, u32[]{:S(2)}) %collective-permute-start.1) | collective-permute-done | bytes 16416 | tf_op jit(solution)/shard_map/ppermute | solution.py:23
  10.6 0.0 collective-permute-done.refs_1_
  10.6 0.0 copy-done.4
  10.6 0.0 copy-done.5
  10.6 0.7 %shard_map.87 = (f32[4,4,512]{2,1,0:T(4,128)S(1)}, f32[16,128]{1,0:T(8,128)S(1)}, bf16[16,512]{1,0:T(8,128)(2,1)S(1)}, f32[16,4480]{1,0:T(8,128)S(1)}) custom-call(s32[1,4]{1,0:T(1,128)S(1)} %bitcast.21, f32[16,512]{1,0:T(8,128)S(1)} %get-tuple-element.26.projected_ref, bf16[2,512,2048]{2,1,0:T(8,128)(2,1)S(1)} %get-tuple-element.27.turned_ref, ...), custom_call_target="tpu_custom_call" | custom-call | tf_op jit(solution)/shard_map/pallas_call | solution.py:27
  11.4 0.1 collective-permute-start.3
  11.5 1.2 %shard_map.88 = (f32[16,4096]{1,0:T(8,128)S(1)}, f32[32,128]{1,0:T(8,128)S(1)}) custom-call(bf16[16,512]{1,0:T(8,128)(2,1)S(1)} %get-tuple-element.32.lhs_ref, bf16[8192,512]{1,0:T(8,128)(2,1)S(1)} %copy-done, f32[16,8192]{1,0:T(8,128)S(1)} %get-tuple-element.28.rows_ref, f32[1,8192]{1,0:T(1,128)S(1)} %bitcast.13, f32[16,128]{1,0:T(8,128)S(1)} %get-tuple-element.29.inv_ref, ...), custom_call_target="tpu_custom_call" | custom-call | tf_op jit(solution)/shard_map/pallas_call | solution.py:27
  12.7 0.3 %collective-permute-done.3.got_ref = f32[16,4480]{1,0:T(8,128)S(1)} collective-permute-done((f32[16,4480]{1,0:T(8,128)S(1)}, f32[16,4480]{1,0:T(8,128)S(1)}, u32[]{:S(2)}, u32[]{:S(2)}) %collective-permute-start.3) | collective-permute-done | bytes 286752 | tf_op jit(solution)/shard_map/ppermute | solution.py:23
  13.0 0.1 shard_map.89
  13.1 1.3 %collective-permute-start.4 = (bf16[16,4608]{1,0:T(8,128)(2,1)S(1)}, bf16[16,4608]{1,0:T(8,128)(2,1)S(1)}, u32[]{:S(2)}, u32[]{:S(2)}) collective-permute-start(bf16[16,4608]{1,0:T(8,128)(2,1)S(1)} %get-tuple-element.37), channel_id=1, source_target_pairs={{0,3},{1,2},{2,1},{3,0},{4,7},{5,6},{6,5},{7,4},{8,11},{9,10},{10,... | collective-permute-start | bytes 442376 | tf_op jit(solution)/shard_map/ppermute | solution.py:23
  14.5 1.4 %collective-permute-start.5 = (f32[16,128]{1,0:T(8,128)S(1)}, f32[16,128]{1,0:T(8,128)S(1)}, u32[]{:S(2)}, u32[]{:S(2)}) collective-permute-start(f32[16,128]{1,0:T(8,128)S(1)} %get-tuple-element.38), channel_id=1, source_target_pairs={{0,7},{1,6},{2,5},{3,4},{4,3},{5,2},{6,1},{7,0},{8,15},{9,14},{10,... | collective-permute-start | bytes 24584 | tf_op jit(solution)/shard_map/ppermute | solution.py:23
  15.8 0.5 %collective-permute-start.6 = (f32[16,128]{1,0:T(8,128)S(1)}, f32[16,128]{1,0:T(8,128)S(1)}, u32[]{:S(2)}, u32[]{:S(2)}) collective-permute-start(f32[16,128]{1,0:T(8,128)S(1)} %get-tuple-element.36.sum_ref), channel_id=1, source_target_pairs={{0,4},{1,5},{2,6},{3,7},{4,0},{5,1},{6,2},{7,3},{8,12},{9,13},{10,... | collective-permute-start | bytes 24584 | tf_op jit(solution)/shard_map/ppermute | solution.py:23
  16.4 2.2 %collective-permute-done.5.refs_1_ = f32[16,128]{1,0:T(8,128)S(1)} collective-permute-done((f32[16,128]{1,0:T(8,128)S(1)}, f32[16,128]{1,0:T(8,128)S(1)}, u32[]{:S(2)}, u32[]{:S(2)}) %collective-permute-start.5) | collective-permute-done | bytes 8224 | tf_op jit(solution)/shard_map/ppermute | solution.py:23
  18.5 0.9 %collective-permute-done.6.refs_2_ = f32[16,128]{1,0:T(8,128)S(1)} collective-permute-done((f32[16,128]{1,0:T(8,128)S(1)}, f32[16,128]{1,0:T(8,128)S(1)}, u32[]{:S(2)}, u32[]{:S(2)}) %collective-permute-start.6) | collective-permute-done | bytes 8224 | tf_op jit(solution)/shard_map/ppermute | solution.py:23
  19.5 0.0 collective-permute-done.4.refs_0_
  19.5 1.6 %collective-permute-start.7 = (f32[32,128]{1,0:T(8,128)S(1)}, f32[32,128]{1,0:T(8,128)S(1)}, u32[]{:S(2)}, u32[]{:S(2)}) collective-permute-start(f32[32,128]{1,0:T(8,128)S(1)} %get-tuple-element.43), channel_id=1, source_target_pairs={{0,24},{8,16},{16,8},{24,0},{1,25},{9,17},{17,9},{25,1},{2,26},{10... | collective-permute-start | bytes 49160 | tf_op jit(solution)/shard_map/ppermute | solution.py:23
  21.1 0.6 %collective-permute-start.8 = (f32[32,128]{1,0:T(8,128)S(1)}, f32[32,128]{1,0:T(8,128)S(1)}, u32[]{:S(2)}, u32[]{:S(2)}) collective-permute-start(f32[32,128]{1,0:T(8,128)S(1)} %get-tuple-element.44), channel_id=1, source_target_pairs={{0,16},{8,24},{16,0},{24,8},{1,17},{9,25},{17,1},{25,9},{2,18},{10... | collective-permute-start | bytes 49160 | tf_op jit(solution)/shard_map/ppermute | solution.py:23
  21.7 2.3 %collective-permute-start.9 = (f32[32,128]{1,0:T(8,128)S(1)}, f32[32,128]{1,0:T(8,128)S(1)}, u32[]{:S(2)}, u32[]{:S(2)}) collective-permute-start(f32[32,128]{1,0:T(8,128)S(1)} %get-tuple-element.45), channel_id=1, source_target_pairs={{0,8},{8,0},{16,24},{24,16},{1,9},{9,1},{17,25},{25,17},{2,10},{10... | collective-permute-start | bytes 49160 | tf_op jit(solution)/shard_map/ppermute | solution.py:23
  23.9 0.8 %shard_map.91 = (bf16[4,4,2048]{2,1,0:T(4,128)(2,1)}, f32[8,128]{1,0:T(8,128)S(1)}) custom-call(f32[16,8192]{1,0:T(8,128)S(1)} %get-tuple-element.28.rows_ref, f32[1,8192]{1,0:T(1,128)S(1)} %bitcast.14, f32[16,128]{1,0:T(8,128)S(1)} %get-tuple-element.29.inv_ref, f32[16,128]{1,0:T(8,128)S(1)} %get-tuple-element.40.dots_ref, ...), custom_call_target="tpu_custom_call" | custom-call | tf_op jit(solution)/shard_map/pallas_call | solution.py:27
  24.8 0.5 %collective-permute-done.7.refs_0_ = f32[32,128]{1,0:T(8,128)S(1)} collective-permute-done((f32[32,128]{1,0:T(8,128)S(1)}, f32[32,128]{1,0:T(8,128)S(1)}, u32[]{:S(2)}, u32[]{:S(2)}) %collective-permute-start.7) | collective-permute-done | bytes 16416 | tf_op jit(solution)/shard_map/ppermute | solution.py:23
  25.3 0.5 %collective-permute-done.8.refs_1_ = f32[32,128]{1,0:T(8,128)S(1)} collective-permute-done((f32[32,128]{1,0:T(8,128)S(1)}, f32[32,128]{1,0:T(8,128)S(1)}, u32[]{:S(2)}, u32[]{:S(2)}) %collective-permute-start.8) | collective-permute-done | bytes 16416 | tf_op jit(solution)/shard_map/ppermute | solution.py:23
  25.7 0.1 collective-permute-done.9.refs_2_
  25.8 0.6 %shard_map.92 = (f32[16,128]{1,0:T(8,128)}, bf16[4,4,512]{2,1,0:T(4,128)(2,1)}) custom-call(f32[16,128]{1,0:T(8,128)S(1)} %get-tuple-element.39.total_ref, f32[4,4,512]{2,1,0:T(4,128)S(1)} %get-tuple-element.30.kv_ref, f32[8,128]{1,0:T(8,128)S(1)} %get-tuple-element.42._, f32[32,128]{1,0:T(8,128)S(1)} %collective-permute-done.7.refs_0_, ...), custom_call_target="tpu_custom_call" | custom-call | tf_op jit(solution)/shard_map/pallas_call | solution.py:27
  (2 shorter events, 0.0 us)
Async XLA Ops:
  0.6 5.8 %copy-start = (bf16[8192,512]{1,0:T(8,128)(2,1)S(1)}, bf16[8192,512]{1,0:T(8,128)(2,1)}, u32[]{:S(2)}) copy-start(bf16[8192,512]{1,0:T(8,128)(2,1)} %weight_ref.5) | copy-start | bytes 25165828
  0.6 5.8 %copy-start.2 = (f32[8192]{0:T(1024)S(1)}, f32[8192]{0:T(1024)}, u32[]{:S(2)}) copy-start(f32[8192]{0:T(1024)} %param.9) | copy-start | bytes 98308
  0.7 5.8 %copy-start.3 = (f32[8192]{0:T(1024)S(1)}, f32[8192]{0:T(1024)}, u32[]{:S(2)}) copy-start(f32[8192]{0:T(1024)} %param.8) | copy-start | bytes 98308
  0.7 5.8 %copy-start.1 = (bf16[1,1,4,4,8192]{4,3,2,1,0:T(4,128)(2,1)S(1)}, bf16[1,1,4,4,8192]{4,3,2,1,0:T(4,128)(2,1)}, u32[]{:S(2)}) copy-start(bf16[1,1,4,4,8192]{4,3,2,1,0:T(4,128)(2,1)} %param.6) | copy-start | bytes 786436
  0.7 7.4 %collective-permute-start.2 = (bf16[4,4,512]{2,1,0:T(4,128)(2,1)}, bf16[4,4,512]{2,1,0:T(4,128)(2,1)S(1)}, u32[]{:S(2)}, u32[]{:S(2)}) collective-permute-start(bf16[4,4,512]{2,1,0:T(4,128)(2,1)} %bitcast.17), channel_id=1, source_target_pairs={{0,24},{8,16},{16,8},{24,0},{1,25},{9,17},{17,9},{25,1},{2,26},{10... | collective-permute-start | bytes 49160 | tf_op jit(solution)/shard_map/ppermute | solution.py:23
  5.8 4.8 %collective-permute-start.1 = (bf16[4,4,512]{2,1,0:T(4,128)(2,1)}, bf16[4,4,512]{2,1,0:T(4,128)(2,1)S(1)}, u32[]{:S(2)}, u32[]{:S(2)}) collective-permute-start(bf16[4,4,512]{2,1,0:T(4,128)(2,1)} %bitcast.18), channel_id=1, source_target_pairs={{0,16},{8,24},{16,0},{24,8},{1,17},{9,25},{17,1},{25,9},{2,18},{10... | collective-permute-start | bytes 49160 | tf_op jit(solution)/shard_map/ppermute | solution.py:23
  5.8 4.8 %collective-permute-start = (bf16[4,4,512]{2,1,0:T(4,128)(2,1)}, bf16[4,4,512]{2,1,0:T(4,128)(2,1)S(1)}, u32[]{:S(2)}, u32[]{:S(2)}) collective-permute-start(bf16[4,4,512]{2,1,0:T(4,128)(2,1)} %bitcast.19), channel_id=1, source_target_pairs={{0,8},{8,0},{16,24},{24,16},{1,9},{9,1},{17,25},{25,17},{2,10},{10... | collective-permute-start | bytes 49160 | tf_op jit(solution)/shard_map/ppermute | solution.py:23
  6.4 4.2 %copy-start.4 = (bf16[1,1,4,4,512]{4,3,2,1,0:T(4,128)(2,1)S(1)}, bf16[1,1,4,4,512]{4,3,2,1,0:T(4,128)(2,1)}, u32[]{:S(2)}) copy-start(bf16[1,1,4,4,512]{4,3,2,1,0:T(4,128)(2,1)} %param.11) | copy-start | bytes 49156
  6.4 4.2 %copy-start.5 = (s32[1,1,4]{2,1,0:T(1,128)S(1)}, s32[1,1,4]{2,1,0:T(1,128)}, u32[]{:S(2)}) copy-start(s32[1,1,4]{2,1,0:T(1,128)} %param.7) | copy-start | bytes 52
  11.4 1.6 %collective-permute-start.3 = (f32[16,4480]{1,0:T(8,128)S(1)}, f32[16,4480]{1,0:T(8,128)S(1)}, u32[]{:S(2)}, u32[]{:S(2)}) collective-permute-start(f32[16,4480]{1,0:T(8,128)S(1)} %get-tuple-element.31), channel_id=1, source_target_pairs={{0,1},{1,0},{2,3},{3,2},{4,5},{5,4},{6,7},{7,6},{8,9},{9,8},{10,11... | collective-permute-start | bytes 860168 | tf_op jit(solution)/shard_map/ppermute | solution.py:23
  13.1 6.4 %collective-permute-start.4 = (bf16[16,4608]{1,0:T(8,128)(2,1)S(1)}, bf16[16,4608]{1,0:T(8,128)(2,1)S(1)}, u32[]{:S(2)}, u32[]{:S(2)}) collective-permute-start(bf16[16,4608]{1,0:T(8,128)(2,1)S(1)} %get-tuple-element.37), channel_id=1, source_target_pairs={{0,3},{1,2},{2,1},{3,0},{4,7},{5,6},{6,5},{7,4},{8,11},{9,10},{10,... | collective-permute-start | bytes 442376 | tf_op jit(solution)/shard_map/ppermute | solution.py:23
  14.5 4.1 %collective-permute-start.5 = (f32[16,128]{1,0:T(8,128)S(1)}, f32[16,128]{1,0:T(8,128)S(1)}, u32[]{:S(2)}, u32[]{:S(2)}) collective-permute-start(f32[16,128]{1,0:T(8,128)S(1)} %get-tuple-element.38), channel_id=1, source_target_pairs={{0,7},{1,6},{2,5},{3,4},{4,3},{5,2},{6,1},{7,0},{8,15},{9,14},{10,... | collective-permute-start | bytes 24584 | tf_op jit(solution)/shard_map/ppermute | solution.py:23
  15.8 3.7 %collective-permute-start.6 = (f32[16,128]{1,0:T(8,128)S(1)}, f32[16,128]{1,0:T(8,128)S(1)}, u32[]{:S(2)}, u32[]{:S(2)}) collective-permute-start(f32[16,128]{1,0:T(8,128)S(1)} %get-tuple-element.36.sum_ref), channel_id=1, source_target_pairs={{0,4},{1,5},{2,6},{3,7},{4,0},{5,1},{6,2},{7,3},{8,12},{9,13},{10,... | collective-permute-start | bytes 24584 | tf_op jit(solution)/shard_map/ppermute | solution.py:23
  19.5 5.8 %collective-permute-start.7 = (f32[32,128]{1,0:T(8,128)S(1)}, f32[32,128]{1,0:T(8,128)S(1)}, u32[]{:S(2)}, u32[]{:S(2)}) collective-permute-start(f32[32,128]{1,0:T(8,128)S(1)} %get-tuple-element.43), channel_id=1, source_target_pairs={{0,24},{8,16},{16,8},{24,0},{1,25},{9,17},{17,9},{25,1},{2,26},{10... | collective-permute-start | bytes 49160 | tf_op jit(solution)/shard_map/ppermute | solution.py:23
  21.1 4.7 %collective-permute-start.8 = (f32[32,128]{1,0:T(8,128)S(1)}, f32[32,128]{1,0:T(8,128)S(1)}, u32[]{:S(2)}, u32[]{:S(2)}) collective-permute-start(f32[32,128]{1,0:T(8,128)S(1)} %get-tuple-element.44), channel_id=1, source_target_pairs={{0,16},{8,24},{16,0},{24,8},{1,17},{9,25},{17,1},{25,9},{2,18},{10... | collective-permute-start | bytes 49160 | tf_op jit(solution)/shard_map/ppermute | solution.py:23
  21.7 4.2 %collective-permute-start.9 = (f32[32,128]{1,0:T(8,128)S(1)}, f32[32,128]{1,0:T(8,128)S(1)}, u32[]{:S(2)}, u32[]{:S(2)}) collective-permute-start(f32[32,128]{1,0:T(8,128)S(1)} %get-tuple-element.45), channel_id=1, source_target_pairs={{0,8},{8,0},{16,24},{24,16},{1,9},{9,1},{17,25},{25,17},{2,10},{10... | collective-permute-start | bytes 49160 | tf_op jit(solution)/shard_map/ppermute | solution.py:23

commit v12 on v11

--- a/solution.py
+++ b/solution.py
@@ -10,7 +10,7 @@
 LANES = 128
 PIECES = 3
 TERMS = 2
-STEPS = 8
+STEPS = 4
 TURNED = 2
 VMEM = pl.BlockSpec(memory_space=pltpu.VMEM)
 HBM = pl.BlockSpec(memory_space=pltpu.HBM)

time: 26.6 us -> 26.6 us (level)
  no operation moved by 1% of the time
where the time goes in v12:
time: 26.6 us; the launch traced here: 26.5 us
  starting transfers between devices  13.5 us (51%)
  waiting for transfers between devices  7.12 us (27%)
  Pallas kernels  5.06 us (19%)
  between operations  0.73 us (3%)
    ppermute x10, starting transfers between devices, swap(): return lax.ppermute(x, axis, [(i, i ^ k) for i in range(n)])  13.5 us
    ppermute x10, waiting for transfers between devices, swap(): return lax.ppermute(x, axis, [(i, i ^ k) for i in range(n)])  7.12 us
    pallas_call x8, Pallas kernels, call(): pl.pallas_call(kernel, out_shape=tuple(outs), in_specs=specs or [VMEM] *...  5.06 us
  transfers between devices with their start and end apart: 10, of which 7 were waited for; matrix products, arithmetic and copies ran while one was open for 0% of the time, Pallas kernels for 14%

profile of v12, /device:TPU:0, one launch (start us, length us, event | category | flops | bytes accessed | tf_op | source)
XLA Modules:
  0.0 26.5 jit_solution(10287742415830678336)
XLA Ops:
  0.6 0.0 copy-start
  0.6 0.0 copy-start.2
  0.7 0.0 copy-start.3
  0.7 0.0 copy-start.1
  0.7 5.1 %collective-permute-start.2 = (bf16[4,4,512]{2,1,0:T(4,128)(2,1)}, bf16[4,4,512]{2,1,0:T(4,128)(2,1)S(1)}, u32[]{:S(2)}, u32[]{:S(2)}) collective-permute-start(bf16[4,4,512]{2,1,0:T(4,128)(2,1)} %bitcast.17), channel_id=1, source_target_pairs={{0,24},{8,16},{16,8},{24,0},{1,25},{9,17},{17,9},{25,1},{2,26},{10... | collective-permute-start | bytes 49160 | tf_op jit(solution)/shard_map/ppermute | solution.py:23
  5.8 0.0 collective-permute-start.1
  5.8 0.6 %collective-permute-start = (bf16[4,4,512]{2,1,0:T(4,128)(2,1)}, bf16[4,4,512]{2,1,0:T(4,128)(2,1)S(1)}, u32[]{:S(2)}, u32[]{:S(2)}) collective-permute-start(bf16[4,4,512]{2,1,0:T(4,128)(2,1)} %bitcast.19), channel_id=1, source_target_pairs={{0,8},{8,0},{16,24},{24,16},{1,9},{9,1},{17,25},{25,17},{2,10},{10... | collective-permute-start | bytes 49160 | tf_op jit(solution)/shard_map/ppermute | solution.py:23
  6.4 0.0 copy-start.4
  6.4 0.0 copy-start.5
  6.4 0.0 copy-done
  6.4 0.0 copy-done.2
  6.5 0.0 copy-done.3
  6.5 0.0 copy-done.1
  6.5 1.6 %shard_map.86 = (f32[16,512]{1,0:T(8,128)S(1)}, f32[16,128]{1,0:T(8,128)S(1)}, bf16[2,512,2048]{2,1,0:T(8,128)(2,1)S(1)}, f32[16,8192]{1,0:T(8,128)S(1)}) custom-call(bf16[4,4,8192]{2,1,0:T(4,128)(2,1)S(1)} %bitcast.9, f32[1,8192]{1,0:T(1,128)S(1)} %bitcast.16, f32[1,8192]{1,0:T(1,128)S(1)} %bitcast.11, bf16[8192,512]{1,0:T(8,128)(2,1)S(1)} %copy-done, ...), custom_call_target="tpu_custom_call" | custom-call | tf_op jit(solution)/shard_map/pallas_call | solution.py:27
  8.0 0.0 collective-permute-done.2.refs_3_
  8.0 2.6 %collective-permute-done.1.refs_2_ = bf16[4,4,512]{2,1,0:T(4,128)(2,1)S(1)} collective-permute-done((bf16[4,4,512]{2,1,0:T(4,128)(2,1)}, bf16[4,4,512]{2,1,0:T(4,128)(2,1)S(1)}, u32[]{:S(2)}, u32[]{:S(2)}) %collective-permute-start.1) | collective-permute-done | bytes 16416 | tf_op jit(solution)/shard_map/ppermute | solution.py:23
  10.6 0.0 collective-permute-done.refs_1_
  10.6 0.0 copy-done.4
  10.6 0.0 copy-done.5
  10.6 0.7 %shard_map.87 = (f32[4,4,512]{2,1,0:T(4,128)S(1)}, f32[16,128]{1,0:T(8,128)S(1)}, bf16[16,512]{1,0:T(8,128)(2,1)S(1)}, f32[16,4480]{1,0:T(8,128)S(1)}) custom-call(s32[1,4]{1,0:T(1,128)S(1)} %bitcast.21, f32[16,512]{1,0:T(8,128)S(1)} %get-tuple-element.26.projected_ref, bf16[2,512,2048]{2,1,0:T(8,128)(2,1)S(1)} %get-tuple-element.27.turned_ref, ...), custom_call_target="tpu_custom_call" | custom-call | tf_op jit(solution)/shard_map/pallas_call | solution.py:27
  11.4 0.1 collective-permute-start.3
  11.5 1.2 %shard_map.88 = (f32[16,4096]{1,0:T(8,128)S(1)}, f32[32,128]{1,0:T(8,128)S(1)}) custom-call(bf16[16,512]{1,0:T(8,128)(2,1)S(1)} %get-tuple-element.32.lhs_ref, bf16[8192,512]{1,0:T(8,128)(2,1)S(1)} %copy-done, f32[16,8192]{1,0:T(8,128)S(1)} %get-tuple-element.28.rows_ref, f32[1,8192]{1,0:T(1,128)S(1)} %bitcast.13, f32[16,128]{1,0:T(8,128)S(1)} %get-tuple-element.29.inv_ref, ...), custom_call_target="tpu_custom_call" | custom-call | tf_op jit(solution)/shard_map/pallas_call | solution.py:27
  12.7 0.3 %collective-permute-done.3.got_ref = f32[16,4480]{1,0:T(8,128)S(1)} collective-permute-done((f32[16,4480]{1,0:T(8,128)S(1)}, f32[16,4480]{1,0:T(8,128)S(1)}, u32[]{:S(2)}, u32[]{:S(2)}) %collective-permute-start.3) | collective-permute-done | bytes 286752 | tf_op jit(solution)/shard_map/ppermute | solution.py:23
  13.0 0.1 shard_map.89
  13.1 1.3 %collective-permute-start.4 = (bf16[16,4608]{1,0:T(8,128)(2,1)S(1)}, bf16[16,4608]{1,0:T(8,128)(2,1)S(1)}, u32[]{:S(2)}, u32[]{:S(2)}) collective-permute-start(bf16[16,4608]{1,0:T(8,128)(2,1)S(1)} %get-tuple-element.37), channel_id=1, source_target_pairs={{0,3},{1,2},{2,1},{3,0},{4,7},{5,6},{6,5},{7,4},{8,11},{9,10},{10,... | collective-permute-start | bytes 442376 | tf_op jit(solution)/shard_map/ppermute | solution.py:23
  14.5 1.4 %collective-permute-start.5 = (f32[16,128]{1,0:T(8,128)S(1)}, f32[16,128]{1,0:T(8,128)S(1)}, u32[]{:S(2)}, u32[]{:S(2)}) collective-permute-start(f32[16,128]{1,0:T(8,128)S(1)} %get-tuple-element.38), channel_id=1, source_target_pairs={{0,7},{1,6},{2,5},{3,4},{4,3},{5,2},{6,1},{7,0},{8,15},{9,14},{10,... | collective-permute-start | bytes 24584 | tf_op jit(solution)/shard_map/ppermute | solution.py:23
  15.8 0.5 %collective-permute-start.6 = (f32[16,128]{1,0:T(8,128)S(1)}, f32[16,128]{1,0:T(8,128)S(1)}, u32[]{:S(2)}, u32[]{:S(2)}) collective-permute-start(f32[16,128]{1,0:T(8,128)S(1)} %get-tuple-element.36.sum_ref), channel_id=1, source_target_pairs={{0,4},{1,5},{2,6},{3,7},{4,0},{5,1},{6,2},{7,3},{8,12},{9,13},{10,... | collective-permute-start | bytes 24584 | tf_op jit(solution)/shard_map/ppermute | solution.py:23
  16.4 2.2 %collective-permute-done.5.refs_1_ = f32[16,128]{1,0:T(8,128)S(1)} collective-permute-done((f32[16,128]{1,0:T(8,128)S(1)}, f32[16,128]{1,0:T(8,128)S(1)}, u32[]{:S(2)}, u32[]{:S(2)}) %collective-permute-start.5) | collective-permute-done | bytes 8224 | tf_op jit(solution)/shard_map/ppermute | solution.py:23
  18.5 0.9 %collective-permute-done.6.refs_2_ = f32[16,128]{1,0:T(8,128)S(1)} collective-permute-done((f32[16,128]{1,0:T(8,128)S(1)}, f32[16,128]{1,0:T(8,128)S(1)}, u32[]{:S(2)}, u32[]{:S(2)}) %collective-permute-start.6) | collective-permute-done | bytes 8224 | tf_op jit(solution)/shard_map/ppermute | solution.py:23
  19.5 0.0 collective-permute-done.4.refs_0_
  19.5 1.6 %collective-permute-start.7 = (f32[32,128]{1,0:T(8,128)S(1)}, f32[32,128]{1,0:T(8,128)S(1)}, u32[]{:S(2)}, u32[]{:S(2)}) collective-permute-start(f32[32,128]{1,0:T(8,128)S(1)} %get-tuple-element.43), channel_id=1, source_target_pairs={{0,24},{8,16},{16,8},{24,0},{1,25},{9,17},{17,9},{25,1},{2,26},{10... | collective-permute-start | bytes 49160 | tf_op jit(solution)/shard_map/ppermute | solution.py:23
  21.1 0.6 %collective-permute-start.8 = (f32[32,128]{1,0:T(8,128)S(1)}, f32[32,128]{1,0:T(8,128)S(1)}, u32[]{:S(2)}, u32[]{:S(2)}) collective-permute-start(f32[32,128]{1,0:T(8,128)S(1)} %get-tuple-element.44), channel_id=1, source_target_pairs={{0,16},{8,24},{16,0},{24,8},{1,17},{9,25},{17,1},{25,9},{2,18},{10... | collective-permute-start | bytes 49160 | tf_op jit(solution)/shard_map/ppermute | solution.py:23
  21.7 2.3 %collective-permute-start.9 = (f32[32,128]{1,0:T(8,128)S(1)}, f32[32,128]{1,0:T(8,128)S(1)}, u32[]{:S(2)}, u32[]{:S(2)}) collective-permute-start(f32[32,128]{1,0:T(8,128)S(1)} %get-tuple-element.45), channel_id=1, source_target_pairs={{0,8},{8,0},{16,24},{24,16},{1,9},{9,1},{17,25},{25,17},{2,10},{10... | collective-permute-start | bytes 49160 | tf_op jit(solution)/shard_map/ppermute | solution.py:23
  23.9 0.8 %shard_map.91 = (bf16[4,4,2048]{2,1,0:T(4,128)(2,1)}, f32[8,128]{1,0:T(8,128)S(1)}) custom-call(f32[16,8192]{1,0:T(8,128)S(1)} %get-tuple-element.28.rows_ref, f32[1,8192]{1,0:T(1,128)S(1)} %bitcast.14, f32[16,128]{1,0:T(8,128)S(1)} %get-tuple-element.29.inv_ref, f32[16,128]{1,0:T(8,128)S(1)} %get-tuple-element.40.dots_ref, ...), custom_call_target="tpu_custom_call" | custom-call | tf_op jit(solution)/shard_map/pallas_call | solution.py:27
  24.8 0.5 %collective-permute-done.7.refs_0_ = f32[32,128]{1,0:T(8,128)S(1)} collective-permute-done((f32[32,128]{1,0:T(8,128)S(1)}, f32[32,128]{1,0:T(8,128)S(1)}, u32[]{:S(2)}, u32[]{:S(2)}) %collective-permute-start.7) | collective-permute-done | bytes 16416 | tf_op jit(solution)/shard_map/ppermute | solution.py:23
  25.3 0.5 %collective-permute-done.8.refs_1_ = f32[32,128]{1,0:T(8,128)S(1)} collective-permute-done((f32[32,128]{1,0:T(8,128)S(1)}, f32[32,128]{1,0:T(8,128)S(1)}, u32[]{:S(2)}, u32[]{:S(2)}) %collective-permute-start.8) | collective-permute-done | bytes 16416 | tf_op jit(solution)/shard_map/ppermute | solution.py:23
  25.7 0.1 collective-permute-done.9.refs_2_
  25.8 0.6 %shard_map.92 = (f32[16,128]{1,0:T(8,128)}, bf16[4,4,512]{2,1,0:T(4,128)(2,1)}) custom-call(f32[16,128]{1,0:T(8,128)S(1)} %get-tuple-element.39.total_ref, f32[4,4,512]{2,1,0:T(4,128)S(1)} %get-tuple-element.30.kv_ref, f32[8,128]{1,0:T(8,128)S(1)} %get-tuple-element.42._, f32[32,128]{1,0:T(8,128)S(1)} %collective-permute-done.7.refs_0_, ...), custom_call_target="tpu_custom_call" | custom-call | tf_op jit(solution)/shard_map/pallas_call | solution.py:27
  (2 shorter events, 0.0 us)
Async XLA Ops:
  0.6 5.8 %copy-start = (bf16[8192,512]{1,0:T(8,128)(2,1)S(1)}, bf16[8192,512]{1,0:T(8,128)(2,1)}, u32[]{:S(2)}) copy-start(bf16[8192,512]{1,0:T(8,128)(2,1)} %weight_ref.5) | copy-start | bytes 25165828
  0.6 5.8 %copy-start.2 = (f32[8192]{0:T(1024)S(1)}, f32[8192]{0:T(1024)}, u32[]{:S(2)}) copy-start(f32[8192]{0:T(1024)} %param.9) | copy-start | bytes 98308
  0.7 5.8 %copy-start.3 = (f32[8192]{0:T(1024)S(1)}, f32[8192]{0:T(1024)}, u32[]{:S(2)}) copy-start(f32[8192]{0:T(1024)} %param.8) | copy-start | bytes 98308
  0.7 5.8 %copy-start.1 = (bf16[1,1,4,4,8192]{4,3,2,1,0:T(4,128)(2,1)S(1)}, bf16[1,1,4,4,8192]{4,3,2,1,0:T(4,128)(2,1)}, u32[]{:S(2)}) copy-start(bf16[1,1,4,4,8192]{4,3,2,1,0:T(4,128)(2,1)} %param.6) | copy-start | bytes 786436
  0.7 7.4 %collective-permute-start.2 = (bf16[4,4,512]{2,1,0:T(4,128)(2,1)}, bf16[4,4,512]{2,1,0:T(4,128)(2,1)S(1)}, u32[]{:S(2)}, u32[]{:S(2)}) collective-permute-start(bf16[4,4,512]{2,1,0:T(4,128)(2,1)} %bitcast.17), channel_id=1, source_target_pairs={{0,24},{8,16},{16,8},{24,0},{1,25},{9,17},{17,9},{25,1},{2,26},{10... | collective-permute-start | bytes 49160 | tf_op jit(solution)/shard_map/ppermute | solution.py:23
  5.8 4.8 %collective-permute-start.1 = (bf16[4,4,512]{2,1,0:T(4,128)(2,1)}, bf16[4,4,512]{2,1,0:T(4,128)(2,1)S(1)}, u32[]{:S(2)}, u32[]{:S(2)}) collective-permute-start(bf16[4,4,512]{2,1,0:T(4,128)(2,1)} %bitcast.18), channel_id=1, source_target_pairs={{0,16},{8,24},{16,0},{24,8},{1,17},{9,25},{17,1},{25,9},{2,18},{10... | collective-permute-start | bytes 49160 | tf_op jit(solution)/shard_map/ppermute | solution.py:23
  5.8 4.8 %collective-permute-start = (bf16[4,4,512]{2,1,0:T(4,128)(2,1)}, bf16[4,4,512]{2,1,0:T(4,128)(2,1)S(1)}, u32[]{:S(2)}, u32[]{:S(2)}) collective-permute-start(bf16[4,4,512]{2,1,0:T(4,128)(2,1)} %bitcast.19), channel_id=1, source_target_pairs={{0,8},{8,0},{16,24},{24,16},{1,9},{9,1},{17,25},{25,17},{2,10},{10... | collective-permute-start | bytes 49160 | tf_op jit(solution)/shard_map/ppermute | solution.py:23
  6.4 4.2 %copy-start.4 = (bf16[1,1,4,4,512]{4,3,2,1,0:T(4,128)(2,1)S(1)}, bf16[1,1,4,4,512]{4,3,2,1,0:T(4,128)(2,1)}, u32[]{:S(2)}) copy-start(bf16[1,1,4,4,512]{4,3,2,1,0:T(4,128)(2,1)} %param.11) | copy-start | bytes 49156
  6.4 4.2 %copy-start.5 = (s32[1,1,4]{2,1,0:T(1,128)S(1)}, s32[1,1,4]{2,1,0:T(1,128)}, u32[]{:S(2)}) copy-start(s32[1,1,4]{2,1,0:T(1,128)} %param.7) | copy-start | bytes 52
  11.4 1.6 %collective-permute-start.3 = (f32[16,4480]{1,0:T(8,128)S(1)}, f32[16,4480]{1,0:T(8,128)S(1)}, u32[]{:S(2)}, u32[]{:S(2)}) collective-permute-start(f32[16,4480]{1,0:T(8,128)S(1)} %get-tuple-element.31), channel_id=1, source_target_pairs={{0,1},{1,0},{2,3},{3,2},{4,5},{5,4},{6,7},{7,6},{8,9},{9,8},{10,11... | collective-permute-start | bytes 860168 | tf_op jit(solution)/shard_map/ppermute | solution.py:23
  13.1 6.4 %collective-permute-start.4 = (bf16[16,4608]{1,0:T(8,128)(2,1)S(1)}, bf16[16,4608]{1,0:T(8,128)(2,1)S(1)}, u32[]{:S(2)}, u32[]{:S(2)}) collective-permute-start(bf16[16,4608]{1,0:T(8,128)(2,1)S(1)} %get-tuple-element.37), channel_id=1, source_target_pairs={{0,3},{1,2},{2,1},{3,0},{4,7},{5,6},{6,5},{7,4},{8,11},{9,10},{10,... | collective-permute-start | bytes 442376 | tf_op jit(solution)/shard_map/ppermute | solution.py:23
  14.5 4.1 %collective-permute-start.5 = (f32[16,128]{1,0:T(8,128)S(1)}, f32[16,128]{1,0:T(8,128)S(1)}, u32[]{:S(2)}, u32[]{:S(2)}) collective-permute-start(f32[16,128]{1,0:T(8,128)S(1)} %get-tuple-element.38), channel_id=1, source_target_pairs={{0,7},{1,6},{2,5},{3,4},{4,3},{5,2},{6,1},{7,0},{8,15},{9,14},{10,... | collective-permute-start | bytes 24584 | tf_op jit(solution)/shard_map/ppermute | solution.py:23
  15.8 3.7 %collective-permute-start.6 = (f32[16,128]{1,0:T(8,128)S(1)}, f32[16,128]{1,0:T(8,128)S(1)}, u32[]{:S(2)}, u32[]{:S(2)}) collective-permute-start(f32[16,128]{1,0:T(8,128)S(1)} %get-tuple-element.36.sum_ref), channel_id=1, source_target_pairs={{0,4},{1,5},{2,6},{3,7},{4,0},{5,1},{6,2},{7,3},{8,12},{9,13},{10,... | collective-permute-start | bytes 24584 | tf_op jit(solution)/shard_map/ppermute | solution.py:23
  19.5 5.8 %collective-permute-start.7 = (f32[32,128]{1,0:T(8,128)S(1)}, f32[32,128]{1,0:T(8,128)S(1)}, u32[]{:S(2)}, u32[]{:S(2)}) collective-permute-start(f32[32,128]{1,0:T(8,128)S(1)} %get-tuple-element.43), channel_id=1, source_target_pairs={{0,24},{8,16},{16,8},{24,0},{1,25},{9,17},{17,9},{25,1},{2,26},{10... | collective-permute-start | bytes 49160 | tf_op jit(solution)/shard_map/ppermute | solution.py:23
  21.1 4.7 %collective-permute-start.8 = (f32[32,128]{1,0:T(8,128)S(1)}, f32[32,128]{1,0:T(8,128)S(1)}, u32[]{:S(2)}, u32[]{:S(2)}) collective-permute-start(f32[32,128]{1,0:T(8,128)S(1)} %get-tuple-element.44), channel_id=1, source_target_pairs={{0,16},{8,24},{16,0},{24,8},{1,17},{9,25},{17,1},{25,9},{2,18},{10... | collective-permute-start | bytes 49160 | tf_op jit(solution)/shard_map/ppermute | solution.py:23
  21.7 4.2 %collective-permute-start.9 = (f32[32,128]{1,0:T(8,128)S(1)}, f32[32,128]{1,0:T(8,128)S(1)}, u32[]{:S(2)}, u32[]{:S(2)}) collective-permute-start(f32[32,128]{1,0:T(8,128)S(1)} %get-tuple-element.45), channel_id=1, source_target_pairs={{0,8},{8,0},{16,24},{24,16},{1,9},{9,1},{17,25},{25,17},{2,10},{10... | collective-permute-start | bytes 49160 | tf_op jit(solution)/shard_map/ppermute | solution.py:23

commit v13 on v11

--- a/solution.py
+++ b/solution.py
@@ -137,8 +137,8 @@
 
 def sent_kernel(enc, tp, counts_ref, projected_ref, turned_ref, weight_ref, rows_ref, gain_ref, inv_ref, *refs):
     cots = refs[:enc]
-    kv_ref, dots_ref, lhs_ref, send_ref, sums_ref = refs[enc:]
-    buckets, capacity, columns = kv_ref.shape
+    dots_ref, lhs_ref, send_ref, sums_ref = refs[enc:]
+    buckets, capacity, columns = cots[0].shape
     me = lax.axis_index("enc")
     slot = lax.broadcasted_iota(jnp.int32, (capacity, columns), 0)
     blocks = [cot[me].astype(F32) for cot in cots]
@@ -149,7 +149,6 @@
             block = jnp.where((me ^ k) == q, blocks[k], block)
         live = slot < counts_ref[:, q : q + 1]
         parts.append(jnp.where(live, block, 0.0))
-        kv_ref[q] = jnp.where(live, projected_ref[q * capacity : (q + 1) * capacity, :], 0.0)
     masked = jnp.concatenate(parts, axis=0)
     lhs = masked.astype(BF16)
     lhs_ref[...] = lhs
@@ -173,7 +172,7 @@
     put_side(send_ref, half, dots_ref[...], sums_ref[...])
 
 
-def kept_kernel(tp, lhs_ref, weight_ref, rows_ref, gain_ref, inv_ref, dots_ref, kept_ref, sums_ref):
+def kept_kernel(tp, counts_ref, projected_ref, lhs_ref, weight_ref, rows_ref, gain_ref, inv_ref, dots_ref, kept_ref, sums_ref, kv_ref):
     width = rows_ref.shape[1] // tp
     chunks = width // LANES
     steps = [kept(j) for j in range(tp // 2)]
@@ -183,6 +182,11 @@
         row = row_sum(k, tp, term, rows_ref, gain_ref, inv_ref[:, :1], dots_ref[:, :1])
         for i in range(chunks):
             sums_ref[j * chunks + i : j * chunks + i + 1, :] = row[:, i * LANES : (i + 1) * LANES]
+    buckets, capacity, columns = kv_ref.shape
+    slot = lax.broadcasted_iota(jnp.int32, (capacity, columns), 0)
+    for q in range(buckets):
+        part = projected_ref[q * capacity : (q + 1) * capacity, :]
+        kv_ref[q] = jnp.where(slot < counts_ref[:, q : q + 1], part, 0.0)
 
 
 def fold_kernel(width, got_ref, kept_ref, dots_ref, sums_ref, all_ref, own_ref, *refs):
@@ -295,10 +299,9 @@
     )
     own_cot = cot
     cots = [own_cot] + [swap(cot, "enc", k) for k in range(1, enc)]
-    kv, dots, lhs, send = run(
+    dots, lhs, send = run(
         part(sent_kernel, enc, tp),
         (
-            struct((buckets, capacity, columns), F32),
             struct((rows, LANES), F32),
             struct((rows, columns), BF16),
             struct((rows, half + side(pairs * chunks, rows, F32)), F32),
@@ -307,10 +310,14 @@
         scratch=[pltpu.VMEM((pairs * chunks, LANES), F32)],
     )
     got = swap(send, "tp", 1)
-    terms, sums = run(
+    terms, sums, kv = run(
         part(kept_kernel, tp),
-        (struct((rows, half), F32), struct((pairs * chunks, LANES), F32)),
-        (lhs, kv_weight, inputs, gain, inv_rms, dots),
+        (
+            struct((rows, half), F32),
+            struct((pairs * chunks, LANES), F32),
+            struct((buckets, capacity, columns), F32),
+        ),
+        (counts[0], projected, lhs, kv_weight, inputs, gain, inv_rms, dots),
     )
     dots, own, *refs = run(
         part(fold_kernel, width),

time: 26.6 us -> 26.6 us (level)
  no operation moved by 1% of the time
where the time goes in v13:
time: 26.6 us; the launch traced here: 26.5 us
  starting transfers between devices  13.5 us (51%)
  waiting for transfers between devices  7.12 us (27%)
  Pallas kernels  5.06 us (19%)
  between operations  0.73 us (3%)
    ppermute x10, starting transfers between devices, swap(): return lax.ppermute(x, axis, [(i, i ^ k) for i in range(n)])  13.5 us
    ppermute x10, waiting for transfers between devices, swap(): return lax.ppermute(x, axis, [(i, i ^ k) for i in range(n)])  7.12 us
    pallas_call x8, Pallas kernels, call(): pl.pallas_call(kernel, out_shape=tuple(outs), in_specs=specs or [VMEM] *...  5.06 us
  transfers between devices with their start and end apart: 10, of which 7 were waited for; matrix products, arithmetic and copies ran while one was open for 0% of the time, Pallas kernels for 14%

profile of v13, /device:TPU:0, one launch (start us, length us, event | category | flops | bytes accessed | tf_op | source)
XLA Modules:
  0.0 26.5 jit_solution(7576143860299640147)
XLA Ops:
  0.6 0.0 copy-start
  0.6 0.0 copy-start.2
  0.7 0.0 copy-start.3
  0.7 0.0 copy-start.1
  0.7 5.1 %collective-permute-start.2 = (bf16[4,4,512]{2,1,0:T(4,128)(2,1)}, bf16[4,4,512]{2,1,0:T(4,128)(2,1)S(1)}, u32[]{:S(2)}, u32[]{:S(2)}) collective-permute-start(bf16[4,4,512]{2,1,0:T(4,128)(2,1)} %bitcast.17), channel_id=1, source_target_pairs={{0,24},{8,16},{16,8},{24,0},{1,25},{9,17},{17,9},{25,1},{2,26},{10... | collective-permute-start | bytes 49160 | tf_op jit(solution)/shard_map/ppermute | solution.py:23
  5.8 0.0 collective-permute-start.1
  5.8 0.6 %collective-permute-start = (bf16[4,4,512]{2,1,0:T(4,128)(2,1)}, bf16[4,4,512]{2,1,0:T(4,128)(2,1)S(1)}, u32[]{:S(2)}, u32[]{:S(2)}) collective-permute-start(bf16[4,4,512]{2,1,0:T(4,128)(2,1)} %bitcast.19), channel_id=1, source_target_pairs={{0,8},{8,0},{16,24},{24,16},{1,9},{9,1},{17,25},{25,17},{2,10},{10... | collective-permute-start | bytes 49160 | tf_op jit(solution)/shard_map/ppermute | solution.py:23
  6.4 0.0 copy-start.4
  6.4 0.0 copy-start.5
  6.4 0.0 copy-done
  6.4 0.0 copy-done.2
  6.5 0.0 copy-done.3
  6.5 0.0 copy-done.1
  6.5 1.6 %shard_map.86 = (f32[16,512]{1,0:T(8,128)S(1)}, f32[16,128]{1,0:T(8,128)S(1)}, bf16[2,512,2048]{2,1,0:T(8,128)(2,1)S(1)}, f32[16,8192]{1,0:T(8,128)S(1)}) custom-call(bf16[4,4,8192]{2,1,0:T(4,128)(2,1)S(1)} %bitcast.9, f32[1,8192]{1,0:T(1,128)S(1)} %bitcast.16, f32[1,8192]{1,0:T(1,128)S(1)} %bitcast.11, bf16[8192,512]{1,0:T(8,128)(2,1)S(1)} %copy-done, ...), custom_call_target="tpu_custom_call" | custom-call | tf_op jit(solution)/shard_map/pallas_call | solution.py:27
  8.0 0.0 collective-permute-done.2.refs_3_
  8.0 2.6 %collective-permute-done.1.refs_2_ = bf16[4,4,512]{2,1,0:T(4,128)(2,1)S(1)} collective-permute-done((bf16[4,4,512]{2,1,0:T(4,128)(2,1)}, bf16[4,4,512]{2,1,0:T(4,128)(2,1)S(1)}, u32[]{:S(2)}, u32[]{:S(2)}) %collective-permute-start.1) | collective-permute-done | bytes 16416 | tf_op jit(solution)/shard_map/ppermute | solution.py:23
  10.6 0.0 collective-permute-done.refs_1_
  10.6 0.0 copy-done.4
  10.6 0.0 copy-done.5
  10.6 0.7 %shard_map.87 = (f32[16,128]{1,0:T(8,128)S(1)}, bf16[16,512]{1,0:T(8,128)(2,1)S(1)}, f32[16,4480]{1,0:T(8,128)S(1)}) custom-call(s32[1,4]{1,0:T(1,128)S(1)} %bitcast.21, f32[16,512]{1,0:T(8,128)S(1)} %get-tuple-element.26.projected_ref, bf16[2,512,2048]{2,1,0:T(8,128)(2,1)S(1)} %get-tuple-element.27.turned_ref, bf16[8192,512]{1,0:T(8,128)(2,1)S(1)} %copy-done, ...), custom_call_target="tpu_custom_call" | custom-call | tf_op jit(solution)/shard_map/pallas_call | solution.py:27
  11.4 0.1 collective-permute-start.3
  11.5 1.2 %shard_map.88 = (f32[16,4096]{1,0:T(8,128)S(1)}, f32[32,128]{1,0:T(8,128)S(1)}, f32[4,4,512]{2,1,0:T(4,128)S(1)}) custom-call(s32[1,4]{1,0:T(1,128)S(1)} %bitcast.22, f32[16,512]{1,0:T(8,128)S(1)} %get-tuple-element.26.projected_ref, bf16[16,512]{1,0:T(8,128)(2,1)S(1)} %get-tuple-element.30.lhs_ref, bf16[8192,512]{1,0:T(8,128)(2,1)S(1)} %copy-done, ...), custom_call_target="tpu_custom_call" | custom-call | tf_op jit(solution)/shard_map/pallas_call | solution.py:27
  12.7 0.3 %collective-permute-done.3.got_ref = f32[16,4480]{1,0:T(8,128)S(1)} collective-permute-done((f32[16,4480]{1,0:T(8,128)S(1)}, f32[16,4480]{1,0:T(8,128)S(1)}, u32[]{:S(2)}, u32[]{:S(2)}) %collective-permute-start.3) | collective-permute-done | bytes 286752 | tf_op jit(solution)/shard_map/ppermute | solution.py:23
  13.0 0.1 shard_map.89
  13.1 1.3 %collective-permute-start.4 = (bf16[16,4608]{1,0:T(8,128)(2,1)S(1)}, bf16[16,4608]{1,0:T(8,128)(2,1)S(1)}, u32[]{:S(2)}, u32[]{:S(2)}) collective-permute-start(bf16[16,4608]{1,0:T(8,128)(2,1)S(1)} %get-tuple-element.37), channel_id=1, source_target_pairs={{0,3},{1,2},{2,1},{3,0},{4,7},{5,6},{6,5},{7,4},{8,11},{9,10},{10,... | collective-permute-start | bytes 442376 | tf_op jit(solution)/shard_map/ppermute | solution.py:23
  14.4 1.4 %collective-permute-start.5 = (f32[16,128]{1,0:T(8,128)S(1)}, f32[16,128]{1,0:T(8,128)S(1)}, u32[]{:S(2)}, u32[]{:S(2)}) collective-permute-start(f32[16,128]{1,0:T(8,128)S(1)} %get-tuple-element.38), channel_id=1, source_target_pairs={{0,7},{1,6},{2,5},{3,4},{4,3},{5,2},{6,1},{7,0},{8,15},{9,14},{10,... | collective-permute-start | bytes 24584 | tf_op jit(solution)/shard_map/ppermute | solution.py:23
  15.8 0.5 %collective-permute-start.6 = (f32[16,128]{1,0:T(8,128)S(1)}, f32[16,128]{1,0:T(8,128)S(1)}, u32[]{:S(2)}, u32[]{:S(2)}) collective-permute-start(f32[16,128]{1,0:T(8,128)S(1)} %get-tuple-element.36.sum_ref), channel_id=1, source_target_pairs={{0,4},{1,5},{2,6},{3,7},{4,0},{5,1},{6,2},{7,3},{8,12},{9,13},{10,... | collective-permute-start | bytes 24584 | tf_op jit(solution)/shard_map/ppermute | solution.py:23
  16.3 2.2 %collective-permute-done.5.refs_1_ = f32[16,128]{1,0:T(8,128)S(1)} collective-permute-done((f32[16,128]{1,0:T(8,128)S(1)}, f32[16,128]{1,0:T(8,128)S(1)}, u32[]{:S(2)}, u32[]{:S(2)}) %collective-permute-start.5) | collective-permute-done | bytes 8224 | tf_op jit(solution)/shard_map/ppermute | solution.py:23
  18.5 0.9 %collective-permute-done.6.refs_2_ = f32[16,128]{1,0:T(8,128)S(1)} collective-permute-done((f32[16,128]{1,0:T(8,128)S(1)}, f32[16,128]{1,0:T(8,128)S(1)}, u32[]{:S(2)}, u32[]{:S(2)}) %collective-permute-start.6) | collective-permute-done | bytes 8224 | tf_op jit(solution)/shard_map/ppermute | solution.py:23
  19.5 0.0 collective-permute-done.4.refs_0_
  19.5 1.6 %collective-permute-start.7 = (f32[32,128]{1,0:T(8,128)S(1)}, f32[32,128]{1,0:T(8,128)S(1)}, u32[]{:S(2)}, u32[]{:S(2)}) collective-permute-start(f32[32,128]{1,0:T(8,128)S(1)} %get-tuple-element.43), channel_id=1, source_target_pairs={{0,24},{8,16},{16,8},{24,0},{1,25},{9,17},{17,9},{25,1},{2,26},{10... | collective-permute-start | bytes 49160 | tf_op jit(solution)/shard_map/ppermute | solution.py:23
  21.0 0.6 %collective-permute-start.8 = (f32[32,128]{1,0:T(8,128)S(1)}, f32[32,128]{1,0:T(8,128)S(1)}, u32[]{:S(2)}, u32[]{:S(2)}) collective-permute-start(f32[32,128]{1,0:T(8,128)S(1)} %get-tuple-element.44), channel_id=1, source_target_pairs={{0,16},{8,24},{16,0},{24,8},{1,17},{9,25},{17,1},{25,9},{2,18},{10... | collective-permute-start | bytes 49160 | tf_op jit(solution)/shard_map/ppermute | solution.py:23
  21.6 2.3 %collective-permute-start.9 = (f32[32,128]{1,0:T(8,128)S(1)}, f32[32,128]{1,0:T(8,128)S(1)}, u32[]{:S(2)}, u32[]{:S(2)}) collective-permute-start(f32[32,128]{1,0:T(8,128)S(1)} %get-tuple-element.45), channel_id=1, source_target_pairs={{0,8},{8,0},{16,24},{24,16},{1,9},{9,1},{17,25},{25,17},{2,10},{10... | collective-permute-start | bytes 49160 | tf_op jit(solution)/shard_map/ppermute | solution.py:23
  23.9 0.8 %shard_map.91 = (bf16[4,4,2048]{2,1,0:T(4,128)(2,1)}, f32[8,128]{1,0:T(8,128)S(1)}) custom-call(f32[16,8192]{1,0:T(8,128)S(1)} %get-tuple-element.28.rows_ref, f32[1,8192]{1,0:T(1,128)S(1)} %bitcast.14, f32[16,128]{1,0:T(8,128)S(1)} %get-tuple-element.29.inv_ref, f32[16,128]{1,0:T(8,128)S(1)} %get-tuple-element.40.dots_ref, ...), custom_call_target="tpu_custom_call" | custom-call | tf_op jit(solution)/shard_map/pallas_call | solution.py:27
  24.8 0.5 %collective-permute-done.7.refs_0_ = f32[32,128]{1,0:T(8,128)S(1)} collective-permute-done((f32[32,128]{1,0:T(8,128)S(1)}, f32[32,128]{1,0:T(8,128)S(1)}, u32[]{:S(2)}, u32[]{:S(2)}) %collective-permute-start.7) | collective-permute-done | bytes 16416 | tf_op jit(solution)/shard_map/ppermute | solution.py:23
  25.2 0.5 %collective-permute-done.8.refs_1_ = f32[32,128]{1,0:T(8,128)S(1)} collective-permute-done((f32[32,128]{1,0:T(8,128)S(1)}, f32[32,128]{1,0:T(8,128)S(1)}, u32[]{:S(2)}, u32[]{:S(2)}) %collective-permute-start.8) | collective-permute-done | bytes 16416 | tf_op jit(solution)/shard_map/ppermute | solution.py:23
  25.7 0.1 collective-permute-done.9.refs_2_
  25.8 0.6 %shard_map.92 = (f32[16,128]{1,0:T(8,128)}, bf16[4,4,512]{2,1,0:T(4,128)(2,1)}) custom-call(f32[16,128]{1,0:T(8,128)S(1)} %get-tuple-element.39.total_ref, f32[4,4,512]{2,1,0:T(4,128)S(1)} %get-tuple-element.32.kv_ref, f32[8,128]{1,0:T(8,128)S(1)} %get-tuple-element.42._, f32[32,128]{1,0:T(8,128)S(1)} %collective-permute-done.7.refs_0_, ...), custom_call_target="tpu_custom_call" | custom-call | tf_op jit(solution)/shard_map/pallas_call | solution.py:27
  (2 shorter events, 0.0 us)
Async XLA Ops:
  0.6 5.8 %copy-start = (bf16[8192,512]{1,0:T(8,128)(2,1)S(1)}, bf16[8192,512]{1,0:T(8,128)(2,1)}, u32[]{:S(2)}) copy-start(bf16[8192,512]{1,0:T(8,128)(2,1)} %weight_ref.5) | copy-start | bytes 25165828
  0.6 5.8 %copy-start.2 = (f32[8192]{0:T(1024)S(1)}, f32[8192]{0:T(1024)}, u32[]{:S(2)}) copy-start(f32[8192]{0:T(1024)} %param.9) | copy-start | bytes 98308
  0.7 5.8 %copy-start.3 = (f32[8192]{0:T(1024)S(1)}, f32[8192]{0:T(1024)}, u32[]{:S(2)}) copy-start(f32[8192]{0:T(1024)} %param.8) | copy-start | bytes 98308
  0.7 5.8 %copy-start.1 = (bf16[1,1,4,4,8192]{4,3,2,1,0:T(4,128)(2,1)S(1)}, bf16[1,1,4,4,8192]{4,3,2,1,0:T(4,128)(2,1)}, u32[]{:S(2)}) copy-start(bf16[1,1,4,4,8192]{4,3,2,1,0:T(4,128)(2,1)} %param.6) | copy-start | bytes 786436
  0.7 7.4 %collective-permute-start.2 = (bf16[4,4,512]{2,1,0:T(4,128)(2,1)}, bf16[4,4,512]{2,1,0:T(4,128)(2,1)S(1)}, u32[]{:S(2)}, u32[]{:S(2)}) collective-permute-start(bf16[4,4,512]{2,1,0:T(4,128)(2,1)} %bitcast.17), channel_id=1, source_target_pairs={{0,24},{8,16},{16,8},{24,0},{1,25},{9,17},{17,9},{25,1},{2,26},{10... | collective-permute-start | bytes 49160 | tf_op jit(solution)/shard_map/ppermute | solution.py:23
  5.8 4.8 %collective-permute-start.1 = (bf16[4,4,512]{2,1,0:T(4,128)(2,1)}, bf16[4,4,512]{2,1,0:T(4,128)(2,1)S(1)}, u32[]{:S(2)}, u32[]{:S(2)}) collective-permute-start(bf16[4,4,512]{2,1,0:T(4,128)(2,1)} %bitcast.18), channel_id=1, source_target_pairs={{0,16},{8,24},{16,0},{24,8},{1,17},{9,25},{17,1},{25,9},{2,18},{10... | collective-permute-start | bytes 49160 | tf_op jit(solution)/shard_map/ppermute | solution.py:23
  5.8 4.8 %collective-permute-start = (bf16[4,4,512]{2,1,0:T(4,128)(2,1)}, bf16[4,4,512]{2,1,0:T(4,128)(2,1)S(1)}, u32[]{:S(2)}, u32[]{:S(2)}) collective-permute-start(bf16[4,4,512]{2,1,0:T(4,128)(2,1)} %bitcast.19), channel_id=1, source_target_pairs={{0,8},{8,0},{16,24},{24,16},{1,9},{9,1},{17,25},{25,17},{2,10},{10... | collective-permute-start | bytes 49160 | tf_op jit(solution)/shard_map/ppermute | solution.py:23
  6.4 4.2 %copy-start.4 = (bf16[1,1,4,4,512]{4,3,2,1,0:T(4,128)(2,1)S(1)}, bf16[1,1,4,4,512]{4,3,2,1,0:T(4,128)(2,1)}, u32[]{:S(2)}) copy-start(bf16[1,1,4,4,512]{4,3,2,1,0:T(4,128)(2,1)} %param.11) | copy-start | bytes 49156
  6.4 4.2 %copy-start.5 = (s32[1,1,4]{2,1,0:T(1,128)S(1)}, s32[1,1,4]{2,1,0:T(1,128)}, u32[]{:S(2)}) copy-start(s32[1,1,4]{2,1,0:T(1,128)} %param.7) | copy-start | bytes 52
  11.4 1.6 %collective-permute-start.3 = (f32[16,4480]{1,0:T(8,128)S(1)}, f32[16,4480]{1,0:T(8,128)S(1)}, u32[]{:S(2)}, u32[]{:S(2)}) collective-permute-start(f32[16,4480]{1,0:T(8,128)S(1)} %get-tuple-element.33), channel_id=1, source_target_pairs={{0,1},{1,0},{2,3},{3,2},{4,5},{5,4},{6,7},{7,6},{8,9},{9,8},{10,11... | collective-permute-start | bytes 860168 | tf_op jit(solution)/shard_map/ppermute | solution.py:23
  13.1 6.4 %collective-permute-start.4 = (bf16[16,4608]{1,0:T(8,128)(2,1)S(1)}, bf16[16,4608]{1,0:T(8,128)(2,1)S(1)}, u32[]{:S(2)}, u32[]{:S(2)}) collective-permute-start(bf16[16,4608]{1,0:T(8,128)(2,1)S(1)} %get-tuple-element.37), channel_id=1, source_target_pairs={{0,3},{1,2},{2,1},{3,0},{4,7},{5,6},{6,5},{7,4},{8,11},{9,10},{10,... | collective-permute-start | bytes 442376 | tf_op jit(solution)/shard_map/ppermute | solution.py:23
  14.4 4.1 %collective-permute-start.5 = (f32[16,128]{1,0:T(8,128)S(1)}, f32[16,128]{1,0:T(8,128)S(1)}, u32[]{:S(2)}, u32[]{:S(2)}) collective-permute-start(f32[16,128]{1,0:T(8,128)S(1)} %get-tuple-element.38), channel_id=1, source_target_pairs={{0,7},{1,6},{2,5},{3,4},{4,3},{5,2},{6,1},{7,0},{8,15},{9,14},{10,... | collective-permute-start | bytes 24584 | tf_op jit(solution)/shard_map/ppermute | solution.py:23
  15.8 3.7 %collective-permute-start.6 = (f32[16,128]{1,0:T(8,128)S(1)}, f32[16,128]{1,0:T(8,128)S(1)}, u32[]{:S(2)}, u32[]{:S(2)}) collective-permute-start(f32[16,128]{1,0:T(8,128)S(1)} %get-tuple-element.36.sum_ref), channel_id=1, source_target_pairs={{0,4},{1,5},{2,6},{3,7},{4,0},{5,1},{6,2},{7,3},{8,12},{9,13},{10,... | collective-permute-start | bytes 24584 | tf_op jit(solution)/shard_map/ppermute | solution.py:23
  19.5 5.8 %collective-permute-start.7 = (f32[32,128]{1,0:T(8,128)S(1)}, f32[32,128]{1,0:T(8,128)S(1)}, u32[]{:S(2)}, u32[]{:S(2)}) collective-permute-start(f32[32,128]{1,0:T(8,128)S(1)} %get-tuple-element.43), channel_id=1, source_target_pairs={{0,24},{8,16},{16,8},{24,0},{1,25},{9,17},{17,9},{25,1},{2,26},{10... | collective-permute-start | bytes 49160 | tf_op jit(solution)/shard_map/ppermute | solution.py:23
  21.0 4.7 %collective-permute-start.8 = (f32[32,128]{1,0:T(8,128)S(1)}, f32[32,128]{1,0:T(8,128)S(1)}, u32[]{:S(2)}, u32[]{:S(2)}) collective-permute-start(f32[32,128]{1,0:T(8,128)S(1)} %get-tuple-element.44), channel_id=1, source_target_pairs={{0,16},{8,24},{16,0},{24,8},{1,17},{9,25},{17,1},{25,9},{2,18},{10... | collective-permute-start | bytes 49160 | tf_op jit(solution)/shard_map/ppermute | solution.py:23
  21.6 4.2 %collective-permute-start.9 = (f32[32,128]{1,0:T(8,128)S(1)}, f32[32,128]{1,0:T(8,128)S(1)}, u32[]{:S(2)}, u32[]{:S(2)}) collective-permute-start(f32[32,128]{1,0:T(8,128)S(1)} %get-tuple-element.45), channel_id=1, source_target_pairs={{0,8},{8,0},{16,24},{24,16},{1,9},{9,1},{17,25},{25,17},{2,10},{10... | collective-permute-start | bytes 49160 | tf_op jit(solution)/shard_map/ppermute | solution.py:23
